TPU v7x, 256 devices: a whole 4x4x8 slice. The times are simulated.
256 devices in a mesh: rows: 32 (over y, z), cols: 8 (over x, core).
Axes of the slice: x: 4, y: 4, z: 8, core: 2. Of those that a mesh axis runs over, the one named last changes fastest.
Arguments:
- x_feat: bfloat16 [64, 65536], P(None, ('rows', 'cols')), may hold values from -24 to 24
- y_feat: bfloat16 [64, 65536], P(None, ('cols', 'rows')), may hold values from -24 to 24
- log_a: float32 [65536], P(('rows', 'cols')), may hold values from -8 to 8
- log_b: float32 [65536], P(('cols', 'rows')), may hold values from -8 to 8
- g_init: float32 [65536], P('cols'), may hold values from -3 to 3
Outputs:
- f_pot: float32 [65536], P('rows')
- g_pot: float32 [65536], P('cols')
All inputs are finite; a program needn't handle non-finite values.
Results may differ from a plain program's by a relative error of at most 0.0018.
Values may be sent and summed in bfloat16 or wider, within the bound.
No kernel may reach another device: no remote copies, remote signals or barrier semaphores. Data moves between devices by JAX's collectives and lax.ppermute only.
A program may use at most 64 MiB of HBM per device.

v0:
```python
import jax
import jax.numpy as jnp
from jax import lax
from jax.sharding import PartitionSpec as P

EPS = 0.05


def cost_tile(xb, nxb, y, ny, feat):
    inner = lax.dot_general(xb, y, (((0,), (0,)), ((), ())), preferred_element_type=jnp.float32)
    return (nxb[:, None] + ny[None, :] - 2.0 * inner) / feat


def local(x_feat, y_feat, log_a, log_b, g_init):
    feat = x_feat.shape[0]
    x_all, la_all = (
        lax.all_gather(x_feat, "cols", axis=1, tiled=True),
        lax.all_gather(log_a.astype(jnp.bfloat16), "cols", axis=0, tiled=True).astype(log_a.dtype),
    )
    y_all, lb_all = (
        lax.all_gather(y_feat, "rows", axis=1, tiled=True),
        lax.all_gather(log_b.astype(jnp.bfloat16), "rows", axis=0, tiled=True).astype(log_b.dtype),
    )
    nx = jnp.sum(jnp.square(x_all.astype(jnp.float32)), axis=0)
    ny = jnp.sum(jnp.square(y_all.astype(jnp.float32)), axis=0)
    total = x_all.shape[1]
    block = min(512, total)
    count = total // block
    xs = jnp.transpose(x_all.reshape(feat, count, block), (1, 0, 2))
    nxs = nx.reshape(count, block)

    def row_block(args):
        xb, nxb = args
        cost = cost_tile(xb, nxb, y_all, ny, feat)
        expo = lb_all[None, :] + (g_init[None, :] - cost) / EPS
        top = jnp.max(expo, axis=1)
        return (top, jnp.sum(jnp.exp(expo - top[:, None]), axis=1))

    row_top, row_acc = lax.map(row_block, (xs, nxs))
    row_top = row_top.reshape(total)
    row_acc = row_acc.reshape(total)
    whole_top = lax.pmax(row_top, "cols")
    row_acc = lax.psum(row_acc * jnp.exp(row_top - whole_top), "cols")
    row_top = whole_top
    f_pot = -EPS * (row_top + jnp.log(row_acc))
    fs = f_pot.reshape(count, block)
    las = la_all.reshape(count, block)

    def col_block(carry, args):
        top, acc = carry
        xb, nxb, fb, lab = args
        cost = cost_tile(xb, nxb, y_all, ny, feat)
        expo = lab[:, None] + (fb[:, None] - cost) / EPS
        new_top = jnp.maximum(top, jnp.max(expo, axis=0))
        acc = acc * jnp.exp(top - new_top) + jnp.sum(jnp.exp(expo - new_top[None, :]), axis=0)
        return ((new_top, acc), None)

    start = (jnp.full(ny.shape, -jnp.inf, jnp.float32), jnp.zeros(ny.shape, jnp.float32))
    (col_top, col_acc), unused = lax.scan(col_block, start, (xs, nxs, fs, las))
    whole_col = lax.pmax(col_top.astype(jnp.bfloat16), "rows").astype(col_top.dtype)
    col_acc = lax.psum(
        (col_acc * jnp.exp(col_top - whole_col)).astype(jnp.bfloat16), "rows"
    ).astype(jnp.float32)
    col_top = whole_col
    g_pot = -EPS * (col_top + jnp.log(col_acc))
    return (f_pot, g_pot)


def solution(mesh):
    placed = (
        P(None, ("rows", "cols")),
        P(None, ("cols", "rows")),
        P(("rows", "cols")),
        P(("cols", "rows")),
        P("cols"),
    )
    return jax.shard_map(
        local, mesh=mesh, in_specs=placed, out_specs=(P("rows"), P("cols")), check_vma=False
    )
```

profile of v0, /device:TPU:32, one launch (start us, length us, event | category | flops | bytes accessed | tf_op | source)
XLA Modules:
  0.0 543.6 jit_solution(8197106167575352189)
XLA Ops:
  7.2 0.0 all-gather.4.cloned.1.call-start
  7.2 0.7 all-gather.4.cloned.1.call-update
  7.9 0.7 convert_element_type.32
  8.6 0.7 convert_element_type.28
  9.3 10.5 %all-gather.1 = bf16[8,1,256]{2,1,0:T(2,128)(2,1)S(1)} all-gather(bf16[1,1,256]{2,1,0:T(2,128)(2,1)S(1)} %reshape.50), channel_id=1, replica_groups=mesh['rows'=32,'cols'=8] {'cols'}, dimensions={0}, use_global_device_ids=true | all-gather | bytes 4608 | tf_op jit(solution)/shard_map/all_gather | solution.py:18
  19.9 45.3 %all-gather = bf16[32,1,256]{2,1,0:T(2,128)(2,1)S(1)} all-gather(bf16[1,1,256]{2,1,0:T(2,128)(2,1)S(1)} %reshape.48), channel_id=1, replica_groups=mesh['rows'=32,'cols'=8] {'rows'}, dimensions={0}, use_global_device_ids=true | all-gather | bytes 16896 | tf_op jit(solution)/shard_map/all_gather | solution.py:22
  65.3 13.1 %all_gather.13 = bf16[64,2048]{1,0:T(8,128)(2,1)S(1)} all-gather(bf16[64,256]{1,0:T(8,128)(2,1)} %param.9), channel_id=1, replica_groups=mesh['rows'=32,'cols'=8] {'cols'}, dimensions={1}, use_global_device_ids=true | all-gather | bytes 294912 | tf_op jit(solution)/shard_map/all_gather | solution.py:17
  78.3 0.2 reshape.40
  78.5 0.1 multiply_reduce_fusion.1
  78.7 5.2 all-gather.4.cloned.1.call-done
  83.8 1.5 multiply_reduce_fusion
  85.3 73.2 %while.25 = (s32[]{:T(128)}, f32[4,512]{1,0:T(4,128)S(1)}, f32[4,512]{1,0:T(4,128)S(1)}, f32[8192]{0:T(1024)S(1)}, f32[8192]{0:T(1024)}, /*index=5*/f32[4,512]{1...) while((s32[]{:T(128)}, f32[4,512]{1,0:T(4,128)S(1)}, ...), condition=%wide.region_5.6_spmd, body=%wide.region_2.5_spmd.sunk | while | flops 578812928 | bytes 34787460 | solution.py:39
  85.4 10.1 %fusion.21 = (f32[512]{0:T(512)S(1)}, f32[512,8192]{1,0:T(8,128)}) fusion(bf16[64,8192]{1,0:T(8,128)(2,1)} %get-tuple-element.362, bf16[4,64,512]{2,1,0:T(8,128)(2,1)S(1)} %get-tuple-element.361, s32[]{:T(128)S(6)} %copy.18, f32[8192]{0:T(1024)S(1)} %get-tuple-element.360, f32[512]{0:T(512)S(1)} %bitcast.52, f32[8192]{0:T(1024)} %get-tuple-element.358, ...), kind=kOutput, calls=%fused_computation.28.clone.1 | convolution fusion | flops 570424832 | bytes 17993732 | tf_op jit(solution)/shard_map/while/body/eval_jaxpr/dot_general | solution.py:10
  95.4 8.1 %exponential_reduce_fusion.4 = f32[512]{0:T(512)S(1)} fusion(f32[512,8192]{1,0:T(8,128)} %get-tuple-element.318, f32[512]{0:T(512)S(1)} %get-tuple-element.317), kind=kLoop, calls=%fused_computation.clone.1 | loop fusion | flops 8388096 | bytes 16781312 | tf_op jit(solution)/shard_map/while/body/eval_jaxpr/reduce_sum | solution.py:37
  103.6 0.1 dynamic_update_slice.10
  103.7 10.1 %fusion.21 = (f32[512]{0:T(512)S(1)}, f32[512,8192]{1,0:T(8,128)}) fusion(bf16[64,8192]{1,0:T(8,128)(2,1)} %get-tuple-element.362, bf16[4,64,512]{2,1,0:T(8,128)(2,1)S(1)} %get-tuple-element.361, s32[]{:T(128)S(6)} %copy.18, f32[8192]{0:T(1024)S(1)} %get-tuple-element.360, f32[512]{0:T(512)S(1)} %bitcast.52, f32[8192]{0:T(1024)} %get-tuple-element.358, ...), kind=kOutput, calls=%fused_computation.28.clone.1 | convolution fusion | flops 570424832 | bytes 17993732 | tf_op jit(solution)/shard_map/while/body/eval_jaxpr/dot_general | solution.py:10
  113.7 8.1 %exponential_reduce_fusion.4 = f32[512]{0:T(512)S(1)} fusion(f32[512,8192]{1,0:T(8,128)} %get-tuple-element.318, f32[512]{0:T(512)S(1)} %get-tuple-element.317), kind=kLoop, calls=%fused_computation.clone.1 | loop fusion | flops 8388096 | bytes 16781312 | tf_op jit(solution)/shard_map/while/body/eval_jaxpr/reduce_sum | solution.py:37
  121.9 0.1 dynamic_update_slice.10
  122.0 10.1 %fusion.21 = (f32[512]{0:T(512)S(1)}, f32[512,8192]{1,0:T(8,128)}) fusion(bf16[64,8192]{1,0:T(8,128)(2,1)} %get-tuple-element.362, bf16[4,64,512]{2,1,0:T(8,128)(2,1)S(1)} %get-tuple-element.361, s32[]{:T(128)S(6)} %copy.18, f32[8192]{0:T(1024)S(1)} %get-tuple-element.360, f32[512]{0:T(512)S(1)} %bitcast.52, f32[8192]{0:T(1024)} %get-tuple-element.358, ...), kind=kOutput, calls=%fused_computation.28.clone.1 | convolution fusion | flops 570424832 | bytes 17993732 | tf_op jit(solution)/shard_map/while/body/eval_jaxpr/dot_general | solution.py:10
  132.0 8.1 %exponential_reduce_fusion.4 = f32[512]{0:T(512)S(1)} fusion(f32[512,8192]{1,0:T(8,128)} %get-tuple-element.318, f32[512]{0:T(512)S(1)} %get-tuple-element.317), kind=kLoop, calls=%fused_computation.clone.1 | loop fusion | flops 8388096 | bytes 16781312 | tf_op jit(solution)/shard_map/while/body/eval_jaxpr/reduce_sum | solution.py:37
  140.2 0.1 dynamic_update_slice.10
  140.3 10.1 %fusion.21 = (f32[512]{0:T(512)S(1)}, f32[512,8192]{1,0:T(8,128)}) fusion(bf16[64,8192]{1,0:T(8,128)(2,1)} %get-tuple-element.362, bf16[4,64,512]{2,1,0:T(8,128)(2,1)S(1)} %get-tuple-element.361, s32[]{:T(128)S(6)} %copy.18, f32[8192]{0:T(1024)S(1)} %get-tuple-element.360, f32[512]{0:T(512)S(1)} %bitcast.52, f32[8192]{0:T(1024)} %get-tuple-element.358, ...), kind=kOutput, calls=%fused_computation.28.clone.1 | convolution fusion | flops 570424832 | bytes 17993732 | tf_op jit(solution)/shard_map/while/body/eval_jaxpr/dot_general | solution.py:10
  150.4 8.1 %exponential_reduce_fusion.4 = f32[512]{0:T(512)S(1)} fusion(f32[512,8192]{1,0:T(8,128)} %get-tuple-element.318, f32[512]{0:T(512)S(1)} %get-tuple-element.317), kind=kLoop, calls=%fused_computation.clone.1 | loop fusion | flops 8388096 | bytes 16781312 | tf_op jit(solution)/shard_map/while/body/eval_jaxpr/reduce_sum | solution.py:37
  158.5 0.1 dynamic_update_slice.10
  158.6 12.7 %pmax.14 = f32[2048]{0:T(1024)S(1)} all-reduce(f32[2048]{0:T(1024)S(1)} %bitcast.47), channel_id=1, replica_groups=mesh['rows'=32,'cols'=8] {'cols'}, use_global_device_ids=true, to_apply=%region_6.7 | all-reduce | flops 2048 | bytes 16384 | tf_op jit(solution)/shard_map/pmax | solution.py:42
  171.3 12.8 %psum.14 = f32[2048]{0:T(1024)S(1)} all-reduce(f32[2048]{0:T(1024)S(1)} %exponential_multiply_fusion), channel_id=1, replica_groups=mesh['rows'=32,'cols'=8] {'cols'}, use_global_device_ids=true, to_apply=%region_7.8 | all-reduce | flops 2048 | bytes 16384 | tf_op jit(solution)/shard_map/psum | solution.py:43
  184.2 0.0 copy-start
  184.2 0.6 copy-done
  184.8 74.0 %while.26 = (s32[]{:T(128)}, f32[8192]{0:T(1024)S(1)}, f32[8192]{0:T(1024)S(1)}, f32[4,512]{1,0:T(4,128)S(1)}, f32[4,512]{1,0:T(4,128)S(1)}, /*index=5*/f32[4,51...) while((s32[]{:T(128)}, f32[8192]{0:T(1024)S(1)}, ...), condition=%wide.region_11.12_spmd.clone, body=%wide.region_8.11_spmd.clone.sunk | while | flops 578854912 | bytes 35145864 | solution.py:59
  184.8 10.1 %fusion.23 = (f32[8192]{0:T(1024)S(1)}, f32[512,8192]{1,0:T(8,128)}) fusion(bf16[64,8192]{1,0:T(8,128)(2,1)} %get-tuple-element.395, bf16[4,64,512]{2,1,0:T(8,128)(2,1)S(1)} %get-tuple-element.394, s32[]{:T(128)S(6)} %copy.27, f32[8192]{0:T(1024)S(1)} %get-tuple-element.393, f32[512]{0:T(512)S(1)} %bitcast.49, f32[512]{0:T(512)S(1)} %bitcast.50, ...), kind=kOutput, calls=%fused_computation.29.clone.1 | convolution fusion | flops 570417152 | bytes 17963012 | tf_op jit(solution)/shard_map/while/body/eval_jaxpr/dot_general | solution.py:10
  194.9 8.3 %exponential_reduce_fusion.5 = f32[8192]{0:T(1024)S(1)} fusion(f32[512,8192]{1,0:T(8,128)} %get-tuple-element.331, f32[8192]{0:T(1024)S(1)} %select_maximum_fusion.2), kind=kLoop, calls=%fused_computation.6.clone.1 | loop fusion | flops 8380416 | bytes 16842752 | tf_op jit(solution)/shard_map/while/body/eval_jaxpr/reduce_sum | solution.py:55
  203.3 10.1 %fusion.23 = (f32[8192]{0:T(1024)S(1)}, f32[512,8192]{1,0:T(8,128)}) fusion(bf16[64,8192]{1,0:T(8,128)(2,1)} %get-tuple-element.395, bf16[4,64,512]{2,1,0:T(8,128)(2,1)S(1)} %get-tuple-element.394, s32[]{:T(128)S(6)} %copy.27, f32[8192]{0:T(1024)S(1)} %get-tuple-element.393, f32[512]{0:T(512)S(1)} %bitcast.49, f32[512]{0:T(512)S(1)} %bitcast.50, ...), kind=kOutput, calls=%fused_computation.29.clone.1 | convolution fusion | flops 570417152 | bytes 17963012 | tf_op jit(solution)/shard_map/while/body/eval_jaxpr/dot_general | solution.py:10
  213.4 8.3 %exponential_reduce_fusion.5 = f32[8192]{0:T(1024)S(1)} fusion(f32[512,8192]{1,0:T(8,128)} %get-tuple-element.331, f32[8192]{0:T(1024)S(1)} %select_maximum_fusion.2), kind=kLoop, calls=%fused_computation.6.clone.1 | loop fusion | flops 8380416 | bytes 16842752 | tf_op jit(solution)/shard_map/while/body/eval_jaxpr/reduce_sum | solution.py:55
  221.8 10.1 %fusion.23 = (f32[8192]{0:T(1024)S(1)}, f32[512,8192]{1,0:T(8,128)}) fusion(bf16[64,8192]{1,0:T(8,128)(2,1)} %get-tuple-element.395, bf16[4,64,512]{2,1,0:T(8,128)(2,1)S(1)} %get-tuple-element.394, s32[]{:T(128)S(6)} %copy.27, f32[8192]{0:T(1024)S(1)} %get-tuple-element.393, f32[512]{0:T(512)S(1)} %bitcast.49, f32[512]{0:T(512)S(1)} %bitcast.50, ...), kind=kOutput, calls=%fused_computation.29.clone.1 | convolution fusion | flops 570417152 | bytes 17963012 | tf_op jit(solution)/shard_map/while/body/eval_jaxpr/dot_general | solution.py:10
  231.9 8.3 %exponential_reduce_fusion.5 = f32[8192]{0:T(1024)S(1)} fusion(f32[512,8192]{1,0:T(8,128)} %get-tuple-element.331, f32[8192]{0:T(1024)S(1)} %select_maximum_fusion.2), kind=kLoop, calls=%fused_computation.6.clone.1 | loop fusion | flops 8380416 | bytes 16842752 | tf_op jit(solution)/shard_map/while/body/eval_jaxpr/reduce_sum | solution.py:55
  240.3 10.1 %fusion.23 = (f32[8192]{0:T(1024)S(1)}, f32[512,8192]{1,0:T(8,128)}) fusion(bf16[64,8192]{1,0:T(8,128)(2,1)} %get-tuple-element.395, bf16[4,64,512]{2,1,0:T(8,128)(2,1)S(1)} %get-tuple-element.394, s32[]{:T(128)S(6)} %copy.27, f32[8192]{0:T(1024)S(1)} %get-tuple-element.393, f32[512]{0:T(512)S(1)} %bitcast.49, f32[512]{0:T(512)S(1)} %bitcast.50, ...), kind=kOutput, calls=%fused_computation.29.clone.1 | convolution fusion | flops 570417152 | bytes 17963012 | tf_op jit(solution)/shard_map/while/body/eval_jaxpr/dot_general | solution.py:10
  250.4 8.3 %exponential_reduce_fusion.5 = f32[8192]{0:T(1024)S(1)} fusion(f32[512,8192]{1,0:T(8,128)} %get-tuple-element.331, f32[8192]{0:T(1024)S(1)} %select_maximum_fusion.2), kind=kLoop, calls=%fused_computation.6.clone.1 | loop fusion | flops 8380416 | bytes 16842752 | tf_op jit(solution)/shard_map/while/body/eval_jaxpr/reduce_sum | solution.py:55
  258.8 137.4 %pmax.15 = bf16[8192]{0:T(1024)(128)(2,1)S(1)} all-reduce(bf16[8192]{0:T(1024)(128)(2,1)S(1)} %convert_element_type.33), channel_id=1, replica_groups=mesh['rows'=32,'cols'=8] {'rows'}, use_global_device_ids=true, to_apply=%region_12.13 | all-reduce | flops 8192 | bytes 32768 | tf_op jit(solution)/shard_map/pmax | solution.py:60
  396.2 140.0 %psum.15 = bf16[8192]{0:T(1024)(128)(2,1)S(1)} all-reduce(bf16[8192]{0:T(1024)(128)(2,1)S(1)} %fusion.9), channel_id=1, replica_groups=mesh['rows'=32,'cols'=8] {'rows'}, use_global_device_ids=true, to_apply=%region_13.14 | all-reduce | flops 8192 | bytes 32768 | tf_op jit(solution)/shard_map/psum | solution.py:61
  536.2 0.6 fusion.10
  (46 shorter events, 0.6 us)
Async XLA Ops:
  7.2 76.7 %all-gather.4.cloned.1.call-start = ((), (), s32[]{:S(2)}) async-start(), calls=%async_computation | async-start | bytes 1081344 | tf_op jit(solution)/shard_map/all_gather | solution.py:21
  184.2 0.6 copy-start
Sparse Core Ops, SparseCore 0:
  10.5 73.3 all-gather.3
where the time goes:
time: 546 us; the launch traced here: 544 us
  blocking collectives  372 us (68%)
  matrix products  80.7 us (15%)
  other arithmetic  69.4 us (13%)
  between operations  14.2 us (3%)
  waiting for transfers between devices  5.87 us (1%)
    psum x1, blocking collectives, local(): lax.psum((col_acc * jnp.exp(col_top - whole_col)).astype(jnp.bfloat16), '...  140 us
    pmax x1, blocking collectives, local(): lax.pmax(col_top.astype(jnp.bfloat16), 'rows').astype(col_top.dtype)  137 us
    dot_general x8, matrix products, cost_tile(): lax.dot_general(xb, y, (((0,), (0,)), ((), ())), preferred_element_type=j...  80.7 us
    all_gather x1, blocking collectives, local(): lax.all_gather(log_b.astype(jnp.bfloat16), 'rows', axis=0, tiled=True)  45.3 us
    reduce_sum x4, other arithmetic, col_block(): jnp.sum(jnp.exp(expo - new_top[None, :]), axis=0)  33.2 us
    reduce_sum x4, other arithmetic, row_block(): return (top, jnp.sum(jnp.exp(expo - top[:, None]), axis=1))  32.4 us
    all_gather x1, blocking collectives, local(): lax.all_gather(x_feat, 'cols', axis=1, tiled=True)  13.1 us
    psum x1, blocking collectives, local(): row_acc = lax.psum(row_acc * jnp.exp(row_top - whole_top), 'cols')  12.8 us
  transfers between devices with their start and end apart: 1, of which 1 were waited for; matrix products, arithmetic and copies ran while one was open for 0% of the time, Pallas kernels for 0%

commit v1 on v0

v1 whole, which is shorter than its diff:
```python
import functools

import jax
import jax.numpy as jnp
from jax import lax
from jax.experimental import pallas as pl
from jax.experimental.pallas import tpu as pltpu
from jax.sharding import PartitionSpec as P

EPS = 0.05
LOG2E = 1.4426950408889634
LN2 = 0.6931471805599453
BF16 = jnp.bfloat16
F32 = jnp.float32
PIECE = 256
EXTRA = 16
DEPTH = 256
LOW = -1e30
VMEM_LIMIT = 56 * 1024 * 1024


def split3(v):
    high = v.astype(BF16).astype(F32)
    rest = v - high
    mid = rest.astype(BF16).astype(F32)
    return high, mid, rest - mid


def wide(ref, row):
    pair = ref[pl.ds(row, 2), :]
    return jnp.concatenate([pair[0:1], pair[1:2]], axis=1)


def rows_of(terms, count, width):
    row = lax.broadcasted_iota(jnp.int32, (count, width), 0)
    out = jnp.zeros((count, width), F32)
    for index, term in enumerate(terms):
        out = jnp.where(row == index, term, out)
    return out


def pack_kernel(x_ref, y_ref, la_ref, lb_ref, g_ref, xo_ref, yo_ref):
    feat = x_ref.shape[0]
    la = wide(la_ref, 0) * LOG2E
    y = y_ref[...].astype(F32)
    ny = jnp.sum(y * y, axis=0, keepdims=True)
    mine = lax.axis_index("rows")
    g = wide(g_ref, 2 * mine)
    own = (wide(lb_ref, 0) + (g - ny / feat) / EPS) * LOG2E
    one = jnp.ones((1, PIECE), F32)
    x_extra = rows_of(split3(la), EXTRA, PIECE).astype(BF16)
    y_extra = rows_of(split3(own) + (one, one, one), EXTRA, PIECE).astype(BF16)
    for d in range(xo_ref.shape[0]):
        xo_ref[d, 0:feat, :] = x_ref[...]
        xo_ref[d, feat : feat + EXTRA, :] = x_extra
    for d in range(yo_ref.shape[0]):
        yo_ref[d, 0:feat, :] = y_ref[...]
        yo_ref[d, feat : feat + EXTRA, :] = y_extra


def left_side(x_ref, p, extra, scale):
    feat = x_ref.shape[1] - EXTRA
    parts = split3(x_ref[p, 0:feat, :].astype(F32) * scale)
    fill = jnp.zeros((DEPTH - 3 * feat - EXTRA, PIECE), F32)
    return jnp.transpose(jnp.concatenate(parts + (extra, fill), axis=0)).astype(BF16)


def right_side(y_ref, p):
    feat = y_ref.shape[1] - EXTRA
    y = y_ref[p, 0:feat, :]
    extra = y_ref[p, feat : feat + EXTRA, :]
    fill = jnp.zeros((DEPTH - 3 * feat - EXTRA, PIECE), BF16)
    return jnp.concatenate([y, y, y, extra, fill], axis=0)


def dot(a, b):
    return jnp.dot(a, b, preferred_element_type=F32)


IB = 512
JP = 4


def row_kernel(x_ref, y_ref, out_ref, a_ref, s_ref, m_ref, l_ref, *, scale):
    pieces = x_ref.shape[0]
    n = pieces * PIECE
    one = jnp.ones((1, PIECE), F32)
    extra = rows_of((one, one, one), EXTRA, PIECE)
    for p in range(pieces):
        a_ref[p * PIECE : (p + 1) * PIECE, :] = left_side(x_ref, p, extra, scale)
    m_ref[...] = jnp.full(m_ref.shape, LOW, F32)
    l_ref[...] = jnp.zeros(l_ref.shape, F32)
    blocks = n // IB
    steps = blocks * (y_ref.shape[0] // JP)

    def start(t, k):
        base = pl.multiple_of((t % blocks) * IB, IB)
        return dot(a_ref[pl.ds(base, IB), :], right_side(y_ref, (t // blocks) * JP + k))

    def finish(t, slot, r):
        base = pl.multiple_of((t % blocks) * IB + r, 8)
        rows = pl.ds(base, 8)
        vals = [s_ref[slot, r : r + 8, c * 128 : (c + 1) * 128] for c in range(JP * 2)]
        old = m_ref[rows, :]
        top = old
        for v in vals:
            top = jnp.maximum(top, v)
        acc = l_ref[rows, :] * jnp.exp2(old - top)
        for v in vals:
            acc = acc + jnp.exp2(v - top)
        m_ref[rows, :] = top
        l_ref[rows, :] = acc

    def half(t, slot):
        later = jnp.minimum(t + 1, steps - 1)
        for k in range(JP):
            s_ref[1 - slot, :, k * PIECE : (k + 1) * PIECE] = start(later, k)
            for r in range(k * IB // JP, (k + 1) * IB // JP, 8):
                finish(t, slot, r)

    for k in range(JP):
        s_ref[0, :, k * PIECE : (k + 1) * PIECE] = start(0, k)

    def body(u, carry):
        half(2 * u, 0)
        half(2 * u + 1, 1)
        return carry

    lax.fori_loop(0, steps // 2, body, 0)
    for q in range(n // 128):
        mt = jnp.transpose(m_ref[q * 128 : (q + 1) * 128, :])
        lt = jnp.transpose(l_ref[q * 128 : (q + 1) * 128, :])
        top = jnp.max(mt, axis=0, keepdims=True)
        lse = top + jnp.log2(jnp.sum(lt * jnp.exp2(mt - top), axis=0, keepdims=True))
        for d in range(out_ref.shape[0]):
            out_ref[d, q : q + 1, :] = lse


def col_kernel(x_ref, y_ref, lse_ref, f_ref, out_ref, a_ref, s_ref, *, scale):
    pieces, feat = x_ref.shape[0], x_ref.shape[1] - EXTRA
    n = pieces * PIECE
    tiles = y_ref.shape[0]
    part = lse_ref[...]
    top = jnp.max(part, axis=0)
    whole = top + jnp.log2(jnp.sum(jnp.exp2(part - top[None]), axis=0))
    zero = jnp.zeros((1, PIECE), F32)
    for p in range(pieces):
        lse = jnp.concatenate([whole[2 * p : 2 * p + 1], whole[2 * p + 1 : 2 * p + 2]], axis=1)
        x = x_ref[p, 0:feat, :].astype(F32)
        nx = jnp.sum(x * x, axis=0, keepdims=True)
        f = nx / feat - (EPS * LN2) * lse
        f_ref[2 * p : 2 * p + 1, :] = f[:, 0:128]
        f_ref[2 * p + 1 : 2 * p + 2, :] = f[:, 128:256]
        la = jnp.sum(x_ref[p, feat : feat + EXTRA, :].astype(F32), axis=0, keepdims=True)
        extra = rows_of((zero, zero, zero) + split3(la - lse), EXTRA, PIECE)
        a_ref[p * PIECE : (p + 1) * PIECE, :] = left_side(x_ref, p, extra, scale)
    chunk = 512

    def start(t, k):
        return dot(a_ref[k * chunk : (k + 1) * chunk, :], right_side(y_ref, t))

    def fold(s, how):
        return how(s.reshape(s.shape[0] // 8, 8, s.shape[1]), axis=0)

    def half(t, slot, top):
        later = jnp.minimum(t + 1, tiles - 1)
        new = jnp.full((8, PIECE), LOW, F32)
        acc = jnp.zeros((8, PIECE), F32)
        for k in range(n // chunk):
            s = start(later, k)
            s_ref[1 - slot, k * chunk : (k + 1) * chunk, :] = s
            new = jnp.maximum(new, fold(s, jnp.max))
            for r in range(k * chunk, (k + 1) * chunk, 64):
                v = s_ref[slot, r : r + 64, :].reshape(8, 8, PIECE)
                acc = acc + jnp.sum(jnp.exp2(v - top[None]), axis=0)
        peak = jnp.max(top, axis=0, keepdims=True)
        total = jnp.sum(acc * jnp.exp2(top - peak), axis=0, keepdims=True)
        y = y_ref[t, 0:feat, :].astype(F32)
        ny = jnp.sum(y * y, axis=0, keepdims=True)
        u = peak + jnp.log2(total) - ny * (LOG2E / (feat * EPS))
        for d in range(out_ref.shape[0]):
            out_ref[d, pl.ds(2 * t, 1), :] = u[:, 0:128]
            out_ref[d, pl.ds(2 * t + 1, 1), :] = u[:, 128:256]
        return new

    top = jnp.full((8, PIECE), LOW, F32)
    for k in range(n // chunk):
        s = start(0, k)
        s_ref[0, k * chunk : (k + 1) * chunk, :] = s
        top = jnp.maximum(top, fold(s, jnp.max))

    def body(u, top):
        return half(2 * u + 1, 1, half(2 * u, 0, top))

    lax.fori_loop(0, tiles // 2, body, top)


def merge_kernel(u_ref, out_ref):
    u = u_ref[...]
    top = jnp.max(u, axis=0)
    whole = top + jnp.log2(jnp.sum(jnp.exp2(u - top[None]), axis=0))
    for d in range(out_ref.shape[0]):
        out_ref[d] = whole


def last_kernel(u_ref, out_ref):
    u = u_ref[...]
    top = jnp.max(u, axis=0)
    out_ref[...] = (top + jnp.log2(jnp.sum(jnp.exp2(u - top[None]), axis=0))) * (-EPS * LN2)


def call(kernel, outs, args, scratch=(), name=None):
    vmem = pl.BlockSpec(memory_space=pltpu.VMEM)
    return pl.pallas_call(
        kernel,
        out_shape=outs,
        in_specs=[vmem] * len(args),
        out_specs=jax.tree.map(lambda _: vmem, outs),
        scratch_shapes=list(scratch),
        compiler_params=pltpu.CompilerParams(vmem_limit_bytes=VMEM_LIMIT),
        name=name,
    )(*args)


def local(groups, x_feat, y_feat, log_a, log_b, g_init):
    z_groups, y_groups, nc = groups
    ny_, nz = len(z_groups), len(y_groups)
    feat, piece = x_feat.shape
    scale = 2.0 * LOG2E / (feat * EPS)
    shape = jax.ShapeDtypeStruct
    depth = feat + EXTRA
    xo, yo = call(
        pack_kernel,
        [shape((nc, depth, piece), BF16), shape((nz, depth, piece), BF16)],
        (
            x_feat,
            y_feat,
            log_a.reshape(-1, 128),
            log_b.reshape(-1, 128),
            g_init.reshape(-1, 128),
        ),
        name="pack",
    )
    xs = lax.all_to_all(xo, "cols", 0, 0)
    yz = lax.all_to_all(yo, "rows", 0, 0, axis_index_groups=z_groups)
    ys = lax.all_to_all(
        jnp.broadcast_to(yz[None], (ny_,) + yz.shape), "rows", 0, 0, axis_index_groups=y_groups
    ).reshape(ny_ * nz, depth, piece)
    n, m = nc * piece, ny_ * nz * piece
    lse = call(
        functools.partial(row_kernel, scale=scale),
        shape((nc, n // 128, 128), F32),
        (xs, ys),
        [
            pltpu.VMEM((n, DEPTH), BF16),
            pltpu.VMEM((2, IB, JP * PIECE), F32),
            pltpu.VMEM((n, 128), F32),
            pltpu.VMEM((n, 128), F32),
        ],
        name="row_pass",
    )
    parts = lax.all_to_all(lse, "cols", 0, 0)
    f, u = call(
        functools.partial(col_kernel, scale=scale),
        [shape((n // 128, 128), F32), shape((nz, m // 128, 128), F32)],
        (xs, ys, parts),
        [pltpu.VMEM((n, DEPTH), BF16), pltpu.VMEM((2, n, PIECE), F32)],
        name="col_pass",
    )
    u = lax.all_to_all(u, "rows", 0, 0, axis_index_groups=z_groups)
    u = call(merge_kernel, shape((ny_, m // 128, 128), F32), (u,), name="merge")
    u = lax.all_to_all(u, "rows", 0, 0, axis_index_groups=y_groups)
    g = call(last_kernel, shape((m // 128, 128), F32), (u,), name="last")
    return f.reshape(n), g.reshape(m)


def solution(mesh):
    placed = (
        P(None, ("rows", "cols")),
        P(None, ("cols", "rows")),
        P(("rows", "cols")),
        P(("cols", "rows")),
        P("cols"),
    )
    rows, cols = mesh.shape["rows"], mesh.shape["cols"]
    nz = 8
    z_groups = [[a * nz + b for b in range(nz)] for a in range(rows // nz)]
    y_groups = [[a * nz + b for a in range(rows // nz)] for b in range(nz)]
    return jax.shard_map(
        functools.partial(local, (z_groups, y_groups, cols)),
        mesh=mesh,
        in_specs=placed,
        out_specs=(P("rows"), P("cols")),
        check_vma=False,
    )
```

time: 546 us -> 135 us (0.25)
  blocking collectives: 372 us -> 88.6 us
  matrix products: 80.7 us -> 0 us
  other arithmetic: 69.4 us -> 0 us
  Pallas kernels: 0 us -> 44.4 us
  between operations: 14.2 us -> 0.64 us
  waiting for transfers between devices: 5.87 us -> 0 us
    psum x2 -> x0, blocking collectives: 153 us -> none  [the longest x1 140 us: local(): lax.psum((col_acc * jnp.exp(col_top - whole_col)).astype(jnp.bfloat16), '...]
    pmax x2 -> x0, blocking collectives: 150 us -> none  [the longest x1 137 us: local(): lax.pmax(col_top.astype(jnp.bfloat16), 'rows').astype(col_top.dtype)]
    all_to_all x0 -> x6, blocking collectives: none -> 88.6 us  [the longest x1 20.3 us: local(): yz = lax.all_to_all(yo, 'rows', 0, 0, axis_index_groups=z_groups)]
    dot_general x8 -> x0, matrix products: 80.7 us -> none  [cost_tile(): lax.dot_general(xb, y, (((0,), (0,)), ((), ())), preferred_element_type=j...]
    all_gather x3 -> x0, blocking collectives: 68.9 us -> none  [the longest x1 45.3 us: local(): lax.all_gather(log_b.astype(jnp.bfloat16), 'rows', axis=0, tiled=True)]
    reduce_sum x10 -> x0, other arithmetic: 67.2 us -> none  [the longest x4 33.2 us: col_block(): jnp.sum(jnp.exp(expo - new_top[None, :]), axis=0)]
    pallas_call x0 -> x5, Pallas kernels: none -> 44.4 us  [call(): pl.pallas_call(kernel, out_shape=outs, in_specs=[vmem] * len(args), out_s...]
  transfers between devices with their start and end apart: 1 -> 0, of which waited for: 1 -> 0; matrix products, arithmetic and copies ran while one was open for 0% -> 0% of each run, Pallas kernels for 0% -> 0%
where the time goes in v1:
time: 135 us; the launch traced here: 134 us
  blocking collectives  88.6 us (66%)
  Pallas kernels  44.4 us (33%)
    pallas_call x5, Pallas kernels, call(): pl.pallas_call(kernel, out_shape=outs, in_specs=[vmem] * len(args), out_s...  44.4 us
    all_to_all x1, blocking collectives, local(): yz = lax.all_to_all(yo, 'rows', 0, 0, axis_index_groups=z_groups)  20.3 us
    all_to_all x1, blocking collectives, local(): lax.all_to_all(jnp.broadcast_to(yz[None], (ny_,) + yz.shape), 'rows', 0,...  19.5 us
    all_to_all x1, blocking collectives, local(): u = lax.all_to_all(u, 'rows', 0, 0, axis_index_groups=z_groups)  16.6 us
    all_to_all x1, blocking collectives, local(): xs = lax.all_to_all(xo, 'cols', 0, 0)  12.6 us
    all_to_all x1, blocking collectives, local(): u = lax.all_to_all(u, 'rows', 0, 0, axis_index_groups=y_groups)  9.98 us
    all_to_all x1, blocking collectives, local(): parts = lax.all_to_all(lse, 'cols', 0, 0)  9.57 us

profile of v1, /device:TPU:32, one launch (start us, length us, event | category | flops | bytes accessed | tf_op | source)
XLA Modules:
  0.0 133.8 jit_solution(13286936995058870514)
XLA Ops:
  0.6 1.7 %pack.1 = (bf16[8,80,256]{2,1,0:T(8,128)(2,1)}, bf16[8,80,256]{2,1,0:T(8,128)(2,1)}) custom-call(bf16[64,256]{1,0:T(8,128)(2,1)} %x_ref.1, bf16[64,256]{1,0:T(8,128)(2,1)} %y_ref.1, f32[2,128]{1,0:T(2,128)} %bitcast.10, f32[2,128]{1,0:T(2,128)} %bitcast.11, f32[64,128]{1,0:T(8,128)} %bitcast.8), custom_call_target="tpu_custom_call" | custom-call | tf_op jit(solution)/shard_map/pack/pallas_call | solution.py:214
  2.3 12.6 %all_to_all.30.x_ref = bf16[8,80,256]{2,1,0:T(8,128)(2,1)} all-to-all(bf16[8,80,256]{2,1,0:T(8,128)(2,1)} %get-tuple-element.6), channel_id=1, replica_groups=mesh['rows'=32,'cols'=8] {'cols'}, dimensions={0} | all-to-all | bytes 655360 | tf_op jit(solution)/shard_map/all_to_all | solution.py:244
  15.0 20.3 %all_to_all.31 = bf16[8,80,256]{2,1,0:T(8,128)(2,1)S(1)} all-to-all(bf16[8,80,256]{2,1,0:T(8,128)(2,1)} %get-tuple-element.7), channel_id=1, replica_groups={{0,8,16,24,32,40,48,56},{64,72,80,88,96,104,112,120},{128,136,144,152,1..., dimensions={0} | all-to-all | bytes 655360 | tf_op jit(solution)/shard_map/all_to_all | solution.py:245
  35.3 0.1 broadcast_in_dim.2
  35.4 19.5 %all_to_all.32 = bf16[4,8,80,256]{3,2,1,0:T(8,128)(2,1)} all-to-all(bf16[4,8,80,256]{3,2,1,0:T(8,128)(2,1)S(1)} %broadcast_in_dim.2), channel_id=1, replica_groups={{0,64,128,192},{8,72,136,200},{16,80,144,208},{24,88,152,216},{32,96,16..., dimensions={0} | all-to-all | bytes 2621440 | tf_op jit(solution)/shard_map/all_to_all | solution.py:246
  54.9 20.0 %row_pass.1 = f32[8,16,128]{2,1,0:T(8,128)} custom-call(bf16[8,80,256]{2,1,0:T(8,128)(2,1)} %all_to_all.30.x_ref, bf16[32,80,256]{2,1,0:T(8,128)(2,1)} %bitcast.6), custom_call_target="tpu_custom_call" | custom-call | tf_op jit(solution)/shard_map/row_pass/pallas_call | solution.py:214
  74.9 9.6 %all_to_all.33.lse_ref = f32[8,16,128]{2,1,0:T(8,128)} all-to-all(f32[8,16,128]{2,1,0:T(8,128)} %row_pass.1), channel_id=1, replica_groups=mesh['rows'=32,'cols'=8] {'cols'}, dimensions={0} | all-to-all | bytes 131072 | tf_op jit(solution)/shard_map/all_to_all | solution.py:262
  84.5 19.5 %col_pass.1 = (f32[16,128]{1,0:T(8,128)}, f32[8,64,128]{2,1,0:T(8,128)}) custom-call(bf16[8,80,256]{2,1,0:T(8,128)(2,1)} %all_to_all.30.x_ref, bf16[32,80,256]{2,1,0:T(8,128)(2,1)} %bitcast.7, f32[8,16,128]{2,1,0:T(8,128)} %all_to_all.33.lse_ref), custom_call_target="tpu_custom_call" | custom-call | tf_op jit(solution)/shard_map/col_pass/pallas_call | solution.py:214
  104.0 16.6 %all_to_all.34.u_ref = f32[8,64,128]{2,1,0:T(8,128)} all-to-all(f32[8,64,128]{2,1,0:T(8,128)} %get-tuple-element.9), channel_id=1, replica_groups={{0,8,16,24,32,40,48,56},{64,72,80,88,96,104,112,120},{128,136,144,152,1..., dimensions={0} | all-to-all | bytes 524288 | tf_op jit(solution)/shard_map/all_to_all | solution.py:270
  120.6 1.7 %merge.1 = f32[4,64,128]{2,1,0:T(8,128)} custom-call(f32[8,64,128]{2,1,0:T(8,128)} %all_to_all.34.u_ref), custom_call_target="tpu_custom_call" | custom-call | tf_op jit(solution)/shard_map/merge/pallas_call | solution.py:214
  122.3 10.0 %all_to_all.35.u_ref = f32[4,64,128]{2,1,0:T(8,128)} all-to-all(f32[4,64,128]{2,1,0:T(8,128)} %merge.1), channel_id=1, replica_groups={{0,64,128,192},{8,72,136,200},{16,80,144,208},{24,88,152,216},{32,96,16..., dimensions={0} | all-to-all | bytes 262144 | tf_op jit(solution)/shard_map/all_to_all | solution.py:272
  132.3 1.6 %last.1 = f32[64,128]{1,0:T(8,128)} custom-call(f32[4,64,128]{2,1,0:T(8,128)} %all_to_all.35.u_ref), custom_call_target="tpu_custom_call" | custom-call | tf_op jit(solution)/shard_map/last/pallas_call | solution.py:214

commit v2 on v1

v2 whole, which is shorter than its diff:
```python
import functools

import jax
import jax.numpy as jnp
from jax import lax
from jax.experimental import pallas as pl
from jax.experimental.pallas import tpu as pltpu
from jax.sharding import Mesh
from jax.sharding import PartitionSpec as P

EPS = 0.05
LOG2E = 1.4426950408889634
LN2 = 0.6931471805599453
BF16 = jnp.bfloat16
F32 = jnp.float32
PIECE = 256
EXTRA = 16
DEPTH = 256
GROUP = 16
LOW = -1e30
VMEM_LIMIT = 56 * 1024 * 1024


def split3(v):
    high = v.astype(BF16).astype(F32)
    rest = v - high
    mid = rest.astype(BF16).astype(F32)
    return high, mid, rest - mid


def wide(ref, row):
    pair = ref[pl.ds(row, 2), :]
    return jnp.concatenate([pair[0:1], pair[1:2]], axis=1)


def put_wide(ref, row, v):
    ref[pl.ds(row, 1), :] = v[:, 0:128]
    ref[pl.ds(row + 1, 1), :] = v[:, 128:256]


def rows_of(terms, count, width):
    row = lax.broadcasted_iota(jnp.int32, (count, width), 0)
    out = jnp.zeros((count, width), F32)
    for index, term in enumerate(terms):
        out = jnp.where(row == index, term, out)
    return out


def pack_kernel(x_ref, y_ref, la_ref, lb_ref, g_ref, xo_ref, yo_ref):
    feat = x_ref.shape[0]
    la = wide(la_ref, 0) * LOG2E
    y = y_ref[...].astype(F32)
    ny = jnp.sum(y * y, axis=0, keepdims=True)
    mine = lax.axis_index("y") * 8 + lax.axis_index("zh") * 2 + lax.axis_index("zl")
    g = wide(g_ref, 2 * mine)
    own = (wide(lb_ref, 0) + (g - ny / feat) / EPS) * LOG2E
    one = jnp.ones((1, PIECE), F32)
    xo_ref[0:feat, :] = x_ref[...]
    xo_ref[feat : feat + EXTRA, :] = rows_of(split3(la), EXTRA, PIECE).astype(BF16)
    yo_ref[0:feat, :] = y_ref[...]
    yo_ref[feat : feat + EXTRA, :] = rows_of(split3(own) + (one, one, one), EXTRA, PIECE).astype(BF16)


def right_side(y_ref, p):
    feat = y_ref.shape[1] - EXTRA
    y = y_ref[p, 0:feat, :]
    extra = y_ref[p, feat : feat + EXTRA, :]
    fill = jnp.zeros((DEPTH - 3 * feat - EXTRA, PIECE), BF16)
    return jnp.concatenate([y, y, y, extra, fill], axis=0)


def dot(a, b):
    return jnp.dot(a, b, preferred_element_type=F32)


IB = 2048
JP = 2


def row_kernel(*refs, scale):
    xs, ys = refs[0:4], refs[4:8]
    out_ref, a_ref, y_ref, nx_ref, la_ref, s_ref, m_ref, l_ref = refs[8:]
    feat = y_ref.shape[1] - EXTRA
    n = GROUP * PIECE
    one = jnp.ones((1, PIECE), F32)
    extra = rows_of((one, one, one), EXTRA, PIECE)
    fill = jnp.zeros((DEPTH - 3 * feat - EXTRA, PIECE), F32)
    xi, zl, core = lax.axis_index("x"), lax.axis_index("zl"), lax.axis_index("c")
    yi, zh = lax.axis_index("y"), lax.axis_index("zh")
    for k in range(4):
        for j in range(4):
            p = ((zl + j // 2) % 2 * 4 + (xi + 4 - k) % 4) * 2 + (core + j % 2) % 2
            x = xs[k][j, 0:feat, :].astype(F32)
            block = jnp.concatenate(split3(x * scale) + (extra, fill), axis=0)
            a_ref[pl.ds(pl.multiple_of(p * PIECE, PIECE), PIECE), :] = jnp.transpose(block).astype(BF16)
            put_wide(nx_ref, 2 * p, jnp.sum(x * x, axis=0, keepdims=True) / feat)
            own = xs[k][j, feat : feat + EXTRA, :].astype(F32)
            put_wide(la_ref, 2 * p, jnp.sum(own, axis=0, keepdims=True))
            y_ref[(yi + 4 - k) % 4 * 4 + (zh + 4 - j) % 4] = ys[k][j]
    m_ref[...] = jnp.full(m_ref.shape, LOW, F32)
    l_ref[...] = jnp.zeros(l_ref.shape, F32)
    blocks = n // IB
    steps = blocks * (GROUP // JP)

    def start(t, k):
        base = pl.multiple_of((t % blocks) * IB, IB)
        return dot(a_ref[pl.ds(base, IB), :], right_side(y_ref, (t // blocks) * JP + k))

    def finish(t, slot, r):
        base = pl.multiple_of((t % blocks) * IB + r, 8)
        rows = pl.ds(base, 8)
        vals = [s_ref[slot, r : r + 8, c * 128 : (c + 1) * 128] for c in range(JP * 2)]
        old = m_ref[rows, :]
        top = old
        for v in vals:
            top = jnp.maximum(top, v)
        acc = l_ref[rows, :] * jnp.exp2(old - top)
        for v in vals:
            acc = acc + jnp.exp2(v - top)
        m_ref[rows, :] = top
        l_ref[rows, :] = acc

    def half(t, slot):
        later = jnp.minimum(t + 1, steps - 1)
        for k in range(JP):
            s_ref[1 - slot, :, k * PIECE : (k + 1) * PIECE] = start(later, k)
            for r in range(k * IB // JP, (k + 1) * IB // JP, 8):
                finish(t, slot, r)

    for k in range(JP):
        s_ref[0, :, k * PIECE : (k + 1) * PIECE] = start(0, k)

    def body(u, carry):
        half(2 * u, 0)
        half(2 * u + 1, 1)
        return carry

    lax.fori_loop(0, steps // 2, body, 0)
    for q in range(n // 128):
        mt = jnp.transpose(m_ref[q * 128 : (q + 1) * 128, :])
        lt = jnp.transpose(l_ref[q * 128 : (q + 1) * 128, :])
        top = jnp.max(mt, axis=0, keepdims=True)
        lse = top + jnp.log2(jnp.sum(lt * jnp.exp2(mt - top), axis=0, keepdims=True))
        for d in range(out_ref.shape[0]):
            out_ref[d, q : q + 1, :] = lse


def col_kernel(a_in, y_ref, nx_ref, la_ref, lse_ref, f_ref, out_ref, a_ref, s_ref, fs_ref):
    feat = y_ref.shape[1] - EXTRA
    n = GROUP * PIECE
    tiles = GROUP
    part = lse_ref[...]
    top = jnp.max(part, axis=0)
    whole = top + jnp.log2(jnp.sum(jnp.exp2(part - top[None]), axis=0))
    fs_ref[...] = nx_ref[...] - (EPS * LN2) * whole
    f_ref[...] = fs_ref[pl.ds(pl.multiple_of(lax.axis_index("zl") * 16, 16), 16), :]
    own = la_ref[...] - whole
    zero = jnp.zeros((1, PIECE), F32)
    keep = 3 * feat - 128
    a_ref[:, 0:128] = a_in[:, 0:128]
    for p in range(GROUP):
        term = jnp.concatenate([own[2 * p : 2 * p + 1], own[2 * p + 1 : 2 * p + 2]], axis=1)
        extra = rows_of((zero, zero, zero) + split3(term), 128 - keep, PIECE)
        rows = slice(p * PIECE, (p + 1) * PIECE)
        a_ref[rows, 128:256] = jnp.concatenate(
            [a_in[rows, 128 : 128 + keep], jnp.transpose(extra).astype(BF16)], axis=1
        )
    chunk = 1024

    def start(t, k):
        return dot(a_ref[k * chunk : (k + 1) * chunk, :], right_side(y_ref, t))

    def fold(s, how):
        return how(s.reshape(s.shape[0] // 8, 8, s.shape[1]), axis=0)

    def half(t, slot, top):
        later = jnp.minimum(t + 1, tiles - 1)
        new = jnp.full((8, PIECE), LOW, F32)
        acc = jnp.zeros((8, PIECE), F32)
        for k in range(n // chunk):
            s = start(later, k)
            s_ref[1 - slot, k * chunk : (k + 1) * chunk, :] = s
            new = jnp.maximum(new, fold(s, jnp.max))
            for r in range(k * chunk, (k + 1) * chunk, 64):
                v = s_ref[slot, r : r + 64, :].reshape(8, 8, PIECE)
                acc = acc + jnp.sum(jnp.exp2(v - top[None]), axis=0)
        peak = jnp.max(top, axis=0, keepdims=True)
        total = jnp.sum(acc * jnp.exp2(top - peak), axis=0, keepdims=True)
        y = y_ref[t, 0:feat, :].astype(F32)
        ny = jnp.sum(y * y, axis=0, keepdims=True)
        u = peak + jnp.log2(total) - ny * (LOG2E / (feat * EPS))
        for d in range(out_ref.shape[0]):
            out_ref[d, pl.ds(2 * t, 1), :] = u[:, 0:128]
            out_ref[d, pl.ds(2 * t + 1, 1), :] = u[:, 128:256]
        return new

    top = jnp.full((8, PIECE), LOW, F32)
    for k in range(n // chunk):
        s = start(0, k)
        s_ref[0, k * chunk : (k + 1) * chunk, :] = s
        top = jnp.maximum(top, fold(s, jnp.max))

    def body(u, top):
        return half(2 * u + 1, 1, half(2 * u, 0, top))

    lax.fori_loop(0, tiles // 2, body, top)


def merge_kernel(u_ref, out_ref):
    u = u_ref[...]
    top = jnp.max(u, axis=0)
    out_ref[...] = (top + jnp.log2(jnp.sum(jnp.exp2(u - top[None]), axis=0))) * (-EPS * LN2)


def last_kernel(mine_ref, other_ref, out_ref):
    first = lax.axis_index("zl") == 0
    mine, other = mine_ref[...], other_ref[...]
    even, odd = jnp.where(first, mine, other), jnp.where(first, other, mine)
    for p in range(GROUP):
        out_ref[4 * p : 4 * p + 2, :] = even[2 * p : 2 * p + 2]
        out_ref[4 * p + 2 : 4 * p + 4, :] = odd[2 * p : 2 * p + 2]


def call(kernel, outs, args, scratch=(), name=None):
    vmem = pl.BlockSpec(memory_space=pltpu.VMEM)
    return pl.pallas_call(
        kernel,
        out_shape=outs,
        in_specs=[vmem] * len(args),
        out_specs=jax.tree.map(lambda _: vmem, outs),
        scratch_shapes=list(scratch),
        compiler_params=pltpu.CompilerParams(vmem_limit_bytes=VMEM_LIMIT),
        name=name,
    )(*args)


def ring(v, axis):
    return [v] + [lax.ppermute(v, axis, [(i, (i + k) % 4) for i in range(4)]) for k in (1, 2, 3)]


def local(x_feat, y_feat, log_a, log_b, g_init):
    feat, piece = x_feat.shape
    scale = 2.0 * LOG2E / (feat * EPS)
    shape = jax.ShapeDtypeStruct
    depth = feat + EXTRA
    n = GROUP * piece
    xo, yo = call(
        pack_kernel,
        [shape((depth, piece), BF16), shape((depth, piece), BF16)],
        (
            x_feat,
            y_feat,
            log_a.reshape(-1, 128),
            log_b.reshape(-1, 128),
            g_init.reshape(-1, 128),
        ),
        name="pack",
    )
    ya = ring(yo, "zh")
    xa = [xo] + [lax.ppermute(xo, ("zl", "c"), [(i, i ^ k) for i in range(4)]) for k in (1, 2, 3)]
    xa, ya = lax.optimization_barrier((xa, ya))
    xb = ring(jnp.stack(xa), "x")
    yb = ring(jnp.stack(ya), "y")
    lse, a, ys, nx, la = call(
        functools.partial(row_kernel, scale=scale),
        [
            shape((GROUP, n // 128, 128), F32),
            shape((n, DEPTH), BF16),
            shape((GROUP, depth, piece), BF16),
            shape((n // 128, 128), F32),
            shape((n // 128, 128), F32),
        ],
        (*xb, *yb),
        [
            pltpu.VMEM((2, IB, JP * PIECE), F32),
            pltpu.VMEM((n, 128), F32),
            pltpu.VMEM((n, 128), F32),
        ],
        name="row_pass",
    )
    parts = lax.all_to_all(lse, ("zl", "x", "c"), 0, 0)
    f, u = call(
        col_kernel,
        [shape((n // 256, 128), F32), shape((GROUP, n // 128, 128), F32)],
        (a, ys, nx, la, parts),
        [
            pltpu.VMEM((n, DEPTH), BF16),
            pltpu.VMEM((2, n, PIECE), F32),
            pltpu.VMEM((n // 128, 128), F32),
        ],
        name="col_pass",
    )
    u = lax.all_to_all(u, ("y", "zh"), 0, 0)
    mine = call(merge_kernel, shape((n // 128, 128), F32), (u,), name="merge")
    other = lax.ppermute(mine, "zl", [(0, 1), (1, 0)])
    g = call(last_kernel, shape((n // 64, 128), F32), (mine, other), name="last")
    return f.reshape(n // 2), g.reshape(2 * n)


def solution(mesh):
    inner = Mesh(mesh.devices.reshape(4, 4, 2, 4, 2), ("y", "zh", "zl", "x", "c"))
    rows, cols = ("y", "zh", "zl"), ("x", "c")
    placed = (P(None, rows + cols), P(None, cols + rows), P(rows + cols), P(cols + rows), P(cols))
    return jax.shard_map(
        local, mesh=inner, in_specs=placed, out_specs=(P(rows), P(cols)), check_vma=False
    )
```

time: 135 us -> 116 us (0.86)
  blocking collectives: 88.6 us -> 32.8 us
  starting transfers between devices: 0 us -> 21.4 us
  waiting for transfers between devices: 0 us -> 14.3 us
  other arithmetic: 0 us -> 1.6 us
    all_to_all x6 -> x2, blocking collectives: 88.6 us -> 32.8 us  [the longest x1 20.9 us: local(): u = lax.all_to_all(u, ('y', 'zh'), 0, 0)]
    ppermute x0 -> x13, starting transfers between devices: none -> 21.4 us  [the longest x9 18.5 us: ring(): lax.ppermute(v, axis, [(i, (i + k) % 4) for i in range(4)])]
    ppermute x0 -> x13, waiting for transfers between devices: none -> 14.3 us  [the longest x9 11.2 us: ring(): lax.ppermute(v, axis, [(i, (i + k) % 4) for i in range(4)])]
    another operation x0 -> x2, other arithmetic: none -> 1.6 us  [the longest x1 0.8 us: local(): yb = ring(jnp.stack(ya), 'y')]
  transfers between devices with their start and end apart: 0 -> 13, of which waited for: 0 -> 8; matrix products, arithmetic and copies ran while one was open for 0% -> 1% of each run, Pallas kernels for 0% -> 0%
where the time goes in v2:
time: 116 us; the launch traced here: 115 us
  Pallas kernels  43.5 us (38%)
  blocking collectives  32.8 us (28%)
  starting transfers between devices  21.4 us (18%)
  waiting for transfers between devices  14.3 us (12%)
  other arithmetic  1.6 us (1%)
  local copies, waits for them, and re-layouts  1.27 us (1%)
    pallas_call x5, Pallas kernels, call(): pl.pallas_call(kernel, out_shape=outs, in_specs=[vmem] * len(args), out_s...  43.5 us
    all_to_all x1, blocking collectives, local(): u = lax.all_to_all(u, ('y', 'zh'), 0, 0)  20.9 us
    ppermute x9, starting transfers between devices, ring(): lax.ppermute(v, axis, [(i, (i + k) % 4) for i in range(4)])  18.5 us
    all_to_all x1, blocking collectives, local(): parts = lax.all_to_all(lse, ('zl', 'x', 'c'), 0, 0)  11.9 us
    ppermute x9, waiting for transfers between devices, ring(): lax.ppermute(v, axis, [(i, (i + k) % 4) for i in range(4)])  11.2 us
    ppermute x1, waiting for transfers between devices, local(): other = lax.ppermute(mine, 'zl', [(0, 1), (1, 0)])  3.04 us
  transfers between devices with their start and end apart: 13, of which 8 were waited for; matrix products, arithmetic and copies ran while one was open for 1% of the time, Pallas kernels for 0%

profile of v2, /device:TPU:32, one launch (start us, length us, event | category | flops | bytes accessed | tf_op | source)
XLA Modules:
  0.0 115.5 jit_solution(5698961404240417429)
XLA Ops:
  0.6 1.5 %pack.1 = (bf16[80,256]{1,0:T(8,128)(2,1)}, bf16[80,256]{1,0:T(8,128)(2,1)}) custom-call(bf16[64,256]{1,0:T(8,128)(2,1)} %x_ref.1, bf16[64,256]{1,0:T(8,128)(2,1)} %y_ref.1, f32[2,128]{1,0:T(2,128)} %bitcast.23, f32[2,128]{1,0:T(2,128)} %bitcast.24, f32[64,128]{1,0:T(8,128)} %bitcast.21), custom_call_target="tpu_custom_call" | custom-call | tf_op jit(solution)/shard_map/pack/pallas_call | solution.py:226
  2.1 0.0 collective-permute-start.2
  2.1 1.9 %collective-permute-start.1 = (bf16[80,256]{1,0:T(8,128)(2,1)}, bf16[80,256]{1,0:T(8,128)(2,1)S(1)}, u32[]{:S(2)}, u32[]{:S(2)}) collective-permute-start(bf16[80,256]{1,0:T(8,128)(2,1)} %get-tuple-element.21), channel_id=1, source_target_pairs={{0,8},{1,9},{8,0},{9,1},{2,10},{3,11},{10,2},{11,3},{4,12},{5,13},... | collective-permute-start | bytes 122888 | tf_op jit(solution)/shard_map/ppermute | solution.py:260
  4.0 0.1 collective-permute-start
  4.1 5.3 %collective-permute-start.5 = (bf16[80,256]{1,0:T(8,128)(2,1)}, bf16[80,256]{1,0:T(8,128)(2,1)S(1)}, u32[]{:S(2)}, u32[]{:S(2)}) collective-permute-start(bf16[80,256]{1,0:T(8,128)(2,1)} %get-tuple-element.25), channel_id=1, source_target_pairs={{0,48},{16,0},{32,16},{48,32},{1,49},{17,1},{33,17},{49,33},{2,50}... | collective-permute-start | bytes 122888 | tf_op jit(solution)/shard_map/ppermute | solution.py:238
  9.4 1.4 %collective-permute-start.4 = (bf16[80,256]{1,0:T(8,128)(2,1)}, bf16[80,256]{1,0:T(8,128)(2,1)S(1)}, u32[]{:S(2)}, u32[]{:S(2)}) collective-permute-start(bf16[80,256]{1,0:T(8,128)(2,1)} %get-tuple-element.25), channel_id=1, source_target_pairs={{0,32},{16,48},{32,0},{48,16},{1,33},{17,49},{33,1},{49,17},{2,34}... | collective-permute-start | bytes 122888 | tf_op jit(solution)/shard_map/ppermute | solution.py:238
  10.8 0.0 collective-permute-done.2
  10.8 2.4 %collective-permute-start.3 = (bf16[80,256]{1,0:T(8,128)(2,1)}, bf16[80,256]{1,0:T(8,128)(2,1)S(1)}, u32[]{:S(2)}, u32[]{:S(2)}) collective-permute-start(bf16[80,256]{1,0:T(8,128)(2,1)} %get-tuple-element.25), channel_id=1, source_target_pairs={{0,16},{16,32},{32,48},{48,0},{1,17},{17,33},{33,49},{49,1},{2,18}... | collective-permute-start | bytes 122888 | tf_op jit(solution)/shard_map/ppermute | solution.py:238
  13.2 0.0 collective-permute-done.1
  13.2 0.0 collective-permute-done
  13.2 0.0 collective-permute-done.5
  13.2 4.3 %collective-permute-done.4 = bf16[80,256]{1,0:T(8,128)(2,1)S(1)} collective-permute-done((bf16[80,256]{1,0:T(8,128)(2,1)}, bf16[80,256]{1,0:T(8,128)(2,1)S(1)}, u32[]{:S(2)}, u32[]{:S(2)}) %collective-permute-start.4) | collective-permute-done | bytes 40992 | tf_op jit(solution)/shard_map/ppermute | solution.py:238
  17.5 0.2 collective-permute-done.3
  17.7 0.8 pad_maximum_fusion.1.refs_4_
  18.5 0.0 copy-start
  18.5 3.1 %collective-permute-start.11 = (bf16[4,80,256]{2,1,0:T(8,128)(2,1)S(1)}, bf16[4,80,256]{2,1,0:T(8,128)(2,1)S(1)}, u32[]{:S(2)}, u32[]{:S(2)}) collective-permute-start(bf16[4,80,256]{2,1,0:T(8,128)(2,1)S(1)} %pad_maximum_fusion.1.refs_4_), channel_id=1, source_target_pairs={{0,192},{64,0},{128,64},{192,128},{1,193},{65,1},{129,65},{193,129... | collective-permute-start | bytes 491528 | tf_op jit(solution)/shard_map/ppermute | solution.py:238
  21.6 0.6 collective-permute-start.10
  22.3 1.0 collective-permute-start.9
  23.2 0.8 pad_maximum_fusion.refs_0_
  24.0 0.0 copy-start.1
  24.1 2.8 %collective-permute-start.8 = (bf16[4,80,256]{2,1,0:T(8,128)(2,1)S(1)}, bf16[4,80,256]{2,1,0:T(8,128)(2,1)S(1)}, u32[]{:S(2)}, u32[]{:S(2)}) collective-permute-start(bf16[4,80,256]{2,1,0:T(8,128)(2,1)S(1)} %pad_maximum_fusion.refs_0_), channel_id=1, source_target_pairs={{0,6},{2,0},{4,2},{6,4},{1,7},{3,1},{5,3},{7,5},{8,14},{10,8},{12,... | collective-permute-start | bytes 491528 | tf_op jit(solution)/shard_map/ppermute | solution.py:238
  26.9 0.8 collective-permute-start.7
  27.7 0.0 collective-permute-done.11.refs_7_
  27.7 0.0 copy-start.2
  27.7 1.1 collective-permute-start.6
  28.8 0.5 collective-permute-done.10.refs_6_
  29.3 0.0 copy-start.3
  29.3 1.7 %collective-permute-done.9.refs_5_ = bf16[4,80,256]{2,1,0:T(8,128)(2,1)S(1)} collective-permute-done((bf16[4,80,256]{2,1,0:T(8,128)(2,1)S(1)}, bf16[4,80,256]{2,1,0:T(8,128)(2,1)S(1)}, u32[]{:S(2)}, u32[]{:S(2)}) %collective-permute-start.9) | collective-permute-done | bytes 163872 | tf_op jit(solution)/shard_map/ppermute | solution.py:238
  30.9 0.0 copy-start.4
  30.9 0.7 collective-permute-done.8.refs_3_
  31.7 0.0 copy-start.5
  31.7 2.1 %collective-permute-done.7.refs_2_ = bf16[4,80,256]{2,1,0:T(8,128)(2,1)S(1)} collective-permute-done((bf16[4,80,256]{2,1,0:T(8,128)(2,1)S(1)}, bf16[4,80,256]{2,1,0:T(8,128)(2,1)S(1)}, u32[]{:S(2)}, u32[]{:S(2)}) %collective-permute-start.7) | collective-permute-done | bytes 163872 | tf_op jit(solution)/shard_map/ppermute | solution.py:238
  33.8 0.0 copy-start.6
  33.8 1.6 %collective-permute-done.6.refs_1_ = bf16[4,80,256]{2,1,0:T(8,128)(2,1)S(1)} collective-permute-done((bf16[4,80,256]{2,1,0:T(8,128)(2,1)S(1)}, bf16[4,80,256]{2,1,0:T(8,128)(2,1)S(1)}, u32[]{:S(2)}, u32[]{:S(2)}) %collective-permute-start.6) | collective-permute-done | bytes 163872 | tf_op jit(solution)/shard_map/ppermute | solution.py:238
  35.5 0.0 copy-done
  35.5 0.0 copy-done.1
  35.5 0.0 copy-done.2
  35.5 0.0 copy-done.3
  35.5 0.0 copy-done.4
  35.5 0.0 copy-done.5
  35.5 0.0 copy-done.6
  35.5 0.0 copy-start.7
  35.5 0.6 copy-done.7
  36.2 19.7 %row_pass.1 = (f32[16,32,128]{2,1,0:T(8,128)}, bf16[4096,256]{1,0:T(8,128)(2,1)}, bf16[16,80,256]{2,1,0:T(8,128)(2,1)}, f32[32,128]{1,0:T(8,128)}, f32[32,128]{1,0:T(8,128)}) custom-call(bf16[4,80,256]{2,1,0:T(8,128)(2,1)} %copy-done.1, bf16[4,80,256]{2,1,0:T(8,128)(2,1)} %copy-done.7, bf16[4,80,256]{2,1,0:T(8,128)(2,1)} %copy-done.6, ...), custom_call_target="tpu_custom_call" | custom-call | tf_op jit(solution)/shard_map/row_pass/pallas_call | solution.py:226
  55.9 11.9 %all_to_all.10.lse_ref = f32[16,32,128]{2,1,0:T(8,128)} all-to-all(f32[16,32,128]{2,1,0:T(8,128)} %get-tuple-element.33), channel_id=1, replica_groups=mesh['y'=4,'zh'=4,'zl'=2,'x'=4,'c'=2] {'zl','x','c'}, dimensions={0} | all-to-all | bytes 524288 | tf_op jit(solution)/shard_map/all_to_all | solution.py:281
  67.8 19.3 %col_pass.1 = (f32[16,128]{1,0:T(8,128)}, f32[16,32,128]{2,1,0:T(8,128)}) custom-call(bf16[4096,256]{1,0:T(8,128)(2,1)} %get-tuple-element.29.a_in, bf16[16,80,256]{2,1,0:T(8,128)(2,1)} %get-tuple-element.30.y_ref, f32[32,128]{1,0:T(8,128)} %get-tuple-element.31.nx_ref, f32[32,128]{1,0:T(8,128)} %get-tuple-element.32.la_ref, f32[16,32,128]{2,1,0:T(8,128)} %all_to_all.10.lse_ref), custom_call_target="tpu_custom_call" | custom-call | tf_op jit(solution)/shard_map/col_pass/pallas_call | solution.py:226
  87.1 20.9 %all_to_all.11.u_ref = f32[16,32,128]{2,1,0:T(8,128)} all-to-all(f32[16,32,128]{2,1,0:T(8,128)} %get-tuple-element.35), channel_id=1, replica_groups=mesh['y'=4,'zh'=4,'zl'=2,'x'=4,'c'=2] {'y','zh'}, dimensions={0} | all-to-all | bytes 524288 | tf_op jit(solution)/shard_map/all_to_all | solution.py:293
  108.0 1.6 %merge.1.mine_ref = f32[32,128]{1,0:T(8,128)} custom-call(f32[16,32,128]{2,1,0:T(8,128)} %all_to_all.11.u_ref), custom_call_target="tpu_custom_call" | custom-call | tf_op jit(solution)/shard_map/merge/pallas_call | solution.py:226
  109.6 0.9 collective-permute-start.12
  110.5 3.0 %collective-permute-done.12.other_ref = f32[32,128]{1,0:T(8,128)S(1)} collective-permute-done((f32[32,128]{1,0:T(8,128)}, f32[32,128]{1,0:T(8,128)S(1)}, u32[]{:S(2)}, u32[]{:S(2)}) %collective-permute-start.12) | collective-permute-done | bytes 16416 | tf_op jit(solution)/shard_map/ppermute | solution.py:295
  113.5 0.0 copy-start.8
  113.5 0.6 copy-done.8
  114.1 1.4 %last.1 = f32[64,128]{1,0:T(8,128)} custom-call(f32[32,128]{1,0:T(8,128)} %merge.1.mine_ref, f32[32,128]{1,0:T(8,128)} %copy-done.8), custom_call_target="tpu_custom_call" | custom-call | tf_op jit(solution)/shard_map/last/pallas_call | solution.py:226
Async XLA Ops:
  2.1 8.7 %collective-permute-start.2 = (bf16[80,256]{1,0:T(8,128)(2,1)}, bf16[80,256]{1,0:T(8,128)(2,1)S(1)}, u32[]{:S(2)}, u32[]{:S(2)}) collective-permute-start(bf16[80,256]{1,0:T(8,128)(2,1)} %get-tuple-element.21), channel_id=1, source_target_pairs={{0,9},{1,8},{8,1},{9,0},{2,11},{3,10},{10,3},{11,2},{4,13},{5,12},... | collective-permute-start | bytes 122888 | tf_op jit(solution)/shard_map/ppermute | solution.py:260
  2.1 11.1 %collective-permute-start.1 = (bf16[80,256]{1,0:T(8,128)(2,1)}, bf16[80,256]{1,0:T(8,128)(2,1)S(1)}, u32[]{:S(2)}, u32[]{:S(2)}) collective-permute-start(bf16[80,256]{1,0:T(8,128)(2,1)} %get-tuple-element.21), channel_id=1, source_target_pairs={{0,8},{1,9},{8,0},{9,1},{2,10},{3,11},{10,2},{11,3},{4,12},{5,13},... | collective-permute-start | bytes 122888 | tf_op jit(solution)/shard_map/ppermute | solution.py:260
  4.0 9.2 %collective-permute-start = (bf16[80,256]{1,0:T(8,128)(2,1)}, bf16[80,256]{1,0:T(8,128)(2,1)S(1)}, u32[]{:S(2)}, u32[]{:S(2)}) collective-permute-start(bf16[80,256]{1,0:T(8,128)(2,1)} %get-tuple-element.21), channel_id=1, source_target_pairs={{0,1},{1,0},{8,9},{9,8},{2,3},{3,2},{10,11},{11,10},{4,5},{5,4},{1... | collective-permute-start | bytes 122888 | tf_op jit(solution)/shard_map/ppermute | solution.py:260
  4.1 9.1 %collective-permute-start.5 = (bf16[80,256]{1,0:T(8,128)(2,1)}, bf16[80,256]{1,0:T(8,128)(2,1)S(1)}, u32[]{:S(2)}, u32[]{:S(2)}) collective-permute-start(bf16[80,256]{1,0:T(8,128)(2,1)} %get-tuple-element.25), channel_id=1, source_target_pairs={{0,48},{16,0},{32,16},{48,32},{1,49},{17,1},{33,17},{49,33},{2,50}... | collective-permute-start | bytes 122888 | tf_op jit(solution)/shard_map/ppermute | solution.py:238
  9.4 8.1 %collective-permute-start.4 = (bf16[80,256]{1,0:T(8,128)(2,1)}, bf16[80,256]{1,0:T(8,128)(2,1)S(1)}, u32[]{:S(2)}, u32[]{:S(2)}) collective-permute-start(bf16[80,256]{1,0:T(8,128)(2,1)} %get-tuple-element.25), channel_id=1, source_target_pairs={{0,32},{16,48},{32,0},{48,16},{1,33},{17,49},{33,1},{49,17},{2,34}... | collective-permute-start | bytes 122888 | tf_op jit(solution)/shard_map/ppermute | solution.py:238
  10.8 6.9 %collective-permute-start.3 = (bf16[80,256]{1,0:T(8,128)(2,1)}, bf16[80,256]{1,0:T(8,128)(2,1)S(1)}, u32[]{:S(2)}, u32[]{:S(2)}) collective-permute-start(bf16[80,256]{1,0:T(8,128)(2,1)} %get-tuple-element.25), channel_id=1, source_target_pairs={{0,16},{16,32},{32,48},{48,0},{1,17},{17,33},{33,49},{49,1},{2,18}... | collective-permute-start | bytes 122888 | tf_op jit(solution)/shard_map/ppermute | solution.py:238
  18.5 16.9 %copy-start = (bf16[4,80,256]{2,1,0:T(8,128)(2,1)}, bf16[4,80,256]{2,1,0:T(8,128)(2,1)S(1)}, u32[]{:S(2)}) copy-start(bf16[4,80,256]{2,1,0:T(8,128)(2,1)S(1)} %pad_maximum_fusion.1.refs_4_) | copy-start | bytes 491524
  18.5 9.2 %collective-permute-start.11 = (bf16[4,80,256]{2,1,0:T(8,128)(2,1)S(1)}, bf16[4,80,256]{2,1,0:T(8,128)(2,1)S(1)}, u32[]{:S(2)}, u32[]{:S(2)}) collective-permute-start(bf16[4,80,256]{2,1,0:T(8,128)(2,1)S(1)} %pad_maximum_fusion.1.refs_4_), channel_id=1, source_target_pairs={{0,192},{64,0},{128,64},{192,128},{1,193},{65,1},{129,65},{193,129... | collective-permute-start | bytes 491528 | tf_op jit(solution)/shard_map/ppermute | solution.py:238
  21.6 7.6 %collective-permute-start.10 = (bf16[4,80,256]{2,1,0:T(8,128)(2,1)S(1)}, bf16[4,80,256]{2,1,0:T(8,128)(2,1)S(1)}, u32[]{:S(2)}, u32[]{:S(2)}) collective-permute-start(bf16[4,80,256]{2,1,0:T(8,128)(2,1)S(1)} %pad_maximum_fusion.1.refs_4_), channel_id=1, source_target_pairs={{0,128},{64,192},{128,0},{192,64},{1,129},{65,193},{129,1},{193,65... | collective-permute-start | bytes 491528 | tf_op jit(solution)/shard_map/ppermute | solution.py:238
  22.3 8.7 %collective-permute-start.9 = (bf16[4,80,256]{2,1,0:T(8,128)(2,1)S(1)}, bf16[4,80,256]{2,1,0:T(8,128)(2,1)S(1)}, u32[]{:S(2)}, u32[]{:S(2)}) collective-permute-start(bf16[4,80,256]{2,1,0:T(8,128)(2,1)S(1)} %pad_maximum_fusion.1.refs_4_), channel_id=1, source_target_pairs={{0,64},{64,128},{128,192},{192,0},{1,65},{65,129},{129,193},{193,1... | collective-permute-start | bytes 491528 | tf_op jit(solution)/shard_map/ppermute | solution.py:238
  24.0 11.4 %copy-start.1 = (bf16[4,80,256]{2,1,0:T(8,128)(2,1)}, bf16[4,80,256]{2,1,0:T(8,128)(2,1)S(1)}, u32[]{:S(2)}) copy-start(bf16[4,80,256]{2,1,0:T(8,128)(2,1)S(1)} %pad_maximum_fusion.refs_0_) | copy-start | bytes 491524
  24.1 7.6 %collective-permute-start.8 = (bf16[4,80,256]{2,1,0:T(8,128)(2,1)S(1)}, bf16[4,80,256]{2,1,0:T(8,128)(2,1)S(1)}, u32[]{:S(2)}, u32[]{:S(2)}) collective-permute-start(bf16[4,80,256]{2,1,0:T(8,128)(2,1)S(1)} %pad_maximum_fusion.refs_0_), channel_id=1, source_target_pairs={{0,6},{2,0},{4,2},{6,4},{1,7},{3,1},{5,3},{7,5},{8,14},{10,8},{12,... | collective-permute-start | bytes 491528 | tf_op jit(solution)/shard_map/ppermute | solution.py:238
  26.9 6.9 %collective-permute-start.7 = (bf16[4,80,256]{2,1,0:T(8,128)(2,1)S(1)}, bf16[4,80,256]{2,1,0:T(8,128)(2,1)S(1)}, u32[]{:S(2)}, u32[]{:S(2)}) collective-permute-start(bf16[4,80,256]{2,1,0:T(8,128)(2,1)S(1)} %pad_maximum_fusion.refs_0_), channel_id=1, source_target_pairs={{0,4},{2,6},{4,0},{6,2},{1,5},{3,7},{5,1},{7,3},{8,12},{10,14},{12... | collective-permute-start | bytes 491528 | tf_op jit(solution)/shard_map/ppermute | solution.py:238
  27.7 7.8 %copy-start.2 = (bf16[4,80,256]{2,1,0:T(8,128)(2,1)}, bf16[4,80,256]{2,1,0:T(8,128)(2,1)S(1)}, u32[]{:S(2)}) copy-start(bf16[4,80,256]{2,1,0:T(8,128)(2,1)S(1)} %collective-permute-done.11.refs_7_) | copy-start | bytes 491524
  27.7 7.8 %collective-permute-start.6 = (bf16[4,80,256]{2,1,0:T(8,128)(2,1)S(1)}, bf16[4,80,256]{2,1,0:T(8,128)(2,1)S(1)}, u32[]{:S(2)}, u32[]{:S(2)}) collective-permute-start(bf16[4,80,256]{2,1,0:T(8,128)(2,1)S(1)} %pad_maximum_fusion.refs_0_), channel_id=1, source_target_pairs={{0,2},{2,4},{4,6},{6,0},{1,3},{3,5},{5,7},{7,1},{8,10},{10,12},{12... | collective-permute-start | bytes 491528 | tf_op jit(solution)/shard_map/ppermute | solution.py:238
  29.3 6.2 %copy-start.3 = (bf16[4,80,256]{2,1,0:T(8,128)(2,1)}, bf16[4,80,256]{2,1,0:T(8,128)(2,1)S(1)}, u32[]{:S(2)}) copy-start(bf16[4,80,256]{2,1,0:T(8,128)(2,1)S(1)} %collective-permute-done.10.refs_6_) | copy-start | bytes 491524
  30.9 4.6 %copy-start.4 = (bf16[4,80,256]{2,1,0:T(8,128)(2,1)}, bf16[4,80,256]{2,1,0:T(8,128)(2,1)S(1)}, u32[]{:S(2)}) copy-start(bf16[4,80,256]{2,1,0:T(8,128)(2,1)S(1)} %collective-permute-done.9.refs_5_) | copy-start | bytes 491524
  31.7 3.8 %copy-start.5 = (bf16[4,80,256]{2,1,0:T(8,128)(2,1)}, bf16[4,80,256]{2,1,0:T(8,128)(2,1)S(1)}, u32[]{:S(2)}) copy-start(bf16[4,80,256]{2,1,0:T(8,128)(2,1)S(1)} %collective-permute-done.8.refs_3_) | copy-start | bytes 491524
  33.8 1.7 %copy-start.6 = (bf16[4,80,256]{2,1,0:T(8,128)(2,1)}, bf16[4,80,256]{2,1,0:T(8,128)(2,1)S(1)}, u32[]{:S(2)}) copy-start(bf16[4,80,256]{2,1,0:T(8,128)(2,1)S(1)} %collective-permute-done.7.refs_2_) | copy-start | bytes 491524
  35.5 0.7 copy-start.7
  109.6 3.9 %collective-permute-start.12 = (f32[32,128]{1,0:T(8,128)}, f32[32,128]{1,0:T(8,128)S(1)}, u32[]{:S(2)}, u32[]{:S(2)}) collective-permute-start(f32[32,128]{1,0:T(8,128)} %merge.1.mine_ref), channel_id=1, source_target_pairs={{0,8},{8,0},{1,9},{9,1},{2,10},{10,2},{3,11},{11,3},{4,12},{12,4},... | collective-permute-start | bytes 49160 | tf_op jit(solution)/shard_map/ppermute | solution.py:295
  113.5 0.6 copy-start.8

commit v3 on v2

v3 whole, which is shorter than its diff:
```python
import functools

import jax
import jax.numpy as jnp
from jax import lax
from jax.experimental import pallas as pl
from jax.experimental.pallas import tpu as pltpu
from jax.sharding import Mesh
from jax.sharding import PartitionSpec as P

EPS = 0.05
LOG2E = 1.4426950408889634
LN2 = 0.6931471805599453
BF16 = jnp.bfloat16
F32 = jnp.float32
PIECE = 256
EXTRA = 16
DEPTH = 256
GROUP = 16
LOW = -1e30
VMEM_LIMIT = 24 * 1024 * 1024


def split3(v):
    high = v.astype(BF16).astype(F32)
    rest = v - high
    mid = rest.astype(BF16).astype(F32)
    return high, mid, rest - mid


def wide(ref, row):
    pair = ref[pl.ds(row, 2), :]
    return jnp.concatenate([pair[0:1], pair[1:2]], axis=1)


def put_wide(ref, row, v):
    ref[pl.ds(row, 1), :] = v[:, 0:128]
    ref[pl.ds(row + 1, 1), :] = v[:, 128:256]


def rows_of(terms, count, width):
    row = lax.broadcasted_iota(jnp.int32, (count, width), 0)
    out = jnp.zeros((count, width), F32)
    for index, term in enumerate(terms):
        out = jnp.where(row == index, term, out)
    return out


def pack_kernel(x_ref, y_ref, la_ref, lb_ref, g_ref, xo_ref, yo_ref):
    feat = x_ref.shape[0]
    la = wide(la_ref, 0) * LOG2E
    y = y_ref[...].astype(F32)
    ny = jnp.sum(y * y, axis=0, keepdims=True)
    mine = lax.axis_index("y") * 8 + lax.axis_index("zh") * 2 + lax.axis_index("zl")
    g = wide(g_ref, 2 * mine)
    own = (wide(lb_ref, 0) + (g - ny / feat) / EPS) * LOG2E
    one = jnp.ones((1, PIECE), F32)
    xo_ref[0:feat, :] = x_ref[...]
    xo_ref[feat : feat + EXTRA, :] = rows_of(split3(la) + (one, one, one), EXTRA, PIECE).astype(BF16)
    yo_ref[0:feat, :] = y_ref[...]
    yo_ref[feat : feat + EXTRA, :] = rows_of(split3(own) + (one, one, one), EXTRA, PIECE).astype(BF16)


def left_side(ref, scale, term):
    feat = ref.shape[0] - EXTRA
    zero = jnp.zeros((1, PIECE), F32)
    extra = rows_of((zero, zero, zero) + split3(term), DEPTH - 3 * feat, PIECE)
    parts = split3(ref[0:feat, :].astype(F32) * scale)
    return jnp.transpose(jnp.concatenate(parts + (extra,), axis=0)).astype(BF16)


def right_side(ref, p):
    feat = ref.shape[1] - EXTRA
    v = ref[p, 0:feat, :]
    extra = ref[p, feat : feat + EXTRA, :]
    fill = jnp.zeros((DEPTH - 3 * feat - EXTRA, PIECE), BF16)
    return jnp.concatenate([v, v, v, extra, fill], axis=0)


def own_term(ref):
    feat = ref.shape[0] - EXTRA
    row = lax.broadcasted_iota(jnp.int32, (EXTRA, PIECE), 0)
    extra = ref[feat : feat + EXTRA, :].astype(F32)
    return jnp.sum(jnp.where(row < 3, extra, 0.0), axis=0, keepdims=True)


def norm(ref):
    feat = ref.shape[0] - EXTRA
    v = ref[0:feat, :].astype(F32)
    return jnp.sum(v * v, axis=0, keepdims=True)


def fold(s, how):
    return how(s.reshape(s.shape[0] // 8, 8, s.shape[1]), axis=0)


CHUNK = 1024
SAMPLE = 256
ROOM = 100.0


def sweep(a_ref, r_ref, top_ref, peak_ref, acc_ref):
    n, tiles = a_ref.shape[0], r_ref.shape[0]

    def dot(first, count, right):
        return jnp.dot(a_ref[first : first + count, :], right, preferred_element_type=F32)

    def sample(t):
        return jnp.max(dot(0, SAMPLE, right_side(r_ref, t)), axis=0, keepdims=True)

    def total(t, top, peak):
        right = right_side(r_ref, t)
        acc = jnp.zeros((8, PIECE), F32)
        for first in range(0, n, CHUNK):
            s = dot(first, CHUNK, right)
            if peak is not None:
                peak = jnp.maximum(peak, fold(s, jnp.max))
            acc = acc + fold(jnp.exp2(s - top), jnp.sum)
        top_ref[t] = jnp.broadcast_to(top, (8, PIECE))
        acc_ref[t] = acc
        return peak

    def body(u, top):
        for t in (2 * u, 2 * u + 1):
            peak_ref[t] = total(t, top, jnp.full((8, PIECE), LOW, F32))
            top = sample(jnp.minimum(t + 1, tiles - 1))
        return top

    lax.fori_loop(0, tiles // 2, body, sample(0))

    @pl.when(jnp.max(peak_ref[...] - top_ref[...]) > ROOM)
    def _():
        def again(t, carry):
            @pl.when(jnp.max(peak_ref[t] - top_ref[t]) > ROOM)
            def _():
                total(t, jnp.max(peak_ref[t], axis=0, keepdims=True), None)

            return carry

        lax.fori_loop(0, tiles, again, 0)


def lse_of(top_ref, acc_ref, t):
    return top_ref[t, 0:1, :] + jnp.log2(jnp.sum(acc_ref[t], axis=0, keepdims=True))


def row_kernel(*refs, scale):
    xs, ys = refs[0:4], refs[4:8]
    out_ref, x_ref, y_ref, a_ref, top_ref, peak_ref, acc_ref = refs[8:]
    xi, zl, core = lax.axis_index("x"), lax.axis_index("zl"), lax.axis_index("c")
    yi, zh = lax.axis_index("y"), lax.axis_index("zh")
    for k in range(4):
        for j in range(4):
            x_ref[((zl + j // 2) % 2 * 4 + (xi + 4 - k) % 4) * 2 + (core + j % 2) % 2] = xs[k][j]
            y_ref[(yi + 4 - k) % 4 * 4 + (zh + 4 - j) % 4] = ys[k][j]
            p = 4 * k + j
            left = left_side(ys[k].at[j], scale, own_term(ys[k].at[j]))
            a_ref[p * PIECE : (p + 1) * PIECE, :] = left
    sweep(a_ref, x_ref, top_ref, peak_ref, acc_ref)
    for p in range(GROUP):
        lse = lse_of(top_ref, acc_ref, p)
        for d in range(out_ref.shape[0]):
            put_wide(out_ref.at[d], 2 * p, lse)


def col_kernel(x_ref, y_ref, lse_ref, f_ref, out_ref, a_ref, top_ref, peak_ref, acc_ref, fs_ref, *, scale):
    feat = x_ref.shape[1] - EXTRA
    part = lse_ref[...]
    top = jnp.max(part, axis=0)
    whole = top + jnp.log2(jnp.sum(jnp.exp2(part - top[None]), axis=0))
    for p in range(GROUP):
        lse = jnp.concatenate([whole[2 * p : 2 * p + 1], whole[2 * p + 1 : 2 * p + 2]], axis=1)
        put_wide(fs_ref, 2 * p, norm(x_ref.at[p]) / feat - (EPS * LN2) * lse)
        left = left_side(x_ref.at[p], scale, own_term(x_ref.at[p]) - lse)
        a_ref[p * PIECE : (p + 1) * PIECE, :] = left
    f_ref[...] = fs_ref[pl.ds(pl.multiple_of(lax.axis_index("zl") * GROUP, GROUP), GROUP), :]
    sweep(a_ref, y_ref, top_ref, peak_ref, acc_ref)
    for p in range(GROUP):
        u = lse_of(top_ref, acc_ref, p) - norm(y_ref.at[p]) * (LOG2E / (feat * EPS))
        for d in range(out_ref.shape[0]):
            put_wide(out_ref.at[d], 2 * p, u)


def merge_kernel(u_ref, out_ref):
    u = u_ref[...]
    top = jnp.max(u, axis=0)
    out_ref[...] = (top + jnp.log2(jnp.sum(jnp.exp2(u - top[None]), axis=0))) * (-EPS * LN2)


def last_kernel(mine_ref, other_ref, out_ref):
    first = lax.axis_index("zl") == 0
    mine, other = mine_ref[...], other_ref[...]
    even, odd = jnp.where(first, mine, other), jnp.where(first, other, mine)
    for p in range(GROUP):
        out_ref[4 * p : 4 * p + 2, :] = even[2 * p : 2 * p + 2]
        out_ref[4 * p + 2 : 4 * p + 4, :] = odd[2 * p : 2 * p + 2]


def call(kernel, outs, args, scratch=(), name=None):
    vmem = pl.BlockSpec(memory_space=pltpu.VMEM)
    return pl.pallas_call(
        kernel,
        out_shape=outs,
        in_specs=[vmem] * len(args),
        out_specs=jax.tree.map(lambda _: vmem, outs),
        scratch_shapes=list(scratch),
        compiler_params=pltpu.CompilerParams(vmem_limit_bytes=VMEM_LIMIT),
        name=name,
    )(*args)


def ring(v, axis):
    return [v] + [lax.ppermute(v, axis, [(i, (i + k) % 4) for i in range(4)]) for k in (1, 2, 3)]


def local(x_feat, y_feat, log_a, log_b, g_init):
    feat, piece = x_feat.shape
    scale = 2.0 * LOG2E / (feat * EPS)
    shape = jax.ShapeDtypeStruct
    depth = feat + EXTRA
    n = GROUP * piece
    xo, yo = call(
        pack_kernel,
        [shape((depth, piece), BF16), shape((depth, piece), BF16)],
        (
            x_feat,
            y_feat,
            log_a.reshape(-1, 128),
            log_b.reshape(-1, 128),
            g_init.reshape(-1, 128),
        ),
        name="pack",
    )
    ya = ring(yo, "zh")
    xa = [xo] + [lax.ppermute(xo, ("zl", "c"), [(i, i ^ k) for i in range(4)]) for k in (1, 2, 3)]
    xa, ya = lax.optimization_barrier((xa, ya))
    xb = ring(jnp.stack(xa), "x")
    yb = ring(jnp.stack(ya), "y")
    left = pltpu.VMEM((n, DEPTH), BF16)
    stats = [pltpu.VMEM((GROUP, 8, piece), F32)] * 3
    pieces = shape((GROUP, depth, piece), BF16)
    spread = shape((GROUP, n // 128, 128), F32)
    lse, xs, ys = call(
        functools.partial(row_kernel, scale=scale),
        [spread, pieces, pieces],
        (*xb, *yb),
        [left] + stats,
        name="row_pass",
    )
    parts = lax.all_to_all(lse, ("zl", "x", "c"), 0, 0)
    f, u = call(
        functools.partial(col_kernel, scale=scale),
        [shape((n // 256, 128), F32), spread],
        (xs, ys, parts),
        [left] + stats + [pltpu.VMEM((n // 128, 128), F32)],
        name="col_pass",
    )
    u = lax.all_to_all(u, ("y", "zh"), 0, 0)
    mine = call(merge_kernel, shape((n // 128, 128), F32), (u,), name="merge")
    other = lax.ppermute(mine, "zl", [(0, 1), (1, 0)])
    g = call(last_kernel, shape((n // 64, 128), F32), (mine, other), name="last")
    return f.reshape(n // 2), g.reshape(2 * n)


def solution(mesh):
    inner = Mesh(mesh.devices.reshape(4, 4, 2, 4, 2), ("y", "zh", "zl", "x", "c"))
    rows, cols = ("y", "zh", "zl"), ("x", "c")
    placed = (P(None, rows + cols), P(None, cols + rows), P(rows + cols), P(cols + rows), P(cols))
    return jax.shard_map(
        local, mesh=inner, in_specs=placed, out_specs=(P(rows), P(cols)), check_vma=False
    )
```

time: 116 us -> 104 us (0.90)
  Pallas kernels: 43.5 us -> 29.1 us
  local copies, waits for them, and re-layouts: 1.27 us -> 2.95 us
  other arithmetic: 1.6 us -> 0.05 us
  blocking collectives: 32.8 us -> 34 us
    pallas_call x5, Pallas kernels: 43.5 us -> 29.1 us  [call(): pl.pallas_call(kernel, out_shape=outs, in_specs=[vmem] * len(args), out_s...]
    unnamed x18 -> x10, local copies, waits for them, and re-layouts: 1.27 us -> 2.95 us
    all_to_all x1, blocking collectives: 11.9 us -> 13.4 us  [local(): parts = lax.all_to_all(lse, ('zl', 'x', 'c'), 0, 0)]
  transfers between devices with their start and end apart: 13 -> 13, of which waited for: 8 -> 8; matrix products, arithmetic and copies ran while one was open for 1% -> 0% of each run, Pallas kernels for 0% -> 0%
where the time goes in v3:
time: 104 us; the launch traced here: 103 us
  blocking collectives  34 us (33%)
  Pallas kernels  29.1 us (28%)
  starting transfers between devices  21.8 us (21%)
  waiting for transfers between devices  14 us (13%)
  local copies, waits for them, and re-layouts  2.95 us (3%)
    pallas_call x5, Pallas kernels, call(): pl.pallas_call(kernel, out_shape=outs, in_specs=[vmem] * len(args), out_s...  29.1 us
    all_to_all x1, blocking collectives, local(): u = lax.all_to_all(u, ('y', 'zh'), 0, 0)  20.5 us
    ppermute x9, starting transfers between devices, ring(): lax.ppermute(v, axis, [(i, (i + k) % 4) for i in range(4)])  19.3 us
    all_to_all x1, blocking collectives, local(): parts = lax.all_to_all(lse, ('zl', 'x', 'c'), 0, 0)  13.4 us
    ppermute x9, waiting for transfers between devices, ring(): lax.ppermute(v, axis, [(i, (i + k) % 4) for i in range(4)])  10.6 us
    ppermute x1, waiting for transfers between devices, local(): other = lax.ppermute(mine, 'zl', [(0, 1), (1, 0)])  3.38 us
    unnamed x10, local copies, waits for them, and re-layouts  2.95 us
  transfers between devices with their start and end apart: 13, of which 8 were waited for; matrix products, arithmetic and copies ran while one was open for 0% of the time, Pallas kernels for 0%

profile of v3, /device:TPU:32, one launch (start us, length us, event | category | flops | bytes accessed | tf_op | source)
XLA Modules:
  0.0 102.5 jit_solution(4500331827965372375)
XLA Ops:
  0.6 0.0 copy-start.4
  0.6 0.0 copy-start.3
  0.7 0.7 copy-done.4
  1.3 0.0 copy-done.3
  1.3 0.0 copy-start
  1.3 0.8 copy-done
  2.1 0.0 copy-start.1
  2.1 0.8 copy-done.1
  2.8 0.0 copy-start.2
  2.8 0.8 copy-done.2
  3.6 0.1 collective-permute-start.2
  3.7 1.9 %collective-permute-start.1 = (bf16[80,256]{1,0:T(8,128)(2,1)S(1)}, bf16[80,256]{1,0:T(8,128)(2,1)S(1)}, u32[]{:S(2)}, u32[]{:S(2)}) collective-permute-start(bf16[80,256]{1,0:T(8,128)(2,1)S(1)} %get-tuple-element.19), channel_id=1, source_target_pairs={{0,8},{1,9},{8,0},{9,1},{2,10},{3,11},{10,2},{11,3},{4,12},{5,13},... | collective-permute-start | bytes 122888 | tf_op jit(solution)/shard_map/ppermute | solution.py:235
  5.7 0.0 collective-permute-start
  5.7 5.3 %collective-permute-start.5 = (bf16[80,256]{1,0:T(8,128)(2,1)S(1)}, bf16[80,256]{1,0:T(8,128)(2,1)S(1)}, u32[]{:S(2)}, u32[]{:S(2)}) collective-permute-start(bf16[80,256]{1,0:T(8,128)(2,1)S(1)} %get-tuple-element.23), channel_id=1, source_target_pairs={{0,48},{16,0},{32,16},{48,32},{1,49},{17,1},{33,17},{49,33},{2,50}... | collective-permute-start | bytes 122888 | tf_op jit(solution)/shard_map/ppermute | solution.py:213
  11.0 1.4 %collective-permute-start.4 = (bf16[80,256]{1,0:T(8,128)(2,1)S(1)}, bf16[80,256]{1,0:T(8,128)(2,1)S(1)}, u32[]{:S(2)}, u32[]{:S(2)}) collective-permute-start(bf16[80,256]{1,0:T(8,128)(2,1)S(1)} %get-tuple-element.23), channel_id=1, source_target_pairs={{0,32},{16,48},{32,0},{48,16},{1,33},{17,49},{33,1},{49,17},{2,34}... | collective-permute-start | bytes 122888 | tf_op jit(solution)/shard_map/ppermute | solution.py:213
  12.4 0.0 collective-permute-done.2
  12.4 2.4 %collective-permute-start.3 = (bf16[80,256]{1,0:T(8,128)(2,1)S(1)}, bf16[80,256]{1,0:T(8,128)(2,1)S(1)}, u32[]{:S(2)}, u32[]{:S(2)}) collective-permute-start(bf16[80,256]{1,0:T(8,128)(2,1)S(1)} %get-tuple-element.23), channel_id=1, source_target_pairs={{0,16},{16,32},{32,48},{48,0},{1,17},{17,33},{33,49},{49,1},{2,18}... | collective-permute-start | bytes 122888 | tf_op jit(solution)/shard_map/ppermute | solution.py:213
  14.8 0.0 collective-permute-done.1
  14.8 0.0 collective-permute-done
  14.8 0.0 collective-permute-done.5
  14.8 4.1 %collective-permute-done.4 = bf16[80,256]{1,0:T(8,128)(2,1)S(1)} collective-permute-done((bf16[80,256]{1,0:T(8,128)(2,1)S(1)}, bf16[80,256]{1,0:T(8,128)(2,1)S(1)}, u32[]{:S(2)}, u32[]{:S(2)}) %collective-permute-start.4) | collective-permute-done | bytes 40992 | tf_op jit(solution)/shard_map/ppermute | solution.py:213
  18.9 0.2 collective-permute-done.3
  19.1 3.4 %collective-permute-start.11 = (bf16[4,80,256]{2,1,0:T(8,128)(2,1)S(1)}, bf16[4,80,256]{2,1,0:T(8,128)(2,1)S(1)}, u32[]{:S(2)}, u32[]{:S(2)}) collective-permute-start(bf16[4,80,256]{2,1,0:T(8,128)(2,1)S(1)} %pad_maximum_fusion.1.refs_4_), channel_id=1, source_target_pairs={{0,192},{64,0},{128,64},{192,128},{1,193},{65,1},{129,65},{193,129... | collective-permute-start | bytes 491528 | tf_op jit(solution)/shard_map/ppermute | solution.py:213
  22.6 0.6 collective-permute-start.10
  23.2 1.0 collective-permute-start.9
  24.2 2.8 %collective-permute-start.8 = (bf16[4,80,256]{2,1,0:T(8,128)(2,1)S(1)}, bf16[4,80,256]{2,1,0:T(8,128)(2,1)S(1)}, u32[]{:S(2)}, u32[]{:S(2)}) collective-permute-start(bf16[4,80,256]{2,1,0:T(8,128)(2,1)S(1)} %pad_maximum_fusion.refs_0_), channel_id=1, source_target_pairs={{0,6},{2,0},{4,2},{6,4},{1,7},{3,1},{5,3},{7,5},{8,14},{10,8},{12,... | collective-permute-start | bytes 491528 | tf_op jit(solution)/shard_map/ppermute | solution.py:213
  27.0 0.8 collective-permute-start.7
  27.8 0.0 collective-permute-done.11.refs_7_
  27.9 1.5 %collective-permute-start.6 = (bf16[4,80,256]{2,1,0:T(8,128)(2,1)S(1)}, bf16[4,80,256]{2,1,0:T(8,128)(2,1)S(1)}, u32[]{:S(2)}, u32[]{:S(2)}) collective-permute-start(bf16[4,80,256]{2,1,0:T(8,128)(2,1)S(1)} %pad_maximum_fusion.refs_0_), channel_id=1, source_target_pairs={{0,2},{2,4},{4,6},{6,0},{1,3},{3,5},{5,7},{7,1},{8,10},{10,12},{12... | collective-permute-start | bytes 491528 | tf_op jit(solution)/shard_map/ppermute | solution.py:213
  29.4 0.6 collective-permute-done.10.refs_6_
  29.9 1.6 %collective-permute-done.9.refs_5_ = bf16[4,80,256]{2,1,0:T(8,128)(2,1)S(1)} collective-permute-done((bf16[4,80,256]{2,1,0:T(8,128)(2,1)S(1)}, bf16[4,80,256]{2,1,0:T(8,128)(2,1)S(1)}, u32[]{:S(2)}, u32[]{:S(2)}) %collective-permute-start.9) | collective-permute-done | bytes 163872 | tf_op jit(solution)/shard_map/ppermute | solution.py:213
  31.5 0.1 collective-permute-done.8.refs_3_
  31.7 2.3 %collective-permute-done.7.refs_2_ = bf16[4,80,256]{2,1,0:T(8,128)(2,1)S(1)} collective-permute-done((bf16[4,80,256]{2,1,0:T(8,128)(2,1)S(1)}, bf16[4,80,256]{2,1,0:T(8,128)(2,1)S(1)}, u32[]{:S(2)}, u32[]{:S(2)}) %collective-permute-start.7) | collective-permute-done | bytes 163872 | tf_op jit(solution)/shard_map/ppermute | solution.py:213
  34.0 1.7 %collective-permute-done.6.refs_1_ = bf16[4,80,256]{2,1,0:T(8,128)(2,1)S(1)} collective-permute-done((bf16[4,80,256]{2,1,0:T(8,128)(2,1)S(1)}, bf16[4,80,256]{2,1,0:T(8,128)(2,1)S(1)}, u32[]{:S(2)}, u32[]{:S(2)}) %collective-permute-start.6) | collective-permute-done | bytes 163872 | tf_op jit(solution)/shard_map/ppermute | solution.py:213
  35.6 12.3 %row_pass.1 = (f32[16,32,128]{2,1,0:T(8,128)S(1)}, bf16[16,80,256]{2,1,0:T(8,128)(2,1)S(1)}, bf16[16,80,256]{2,1,0:T(8,128)(2,1)S(1)}) custom-call(bf16[4,80,256]{2,1,0:T(8,128)(2,1)S(1)} %pad_maximum_fusion.refs_0_, bf16[4,80,256]{2,1,0:T(8,128)(2,1)S(1)} %collective-permute-done.6.refs_1_, bf16[4,80,256]{2,1,0:T(8,128)(2,1)S(1)} %collective-permute-done.7.refs_2_, ...), custom_call_target="tpu_custom_call" | custom-call | tf_op jit(solution)/shard_map/row_pass/pallas_call | solution.py:201
  47.9 13.4 %all_to_all.10.lse_ref = f32[16,32,128]{2,1,0:T(8,128)S(1)} all-to-all(f32[16,32,128]{2,1,0:T(8,128)S(1)} %get-tuple-element.29), channel_id=1, replica_groups=mesh['y'=4,'zh'=4,'zl'=2,'x'=4,'c'=2] {'zl','x','c'}, dimensions={0} | all-to-all | bytes 524288 | tf_op jit(solution)/shard_map/all_to_all | solution.py:250
  61.3 16.1 %col_pass.1 = (f32[16,128]{1,0:T(8,128)}, f32[16,32,128]{2,1,0:T(8,128)S(1)}) custom-call(bf16[16,80,256]{2,1,0:T(8,128)(2,1)S(1)} %get-tuple-element.27.x_ref, bf16[16,80,256]{2,1,0:T(8,128)(2,1)S(1)} %get-tuple-element.28.y_ref, f32[16,32,128]{2,1,0:T(8,128)S(1)} %all_to_all.10.lse_ref), custom_call_target="tpu_custom_call" | custom-call | tf_op jit(solution)/shard_map/col_pass/pallas_call | solution.py:201
  77.5 20.5 %all_to_all.11.u_ref = f32[16,32,128]{2,1,0:T(8,128)S(1)} all-to-all(f32[16,32,128]{2,1,0:T(8,128)S(1)} %get-tuple-element.31), channel_id=1, replica_groups=mesh['y'=4,'zh'=4,'zl'=2,'x'=4,'c'=2] {'y','zh'}, dimensions={0} | all-to-all | bytes 524288 | tf_op jit(solution)/shard_map/all_to_all | solution.py:258
  98.0 0.1 merge.1.mine_ref
  98.1 0.4 collective-permute-start.12
  98.5 3.4 %collective-permute-done.12.other_ref = f32[32,128]{1,0:T(8,128)S(1)} collective-permute-done((f32[32,128]{1,0:T(8,128)S(1)}, f32[32,128]{1,0:T(8,128)S(1)}, u32[]{:S(2)}, u32[]{:S(2)}) %collective-permute-start.12) | collective-permute-done | bytes 16416 | tf_op jit(solution)/shard_map/ppermute | solution.py:260
  101.9 0.6 last.1
  (3 shorter events, 0.1 us)
Async XLA Ops:
  0.6 0.7 copy-start.4
  0.6 0.7 copy-start.3
  1.3 0.8 copy-start
  2.1 0.8 copy-start.1
  2.8 0.8 copy-start.2
  3.6 8.8 %collective-permute-start.2 = (bf16[80,256]{1,0:T(8,128)(2,1)S(1)}, bf16[80,256]{1,0:T(8,128)(2,1)S(1)}, u32[]{:S(2)}, u32[]{:S(2)}) collective-permute-start(bf16[80,256]{1,0:T(8,128)(2,1)S(1)} %get-tuple-element.19), channel_id=1, source_target_pairs={{0,9},{1,8},{8,1},{9,0},{2,11},{3,10},{10,3},{11,2},{4,13},{5,12},... | collective-permute-start | bytes 122888 | tf_op jit(solution)/shard_map/ppermute | solution.py:235
  3.7 11.1 %collective-permute-start.1 = (bf16[80,256]{1,0:T(8,128)(2,1)S(1)}, bf16[80,256]{1,0:T(8,128)(2,1)S(1)}, u32[]{:S(2)}, u32[]{:S(2)}) collective-permute-start(bf16[80,256]{1,0:T(8,128)(2,1)S(1)} %get-tuple-element.19), channel_id=1, source_target_pairs={{0,8},{1,9},{8,0},{9,1},{2,10},{3,11},{10,2},{11,3},{4,12},{5,13},... | collective-permute-start | bytes 122888 | tf_op jit(solution)/shard_map/ppermute | solution.py:235
  5.7 9.1 %collective-permute-start = (bf16[80,256]{1,0:T(8,128)(2,1)S(1)}, bf16[80,256]{1,0:T(8,128)(2,1)S(1)}, u32[]{:S(2)}, u32[]{:S(2)}) collective-permute-start(bf16[80,256]{1,0:T(8,128)(2,1)S(1)} %get-tuple-element.19), channel_id=1, source_target_pairs={{0,1},{1,0},{8,9},{9,8},{2,3},{3,2},{10,11},{11,10},{4,5},{5,4},{1... | collective-permute-start | bytes 122888 | tf_op jit(solution)/shard_map/ppermute | solution.py:235
  5.7 9.1 %collective-permute-start.5 = (bf16[80,256]{1,0:T(8,128)(2,1)S(1)}, bf16[80,256]{1,0:T(8,128)(2,1)S(1)}, u32[]{:S(2)}, u32[]{:S(2)}) collective-permute-start(bf16[80,256]{1,0:T(8,128)(2,1)S(1)} %get-tuple-element.23), channel_id=1, source_target_pairs={{0,48},{16,0},{32,16},{48,32},{1,49},{17,1},{33,17},{49,33},{2,50}... | collective-permute-start | bytes 122888 | tf_op jit(solution)/shard_map/ppermute | solution.py:213
  11.0 7.9 %collective-permute-start.4 = (bf16[80,256]{1,0:T(8,128)(2,1)S(1)}, bf16[80,256]{1,0:T(8,128)(2,1)S(1)}, u32[]{:S(2)}, u32[]{:S(2)}) collective-permute-start(bf16[80,256]{1,0:T(8,128)(2,1)S(1)} %get-tuple-element.23), channel_id=1, source_target_pairs={{0,32},{16,48},{32,0},{48,16},{1,33},{17,49},{33,1},{49,17},{2,34}... | collective-permute-start | bytes 122888 | tf_op jit(solution)/shard_map/ppermute | solution.py:213
  12.4 6.7 %collective-permute-start.3 = (bf16[80,256]{1,0:T(8,128)(2,1)S(1)}, bf16[80,256]{1,0:T(8,128)(2,1)S(1)}, u32[]{:S(2)}, u32[]{:S(2)}) collective-permute-start(bf16[80,256]{1,0:T(8,128)(2,1)S(1)} %get-tuple-element.23), channel_id=1, source_target_pairs={{0,16},{16,32},{32,48},{48,0},{1,17},{17,33},{33,49},{49,1},{2,18}... | collective-permute-start | bytes 122888 | tf_op jit(solution)/shard_map/ppermute | solution.py:213
  19.1 8.7 %collective-permute-start.11 = (bf16[4,80,256]{2,1,0:T(8,128)(2,1)S(1)}, bf16[4,80,256]{2,1,0:T(8,128)(2,1)S(1)}, u32[]{:S(2)}, u32[]{:S(2)}) collective-permute-start(bf16[4,80,256]{2,1,0:T(8,128)(2,1)S(1)} %pad_maximum_fusion.1.refs_4_), channel_id=1, source_target_pairs={{0,192},{64,0},{128,64},{192,128},{1,193},{65,1},{129,65},{193,129... | collective-permute-start | bytes 491528 | tf_op jit(solution)/shard_map/ppermute | solution.py:213
  22.6 7.3 %collective-permute-start.10 = (bf16[4,80,256]{2,1,0:T(8,128)(2,1)S(1)}, bf16[4,80,256]{2,1,0:T(8,128)(2,1)S(1)}, u32[]{:S(2)}, u32[]{:S(2)}) collective-permute-start(bf16[4,80,256]{2,1,0:T(8,128)(2,1)S(1)} %pad_maximum_fusion.1.refs_4_), channel_id=1, source_target_pairs={{0,128},{64,192},{128,0},{192,64},{1,129},{65,193},{129,1},{193,65... | collective-permute-start | bytes 491528 | tf_op jit(solution)/shard_map/ppermute | solution.py:213
  23.2 8.3 %collective-permute-start.9 = (bf16[4,80,256]{2,1,0:T(8,128)(2,1)S(1)}, bf16[4,80,256]{2,1,0:T(8,128)(2,1)S(1)}, u32[]{:S(2)}, u32[]{:S(2)}) collective-permute-start(bf16[4,80,256]{2,1,0:T(8,128)(2,1)S(1)} %pad_maximum_fusion.1.refs_4_), channel_id=1, source_target_pairs={{0,64},{64,128},{128,192},{192,0},{1,65},{65,129},{129,193},{193,1... | collective-permute-start | bytes 491528 | tf_op jit(solution)/shard_map/ppermute | solution.py:213
  24.2 7.5 %collective-permute-start.8 = (bf16[4,80,256]{2,1,0:T(8,128)(2,1)S(1)}, bf16[4,80,256]{2,1,0:T(8,128)(2,1)S(1)}, u32[]{:S(2)}, u32[]{:S(2)}) collective-permute-start(bf16[4,80,256]{2,1,0:T(8,128)(2,1)S(1)} %pad_maximum_fusion.refs_0_), channel_id=1, source_target_pairs={{0,6},{2,0},{4,2},{6,4},{1,7},{3,1},{5,3},{7,5},{8,14},{10,8},{12,... | collective-permute-start | bytes 491528 | tf_op jit(solution)/shard_map/ppermute | solution.py:213
  27.0 6.9 %collective-permute-start.7 = (bf16[4,80,256]{2,1,0:T(8,128)(2,1)S(1)}, bf16[4,80,256]{2,1,0:T(8,128)(2,1)S(1)}, u32[]{:S(2)}, u32[]{:S(2)}) collective-permute-start(bf16[4,80,256]{2,1,0:T(8,128)(2,1)S(1)} %pad_maximum_fusion.refs_0_), channel_id=1, source_target_pairs={{0,4},{2,6},{4,0},{6,2},{1,5},{3,7},{5,1},{7,3},{8,12},{10,14},{12... | collective-permute-start | bytes 491528 | tf_op jit(solution)/shard_map/ppermute | solution.py:213
  27.9 7.7 %collective-permute-start.6 = (bf16[4,80,256]{2,1,0:T(8,128)(2,1)S(1)}, bf16[4,80,256]{2,1,0:T(8,128)(2,1)S(1)}, u32[]{:S(2)}, u32[]{:S(2)}) collective-permute-start(bf16[4,80,256]{2,1,0:T(8,128)(2,1)S(1)} %pad_maximum_fusion.refs_0_), channel_id=1, source_target_pairs={{0,2},{2,4},{4,6},{6,0},{1,3},{3,5},{5,7},{7,1},{8,10},{10,12},{12... | collective-permute-start | bytes 491528 | tf_op jit(solution)/shard_map/ppermute | solution.py:213
  98.1 3.8 %collective-permute-start.12 = (f32[32,128]{1,0:T(8,128)S(1)}, f32[32,128]{1,0:T(8,128)S(1)}, u32[]{:S(2)}, u32[]{:S(2)}) collective-permute-start(f32[32,128]{1,0:T(8,128)S(1)} %merge.1.mine_ref), channel_id=1, source_target_pairs={{0,8},{8,0},{1,9},{9,1},{2,10},{10,2},{3,11},{11,3},{4,12},{12,4},... | collective-permute-start | bytes 49160 | tf_op jit(solution)/shard_map/ppermute | solution.py:260

commit v4 on v3

--- a/solution.py
+++ b/solution.py
@@ -95,7 +95,8 @@
 
 
 CHUNK = 1024
-SAMPLE = 256
+SAMPLE = 64
+LIFT = 60.0
 ROOM = 100.0
 
 
@@ -106,7 +107,7 @@
         return jnp.dot(a_ref[first : first + count, :], right, preferred_element_type=F32)
 
     def sample(t):
-        return jnp.max(dot(0, SAMPLE, right_side(r_ref, t)), axis=0, keepdims=True)
+        return jnp.max(dot(0, SAMPLE, right_side(r_ref, t)), axis=0, keepdims=True) + LIFT
 
     def total(t, top, peak):
         right = right_side(r_ref, t)
@@ -121,17 +122,22 @@
         return peak
 
     def body(u, top):
-        for t in (2 * u, 2 * u + 1):
+        for t in (4 * u, 4 * u + 1, 4 * u + 2, 4 * u + 3):
+            later = sample(jnp.minimum(t + 1, tiles - 1))
             peak_ref[t] = total(t, top, jnp.full((8, PIECE), LOW, F32))
-            top = sample(jnp.minimum(t + 1, tiles - 1))
+            top = later
         return top
 
-    lax.fori_loop(0, tiles // 2, body, sample(0))
-
-    @pl.when(jnp.max(peak_ref[...] - top_ref[...]) > ROOM)
+    lax.fori_loop(0, tiles // 4, body, sample(0))
+
+    over = jnp.max(jnp.max(peak_ref[...] - top_ref[...], axis=1), axis=1, keepdims=True) > ROOM
+    bits = jnp.exp2(lax.broadcasted_iota(jnp.int32, (tiles, 1), 0).astype(F32))
+    mask = jnp.sum(jnp.where(over, bits, 0.0)).astype(jnp.int32)
+
+    @pl.when(mask > 0)
     def _():
         def again(t, carry):
-            @pl.when(jnp.max(peak_ref[t] - top_ref[t]) > ROOM)
+            @pl.when((mask >> t) & 1 == 1)
             def _():
                 total(t, jnp.max(peak_ref[t], axis=0, keepdims=True), None)
 
@@ -196,7 +202,7 @@
         out_ref[4 * p + 2 : 4 * p + 4, :] = odd[2 * p : 2 * p + 2]
 
 
-def call(kernel, outs, args, scratch=(), name=None):
+def call(kernel, outs, args, scratch=(), name=None, vmem_limit=VMEM_LIMIT):
     vmem = pl.BlockSpec(memory_space=pltpu.VMEM)
     return pl.pallas_call(
         kernel,
@@ -204,7 +210,7 @@
         in_specs=[vmem] * len(args),
         out_specs=jax.tree.map(lambda _: vmem, outs),
         scratch_shapes=list(scratch),
-        compiler_params=pltpu.CompilerParams(vmem_limit_bytes=VMEM_LIMIT),
+        compiler_params=pltpu.CompilerParams(vmem_limit_bytes=vmem_limit),
         name=name,
     )(*args)
 
@@ -230,6 +236,7 @@
             g_init.reshape(-1, 128),
         ),
         name="pack",
+        vmem_limit=60 * 1024 * 1024,
     )
     ya = ring(yo, "zh")
     xa = [xo] + [lax.ppermute(xo, ("zl", "c"), [(i, i ^ k) for i in range(4)]) for k in (1, 2, 3)]

time: 104 us -> 96.1 us (0.924)
  Pallas kernels: 29.1 us -> 25.3 us
  local copies, waits for them, and re-layouts: 2.95 us -> 0.01 us
  blocking collectives: 34 us -> 31.8 us
  waiting for transfers between devices: 14 us -> 12.5 us
  starting transfers between devices: 21.8 us -> 23.2 us
    pallas_call x5, Pallas kernels: 29.1 us -> 25.3 us  [call(): pl.pallas_call(kernel, out_shape=outs, in_specs=[vmem] * len(args), out_s...]
    all_to_all x1, blocking collectives: 13.4 us -> 10.3 us  [local(): parts = lax.all_to_all(lse, ('zl', 'x', 'c'), 0, 0)]
    unnamed x10 -> x2, local copies, waits for them, and re-layouts: 2.95 us -> 0.01 us
    ppermute x1, starting transfers between devices: 0.44 us -> 2.35 us  [local(): other = lax.ppermute(mine, 'zl', [(0, 1), (1, 0)])]
    ppermute x1, waiting for transfers between devices: 3.38 us -> 1.72 us  [local(): other = lax.ppermute(mine, 'zl', [(0, 1), (1, 0)])]
where the time goes in v4:
time: 96.1 us; the launch traced here: 94.4 us
  blocking collectives  31.8 us (33%)
  Pallas kernels  25.3 us (26%)
  starting transfers between devices  23.2 us (24%)
  waiting for transfers between devices  12.5 us (13%)
    pallas_call x5, Pallas kernels, call(): pl.pallas_call(kernel, out_shape=outs, in_specs=[vmem] * len(args), out_s...  25.3 us
    all_to_all x1, blocking collectives, local(): u = lax.all_to_all(u, ('y', 'zh'), 0, 0)  21.5 us
    ppermute x9, starting transfers between devices, ring(): lax.ppermute(v, axis, [(i, (i + k) % 4) for i in range(4)])  18.9 us
    ppermute x9, waiting for transfers between devices, ring(): lax.ppermute(v, axis, [(i, (i + k) % 4) for i in range(4)])  10.8 us
    all_to_all x1, blocking collectives, local(): parts = lax.all_to_all(lse, ('zl', 'x', 'c'), 0, 0)  10.3 us
    ppermute x1, starting transfers between devices, local(): other = lax.ppermute(mine, 'zl', [(0, 1), (1, 0)])  2.35 us
    ppermute x3, starting transfers between devices, local(): lax.ppermute(xo, ('zl', 'c'), [(i, i ^ k) for i in range(4)])  1.96 us
  transfers between devices with their start and end apart: 13, of which 8 were waited for; matrix products, arithmetic and copies ran while one was open for 0% of the time, Pallas kernels for 0%

profile of v4, /device:TPU:32, one launch (start us, length us, event | category | flops | bytes accessed | tf_op | source)
XLA Modules:
  0.0 94.4 jit_solution(2783635522923462175)
XLA Ops:
  0.6 1.5 %pack.1 = (bf16[80,256]{1,0:T(8,128)(2,1)}, bf16[80,256]{1,0:T(8,128)(2,1)}) custom-call(bf16[64,256]{1,0:T(8,128)(2,1)} %x_ref.1, bf16[64,256]{1,0:T(8,128)(2,1)} %y_ref.1, f32[2,128]{1,0:T(2,128)} %bitcast.23, f32[2,128]{1,0:T(2,128)} %bitcast.24, f32[64,128]{1,0:T(8,128)} %bitcast.21), custom_call_target="tpu_custom_call" | custom-call | tf_op jit(solution)/shard_map/pack/pallas_call | solution.py:207
  2.1 0.0 collective-permute-start.2
  2.1 1.9 %collective-permute-start.1 = (bf16[80,256]{1,0:T(8,128)(2,1)}, bf16[80,256]{1,0:T(8,128)(2,1)S(1)}, u32[]{:S(2)}, u32[]{:S(2)}) collective-permute-start(bf16[80,256]{1,0:T(8,128)(2,1)} %get-tuple-element.19), channel_id=1, source_target_pairs={{0,8},{1,9},{8,0},{9,1},{2,10},{3,11},{10,2},{11,3},{4,12},{5,13},... | collective-permute-start | bytes 122888 | tf_op jit(solution)/shard_map/ppermute | solution.py:242
  4.0 0.1 collective-permute-start
  4.1 5.3 %collective-permute-start.5 = (bf16[80,256]{1,0:T(8,128)(2,1)}, bf16[80,256]{1,0:T(8,128)(2,1)S(1)}, u32[]{:S(2)}, u32[]{:S(2)}) collective-permute-start(bf16[80,256]{1,0:T(8,128)(2,1)} %get-tuple-element.23), channel_id=1, source_target_pairs={{0,48},{16,0},{32,16},{48,32},{1,49},{17,1},{33,17},{49,33},{2,50}... | collective-permute-start | bytes 122888 | tf_op jit(solution)/shard_map/ppermute | solution.py:219
  9.4 1.4 %collective-permute-start.4 = (bf16[80,256]{1,0:T(8,128)(2,1)}, bf16[80,256]{1,0:T(8,128)(2,1)S(1)}, u32[]{:S(2)}, u32[]{:S(2)}) collective-permute-start(bf16[80,256]{1,0:T(8,128)(2,1)} %get-tuple-element.23), channel_id=1, source_target_pairs={{0,32},{16,48},{32,0},{48,16},{1,33},{17,49},{33,1},{49,17},{2,34}... | collective-permute-start | bytes 122888 | tf_op jit(solution)/shard_map/ppermute | solution.py:219
  10.8 0.0 collective-permute-done.2
  10.8 2.4 %collective-permute-start.3 = (bf16[80,256]{1,0:T(8,128)(2,1)}, bf16[80,256]{1,0:T(8,128)(2,1)S(1)}, u32[]{:S(2)}, u32[]{:S(2)}) collective-permute-start(bf16[80,256]{1,0:T(8,128)(2,1)} %get-tuple-element.23), channel_id=1, source_target_pairs={{0,16},{16,32},{32,48},{48,0},{1,17},{17,33},{33,49},{49,1},{2,18}... | collective-permute-start | bytes 122888 | tf_op jit(solution)/shard_map/ppermute | solution.py:219
  13.2 0.0 collective-permute-done.1
  13.2 0.0 collective-permute-done
  13.2 0.0 collective-permute-done.5
  13.2 4.3 %collective-permute-done.4 = bf16[80,256]{1,0:T(8,128)(2,1)S(1)} collective-permute-done((bf16[80,256]{1,0:T(8,128)(2,1)}, bf16[80,256]{1,0:T(8,128)(2,1)S(1)}, u32[]{:S(2)}, u32[]{:S(2)}) %collective-permute-start.4) | collective-permute-done | bytes 40992 | tf_op jit(solution)/shard_map/ppermute | solution.py:219
  17.5 0.2 collective-permute-done.3
  17.7 0.0 copy-start
  17.7 0.8 pad_maximum_fusion.1.refs_4_
  18.5 3.1 %collective-permute-start.11 = (bf16[4,80,256]{2,1,0:T(8,128)(2,1)S(1)}, bf16[4,80,256]{2,1,0:T(8,128)(2,1)S(1)}, u32[]{:S(2)}, u32[]{:S(2)}) collective-permute-start(bf16[4,80,256]{2,1,0:T(8,128)(2,1)S(1)} %pad_maximum_fusion.1.refs_4_), channel_id=1, source_target_pairs={{0,192},{64,0},{128,64},{192,128},{1,193},{65,1},{129,65},{193,129... | collective-permute-start | bytes 491528 | tf_op jit(solution)/shard_map/ppermute | solution.py:219
  21.6 0.6 collective-permute-start.10
  22.3 1.0 %collective-permute-start.9 = (bf16[4,80,256]{2,1,0:T(8,128)(2,1)S(1)}, bf16[4,80,256]{2,1,0:T(8,128)(2,1)S(1)}, u32[]{:S(2)}, u32[]{:S(2)}) collective-permute-start(bf16[4,80,256]{2,1,0:T(8,128)(2,1)S(1)} %pad_maximum_fusion.1.refs_4_), channel_id=1, source_target_pairs={{0,64},{64,128},{128,192},{192,0},{1,65},{65,129},{129,193},{193,1... | collective-permute-start | bytes 491528 | tf_op jit(solution)/shard_map/ppermute | solution.py:219
  23.2 0.0 copy-done
  23.3 2.8 %collective-permute-start.8 = (bf16[4,80,256]{2,1,0:T(8,128)(2,1)S(1)}, bf16[4,80,256]{2,1,0:T(8,128)(2,1)S(1)}, u32[]{:S(2)}, u32[]{:S(2)}) collective-permute-start(bf16[4,80,256]{2,1,0:T(8,128)(2,1)S(1)} %pad_maximum_fusion.refs_0_), channel_id=1, source_target_pairs={{0,6},{2,0},{4,2},{6,4},{1,7},{3,1},{5,3},{7,5},{8,14},{10,8},{12,... | collective-permute-start | bytes 491528 | tf_op jit(solution)/shard_map/ppermute | solution.py:219
  26.1 0.8 collective-permute-start.7
  26.9 0.4 collective-permute-done.11.refs_7_
  27.3 1.5 %collective-permute-start.6 = (bf16[4,80,256]{2,1,0:T(8,128)(2,1)S(1)}, bf16[4,80,256]{2,1,0:T(8,128)(2,1)S(1)}, u32[]{:S(2)}, u32[]{:S(2)}) collective-permute-start(bf16[4,80,256]{2,1,0:T(8,128)(2,1)S(1)} %pad_maximum_fusion.refs_0_), channel_id=1, source_target_pairs={{0,2},{2,4},{4,6},{6,0},{1,3},{3,5},{5,7},{7,1},{8,10},{10,12},{12... | collective-permute-start | bytes 491528 | tf_op jit(solution)/shard_map/ppermute | solution.py:219
  28.7 0.5 collective-permute-done.10.refs_6_
  29.3 1.7 %collective-permute-done.9.refs_5_ = bf16[4,80,256]{2,1,0:T(8,128)(2,1)S(1)} collective-permute-done((bf16[4,80,256]{2,1,0:T(8,128)(2,1)S(1)}, bf16[4,80,256]{2,1,0:T(8,128)(2,1)S(1)}, u32[]{:S(2)}, u32[]{:S(2)}) %collective-permute-start.9) | collective-permute-done | bytes 163872 | tf_op jit(solution)/shard_map/ppermute | solution.py:219
  30.9 0.0 collective-permute-done.8.refs_3_
  30.9 2.1 %collective-permute-done.7.refs_2_ = bf16[4,80,256]{2,1,0:T(8,128)(2,1)S(1)} collective-permute-done((bf16[4,80,256]{2,1,0:T(8,128)(2,1)S(1)}, bf16[4,80,256]{2,1,0:T(8,128)(2,1)S(1)}, u32[]{:S(2)}, u32[]{:S(2)}) %collective-permute-start.7) | collective-permute-done | bytes 163872 | tf_op jit(solution)/shard_map/ppermute | solution.py:219
  33.0 1.7 %collective-permute-done.6.refs_1_ = bf16[4,80,256]{2,1,0:T(8,128)(2,1)S(1)} collective-permute-done((bf16[4,80,256]{2,1,0:T(8,128)(2,1)S(1)}, bf16[4,80,256]{2,1,0:T(8,128)(2,1)S(1)}, u32[]{:S(2)}, u32[]{:S(2)}) %collective-permute-start.6) | collective-permute-done | bytes 163872 | tf_op jit(solution)/shard_map/ppermute | solution.py:219
  34.7 11.0 %row_pass.1 = (f32[16,32,128]{2,1,0:T(8,128)S(1)}, bf16[16,80,256]{2,1,0:T(8,128)(2,1)S(1)}, bf16[16,80,256]{2,1,0:T(8,128)(2,1)S(1)}) custom-call(bf16[4,80,256]{2,1,0:T(8,128)(2,1)S(1)} %pad_maximum_fusion.refs_0_, bf16[4,80,256]{2,1,0:T(8,128)(2,1)S(1)} %collective-permute-done.6.refs_1_, bf16[4,80,256]{2,1,0:T(8,128)(2,1)S(1)} %collective-permute-done.7.refs_2_, ...), custom_call_target="tpu_custom_call" | custom-call | tf_op jit(solution)/shard_map/row_pass/pallas_call | solution.py:207
  45.7 10.3 %all_to_all.10.lse_ref = f32[16,32,128]{2,1,0:T(8,128)S(1)} all-to-all(f32[16,32,128]{2,1,0:T(8,128)S(1)} %get-tuple-element.29), channel_id=1, replica_groups=mesh['y'=4,'zh'=4,'zl'=2,'x'=4,'c'=2] {'zl','x','c'}, dimensions={0} | all-to-all | bytes 524288 | tf_op jit(solution)/shard_map/all_to_all | solution.py:257
  56.0 12.1 %col_pass.1 = (f32[16,128]{1,0:T(8,128)}, f32[16,32,128]{2,1,0:T(8,128)S(1)}) custom-call(bf16[16,80,256]{2,1,0:T(8,128)(2,1)S(1)} %get-tuple-element.27.x_ref, bf16[16,80,256]{2,1,0:T(8,128)(2,1)S(1)} %get-tuple-element.28.y_ref, f32[16,32,128]{2,1,0:T(8,128)S(1)} %all_to_all.10.lse_ref), custom_call_target="tpu_custom_call" | custom-call | tf_op jit(solution)/shard_map/col_pass/pallas_call | solution.py:207
  68.2 21.5 %all_to_all.11.u_ref = f32[16,32,128]{2,1,0:T(8,128)S(1)} all-to-all(f32[16,32,128]{2,1,0:T(8,128)S(1)} %get-tuple-element.31), channel_id=1, replica_groups=mesh['y'=4,'zh'=4,'zl'=2,'x'=4,'c'=2] {'y','zh'}, dimensions={0} | all-to-all | bytes 524288 | tf_op jit(solution)/shard_map/all_to_all | solution.py:265
  89.6 0.1 merge.1.mine_ref
  89.7 2.3 %collective-permute-start.12 = (f32[32,128]{1,0:T(8,128)S(1)}, f32[32,128]{1,0:T(8,128)S(1)}, u32[]{:S(2)}, u32[]{:S(2)}) collective-permute-start(f32[32,128]{1,0:T(8,128)S(1)} %merge.1.mine_ref), channel_id=1, source_target_pairs={{0,8},{8,0},{1,9},{9,1},{2,10},{10,2},{3,11},{11,3},{4,12},{12,4},... | collective-permute-start | bytes 49160 | tf_op jit(solution)/shard_map/ppermute | solution.py:267
  92.0 1.7 %collective-permute-done.12.other_ref = f32[32,128]{1,0:T(8,128)S(1)} collective-permute-done((f32[32,128]{1,0:T(8,128)S(1)}, f32[32,128]{1,0:T(8,128)S(1)}, u32[]{:S(2)}, u32[]{:S(2)}) %collective-permute-start.12) | collective-permute-done | bytes 16416 | tf_op jit(solution)/shard_map/ppermute | solution.py:267
  93.8 0.6 last.1
  (1 shorter events, 0.0 us)
Async XLA Ops:
  2.1 8.7 %collective-permute-start.2 = (bf16[80,256]{1,0:T(8,128)(2,1)}, bf16[80,256]{1,0:T(8,128)(2,1)S(1)}, u32[]{:S(2)}, u32[]{:S(2)}) collective-permute-start(bf16[80,256]{1,0:T(8,128)(2,1)} %get-tuple-element.19), channel_id=1, source_target_pairs={{0,9},{1,8},{8,1},{9,0},{2,11},{3,10},{10,3},{11,2},{4,13},{5,12},... | collective-permute-start | bytes 122888 | tf_op jit(solution)/shard_map/ppermute | solution.py:242
  2.1 11.1 %collective-permute-start.1 = (bf16[80,256]{1,0:T(8,128)(2,1)}, bf16[80,256]{1,0:T(8,128)(2,1)S(1)}, u32[]{:S(2)}, u32[]{:S(2)}) collective-permute-start(bf16[80,256]{1,0:T(8,128)(2,1)} %get-tuple-element.19), channel_id=1, source_target_pairs={{0,8},{1,9},{8,0},{9,1},{2,10},{3,11},{10,2},{11,3},{4,12},{5,13},... | collective-permute-start | bytes 122888 | tf_op jit(solution)/shard_map/ppermute | solution.py:242
  4.0 9.2 %collective-permute-start = (bf16[80,256]{1,0:T(8,128)(2,1)}, bf16[80,256]{1,0:T(8,128)(2,1)S(1)}, u32[]{:S(2)}, u32[]{:S(2)}) collective-permute-start(bf16[80,256]{1,0:T(8,128)(2,1)} %get-tuple-element.19), channel_id=1, source_target_pairs={{0,1},{1,0},{8,9},{9,8},{2,3},{3,2},{10,11},{11,10},{4,5},{5,4},{1... | collective-permute-start | bytes 122888 | tf_op jit(solution)/shard_map/ppermute | solution.py:242
  4.1 9.1 %collective-permute-start.5 = (bf16[80,256]{1,0:T(8,128)(2,1)}, bf16[80,256]{1,0:T(8,128)(2,1)S(1)}, u32[]{:S(2)}, u32[]{:S(2)}) collective-permute-start(bf16[80,256]{1,0:T(8,128)(2,1)} %get-tuple-element.23), channel_id=1, source_target_pairs={{0,48},{16,0},{32,16},{48,32},{1,49},{17,1},{33,17},{49,33},{2,50}... | collective-permute-start | bytes 122888 | tf_op jit(solution)/shard_map/ppermute | solution.py:219
  9.4 8.1 %collective-permute-start.4 = (bf16[80,256]{1,0:T(8,128)(2,1)}, bf16[80,256]{1,0:T(8,128)(2,1)S(1)}, u32[]{:S(2)}, u32[]{:S(2)}) collective-permute-start(bf16[80,256]{1,0:T(8,128)(2,1)} %get-tuple-element.23), channel_id=1, source_target_pairs={{0,32},{16,48},{32,0},{48,16},{1,33},{17,49},{33,1},{49,17},{2,34}... | collective-permute-start | bytes 122888 | tf_op jit(solution)/shard_map/ppermute | solution.py:219
  10.8 6.9 %collective-permute-start.3 = (bf16[80,256]{1,0:T(8,128)(2,1)}, bf16[80,256]{1,0:T(8,128)(2,1)S(1)}, u32[]{:S(2)}, u32[]{:S(2)}) collective-permute-start(bf16[80,256]{1,0:T(8,128)(2,1)} %get-tuple-element.23), channel_id=1, source_target_pairs={{0,16},{16,32},{32,48},{48,0},{1,17},{17,33},{33,49},{49,1},{2,18}... | collective-permute-start | bytes 122888 | tf_op jit(solution)/shard_map/ppermute | solution.py:219
  17.7 5.5 %copy-start = (bf16[80,256]{1,0:T(8,128)(2,1)S(1)}, bf16[80,256]{1,0:T(8,128)(2,1)}, u32[]{:S(2)}) copy-start(bf16[80,256]{1,0:T(8,128)(2,1)} %get-tuple-element.19) | copy-start | bytes 122884
  18.5 8.7 %collective-permute-start.11 = (bf16[4,80,256]{2,1,0:T(8,128)(2,1)S(1)}, bf16[4,80,256]{2,1,0:T(8,128)(2,1)S(1)}, u32[]{:S(2)}, u32[]{:S(2)}) collective-permute-start(bf16[4,80,256]{2,1,0:T(8,128)(2,1)S(1)} %pad_maximum_fusion.1.refs_4_), channel_id=1, source_target_pairs={{0,192},{64,0},{128,64},{192,128},{1,193},{65,1},{129,65},{193,129... | collective-permute-start | bytes 491528 | tf_op jit(solution)/shard_map/ppermute | solution.py:219
  21.6 7.6 %collective-permute-start.10 = (bf16[4,80,256]{2,1,0:T(8,128)(2,1)S(1)}, bf16[4,80,256]{2,1,0:T(8,128)(2,1)S(1)}, u32[]{:S(2)}, u32[]{:S(2)}) collective-permute-start(bf16[4,80,256]{2,1,0:T(8,128)(2,1)S(1)} %pad_maximum_fusion.1.refs_4_), channel_id=1, source_target_pairs={{0,128},{64,192},{128,0},{192,64},{1,129},{65,193},{129,1},{193,65... | collective-permute-start | bytes 491528 | tf_op jit(solution)/shard_map/ppermute | solution.py:219
  22.3 8.7 %collective-permute-start.9 = (bf16[4,80,256]{2,1,0:T(8,128)(2,1)S(1)}, bf16[4,80,256]{2,1,0:T(8,128)(2,1)S(1)}, u32[]{:S(2)}, u32[]{:S(2)}) collective-permute-start(bf16[4,80,256]{2,1,0:T(8,128)(2,1)S(1)} %pad_maximum_fusion.1.refs_4_), channel_id=1, source_target_pairs={{0,64},{64,128},{128,192},{192,0},{1,65},{65,129},{129,193},{193,1... | collective-permute-start | bytes 491528 | tf_op jit(solution)/shard_map/ppermute | solution.py:219
  23.3 7.7 %collective-permute-start.8 = (bf16[4,80,256]{2,1,0:T(8,128)(2,1)S(1)}, bf16[4,80,256]{2,1,0:T(8,128)(2,1)S(1)}, u32[]{:S(2)}, u32[]{:S(2)}) collective-permute-start(bf16[4,80,256]{2,1,0:T(8,128)(2,1)S(1)} %pad_maximum_fusion.refs_0_), channel_id=1, source_target_pairs={{0,6},{2,0},{4,2},{6,4},{1,7},{3,1},{5,3},{7,5},{8,14},{10,8},{12,... | collective-permute-start | bytes 491528 | tf_op jit(solution)/shard_map/ppermute | solution.py:219
  26.1 6.9 %collective-permute-start.7 = (bf16[4,80,256]{2,1,0:T(8,128)(2,1)S(1)}, bf16[4,80,256]{2,1,0:T(8,128)(2,1)S(1)}, u32[]{:S(2)}, u32[]{:S(2)}) collective-permute-start(bf16[4,80,256]{2,1,0:T(8,128)(2,1)S(1)} %pad_maximum_fusion.refs_0_), channel_id=1, source_target_pairs={{0,4},{2,6},{4,0},{6,2},{1,5},{3,7},{5,1},{7,3},{8,12},{10,14},{12... | collective-permute-start | bytes 491528 | tf_op jit(solution)/shard_map/ppermute | solution.py:219
  27.3 7.4 %collective-permute-start.6 = (bf16[4,80,256]{2,1,0:T(8,128)(2,1)S(1)}, bf16[4,80,256]{2,1,0:T(8,128)(2,1)S(1)}, u32[]{:S(2)}, u32[]{:S(2)}) collective-permute-start(bf16[4,80,256]{2,1,0:T(8,128)(2,1)S(1)} %pad_maximum_fusion.refs_0_), channel_id=1, source_target_pairs={{0,2},{2,4},{4,6},{6,0},{1,3},{3,5},{5,7},{7,1},{8,10},{10,12},{12... | collective-permute-start | bytes 491528 | tf_op jit(solution)/shard_map/ppermute | solution.py:219
  89.7 4.1 %collective-permute-start.12 = (f32[32,128]{1,0:T(8,128)S(1)}, f32[32,128]{1,0:T(8,128)S(1)}, u32[]{:S(2)}, u32[]{:S(2)}) collective-permute-start(f32[32,128]{1,0:T(8,128)S(1)} %merge.1.mine_ref), channel_id=1, source_target_pairs={{0,8},{8,0},{1,9},{9,1},{2,10},{10,2},{3,11},{11,3},{4,12},{12,4},... | collective-permute-start | bytes 49160 | tf_op jit(solution)/shard_map/ppermute | solution.py:267

commit v5 on v4

--- a/solution.py
+++ b/solution.py
@@ -157,7 +157,7 @@
     yi, zh = lax.axis_index("y"), lax.axis_index("zh")
     for k in range(4):
         for j in range(4):
-            x_ref[((zl + j // 2) % 2 * 4 + (xi + 4 - k) % 4) * 2 + (core + j % 2) % 2] = xs[k][j]
+            x_ref[((zl + k // 2) % 2 * 4 + (xi + 4 - j) % 4) * 2 + (core + k % 2) % 2] = xs[k][j]
             y_ref[(yi + 4 - k) % 4 * 4 + (zh + 4 - j) % 4] = ys[k][j]
             p = 4 * k + j
             left = left_side(ys[k].at[j], scale, own_term(ys[k].at[j]))
@@ -239,10 +239,14 @@
         vmem_limit=60 * 1024 * 1024,
     )
     ya = ring(yo, "zh")
-    xa = [xo] + [lax.ppermute(xo, ("zl", "c"), [(i, i ^ k) for i in range(4)]) for k in (1, 2, 3)]
-    xa, ya = lax.optimization_barrier((xa, ya))
-    xb = ring(jnp.stack(xa), "x")
+    xa = ring(xo, "x")
+    ya, xa = lax.optimization_barrier((ya, xa))
     yb = ring(jnp.stack(ya), "y")
+    pair = [(0, 1), (1, 0)]
+    xb = [jnp.stack(xa)]
+    xb.append(lax.ppermute(xb[0], "c", pair))
+    xb.append(lax.ppermute(xb[0], "zl", pair))
+    xb.append(lax.ppermute(xb[2], "c", pair))
     left = pltpu.VMEM((n, DEPTH), BF16)
     stats = [pltpu.VMEM((GROUP, 8, piece), F32)] * 3
     pieces = shape((GROUP, depth, piece), BF16)

time: 96.1 us -> 92.3 us (0.960); the launches traced: 94.4 us -> 92.4 us
  starting transfers between devices: 23.2 us -> 20.4 us
  waiting for transfers between devices: 12.5 us -> 14.4 us
  blocking collectives: 31.8 us -> 30.8 us
    ppermute x1, starting transfers between devices: 2.35 us -> 0.41 us  [local(): other = lax.ppermute(mine, 'zl', [(0, 1), (1, 0)])]
    ppermute x1, waiting for transfers between devices: 1.72 us -> 3.42 us  [local(): other = lax.ppermute(mine, 'zl', [(0, 1), (1, 0)])]
    all_to_all x1, blocking collectives: 21.5 us -> 19.9 us  [local(): u = lax.all_to_all(u, ('y', 'zh'), 0, 0)]
  transfers between devices with their start and end apart: 13 -> 13, of which waited for: 8 -> 7; matrix products, arithmetic and copies ran while one was open for 0% -> 0% of each run, Pallas kernels for 0% -> 0%
where the time goes in v5:
time: 92.3 us; the launch traced here: 92.4 us
  blocking collectives  30.8 us (33%)
  Pallas kernels  25.4 us (28%)
  starting transfers between devices  20.4 us (22%)
  waiting for transfers between devices  14.4 us (16%)
    pallas_call x5, Pallas kernels, call(): pl.pallas_call(kernel, out_shape=outs, in_specs=[vmem] * len(args), out_s...  25.4 us
    all_to_all x1, blocking collectives, local(): u = lax.all_to_all(u, ('y', 'zh'), 0, 0)  19.9 us
    ppermute x9, starting transfers between devices, ring(): lax.ppermute(v, axis, [(i, (i + k) % 4) for i in range(4)])  18.4 us
    ppermute x9, waiting for transfers between devices, ring(): lax.ppermute(v, axis, [(i, (i + k) % 4) for i in range(4)])  11 us
    all_to_all x1, blocking collectives, local(): parts = lax.all_to_all(lse, ('zl', 'x', 'c'), 0, 0)  10.9 us
    ppermute x1, waiting for transfers between devices, local(): other = lax.ppermute(mine, 'zl', [(0, 1), (1, 0)])  3.42 us
  transfers between devices with their start and end apart: 13, of which 7 were waited for; matrix products, arithmetic and copies ran while one was open for 0% of the time, Pallas kernels for 0%

profile of v5, /device:TPU:32, one launch (start us, length us, event | category | flops | bytes accessed | tf_op | source)
XLA Modules:
  0.0 92.4 jit_solution(6468879070537191908)
XLA Ops:
  0.6 1.5 %pack.1 = (bf16[80,256]{1,0:T(8,128)(2,1)}, bf16[80,256]{1,0:T(8,128)(2,1)}) custom-call(bf16[64,256]{1,0:T(8,128)(2,1)} %x_ref.1, bf16[64,256]{1,0:T(8,128)(2,1)} %y_ref.1, f32[2,128]{1,0:T(2,128)} %bitcast.23, f32[2,128]{1,0:T(2,128)} %bitcast.24, f32[64,128]{1,0:T(8,128)} %bitcast.21), custom_call_target="tpu_custom_call" | custom-call | tf_op jit(solution)/shard_map/pack/pallas_call | solution.py:207
  2.1 5.4 %collective-permute-start.2 = (bf16[80,256]{1,0:T(8,128)(2,1)}, bf16[80,256]{1,0:T(8,128)(2,1)S(1)}, u32[]{:S(2)}, u32[]{:S(2)}) collective-permute-start(bf16[80,256]{1,0:T(8,128)(2,1)} %get-tuple-element.23), channel_id=1, source_target_pairs={{0,48},{16,0},{32,16},{48,32},{1,49},{17,1},{33,17},{49,33},{2,50}... | collective-permute-start | bytes 122888 | tf_op jit(solution)/shard_map/ppermute | solution.py:219
  7.5 1.4 %collective-permute-start.1 = (bf16[80,256]{1,0:T(8,128)(2,1)}, bf16[80,256]{1,0:T(8,128)(2,1)S(1)}, u32[]{:S(2)}, u32[]{:S(2)}) collective-permute-start(bf16[80,256]{1,0:T(8,128)(2,1)} %get-tuple-element.23), channel_id=1, source_target_pairs={{0,32},{16,48},{32,0},{48,16},{1,33},{17,49},{33,1},{49,17},{2,34}... | collective-permute-start | bytes 122888 | tf_op jit(solution)/shard_map/ppermute | solution.py:219
  9.0 2.4 %collective-permute-start = (bf16[80,256]{1,0:T(8,128)(2,1)}, bf16[80,256]{1,0:T(8,128)(2,1)S(1)}, u32[]{:S(2)}, u32[]{:S(2)}) collective-permute-start(bf16[80,256]{1,0:T(8,128)(2,1)} %get-tuple-element.23), channel_id=1, source_target_pairs={{0,16},{16,32},{32,48},{48,0},{1,17},{17,33},{33,49},{49,1},{2,18}... | collective-permute-start | bytes 122888 | tf_op jit(solution)/shard_map/ppermute | solution.py:219
  11.3 2.8 %collective-permute-start.5 = (bf16[80,256]{1,0:T(8,128)(2,1)}, bf16[80,256]{1,0:T(8,128)(2,1)S(1)}, u32[]{:S(2)}, u32[]{:S(2)}) collective-permute-start(bf16[80,256]{1,0:T(8,128)(2,1)} %get-tuple-element.19), channel_id=1, source_target_pairs={{0,6},{2,0},{4,2},{6,4},{1,7},{3,1},{5,3},{7,5},{8,14},{10,8},{12,... | collective-permute-start | bytes 122888 | tf_op jit(solution)/shard_map/ppermute | solution.py:219
  14.1 0.8 collective-permute-start.4
  14.9 0.0 collective-permute-done.2
  14.9 0.9 collective-permute-start.3
  15.8 0.0 collective-permute-done.1
  15.8 0.0 collective-permute-done
  15.8 0.3 collective-permute-done.5
  16.1 3.7 %collective-permute-done.4 = bf16[80,256]{1,0:T(8,128)(2,1)S(1)} collective-permute-done((bf16[80,256]{1,0:T(8,128)(2,1)}, bf16[80,256]{1,0:T(8,128)(2,1)S(1)}, u32[]{:S(2)}, u32[]{:S(2)}) %collective-permute-start.4) | collective-permute-done | bytes 40992 | tf_op jit(solution)/shard_map/ppermute | solution.py:219
  19.8 0.5 collective-permute-done.3
  20.3 0.0 copy-start
  20.3 0.8 pad_maximum_fusion.refs_0_
  21.1 1.1 %collective-permute-start.7 = (bf16[4,80,256]{2,1,0:T(8,128)(2,1)S(1)}, bf16[4,80,256]{2,1,0:T(8,128)(2,1)S(1)}, u32[]{:S(2)}, u32[]{:S(2)}) collective-permute-start(bf16[4,80,256]{2,1,0:T(8,128)(2,1)S(1)} %pad_maximum_fusion.refs_0_), channel_id=1, source_target_pairs={{0,8},{8,0},{1,9},{9,1},{2,10},{10,2},{3,11},{11,3},{4,12},{12,4},... | collective-permute-start | bytes 491528 | tf_op jit(solution)/shard_map/ppermute | solution.py:248
  22.2 0.0 copy-done
  22.3 3.1 %collective-permute-start.11 = (bf16[4,80,256]{2,1,0:T(8,128)(2,1)S(1)}, bf16[4,80,256]{2,1,0:T(8,128)(2,1)S(1)}, u32[]{:S(2)}, u32[]{:S(2)}) collective-permute-start(bf16[4,80,256]{2,1,0:T(8,128)(2,1)S(1)} %pad_maximum_fusion.1.refs_4_), channel_id=1, source_target_pairs={{0,192},{64,0},{128,64},{192,128},{1,193},{65,1},{129,65},{193,129... | collective-permute-start | bytes 491528 | tf_op jit(solution)/shard_map/ppermute | solution.py:219
  25.3 0.6 collective-permute-start.10
  26.0 1.0 %collective-permute-start.9 = (bf16[4,80,256]{2,1,0:T(8,128)(2,1)S(1)}, bf16[4,80,256]{2,1,0:T(8,128)(2,1)S(1)}, u32[]{:S(2)}, u32[]{:S(2)}) collective-permute-start(bf16[4,80,256]{2,1,0:T(8,128)(2,1)S(1)} %pad_maximum_fusion.1.refs_4_), channel_id=1, source_target_pairs={{0,64},{64,128},{128,192},{192,0},{1,65},{65,129},{129,193},{193,1... | collective-permute-start | bytes 491528 | tf_op jit(solution)/shard_map/ppermute | solution.py:219
  26.9 0.0 collective-permute-start.6
  26.9 0.0 collective-permute-done.7.refs_2_
  27.0 0.5 collective-permute-start.8
  27.5 2.5 %collective-permute-done.11.refs_7_ = bf16[4,80,256]{2,1,0:T(8,128)(2,1)S(1)} collective-permute-done((bf16[4,80,256]{2,1,0:T(8,128)(2,1)S(1)}, bf16[4,80,256]{2,1,0:T(8,128)(2,1)S(1)}, u32[]{:S(2)}, u32[]{:S(2)}) %collective-permute-start.11) | collective-permute-done | bytes 163872 | tf_op jit(solution)/shard_map/ppermute | solution.py:219
  30.0 2.3 %collective-permute-done.10.refs_6_ = bf16[4,80,256]{2,1,0:T(8,128)(2,1)S(1)} collective-permute-done((bf16[4,80,256]{2,1,0:T(8,128)(2,1)S(1)}, bf16[4,80,256]{2,1,0:T(8,128)(2,1)S(1)}, u32[]{:S(2)}, u32[]{:S(2)}) %collective-permute-start.10) | collective-permute-done | bytes 163872 | tf_op jit(solution)/shard_map/ppermute | solution.py:219
  32.3 1.7 %collective-permute-done.9.refs_5_ = bf16[4,80,256]{2,1,0:T(8,128)(2,1)S(1)} collective-permute-done((bf16[4,80,256]{2,1,0:T(8,128)(2,1)S(1)}, bf16[4,80,256]{2,1,0:T(8,128)(2,1)S(1)}, u32[]{:S(2)}, u32[]{:S(2)}) %collective-permute-start.9) | collective-permute-done | bytes 163872 | tf_op jit(solution)/shard_map/ppermute | solution.py:219
  33.9 0.0 collective-permute-done.6.refs_1_
  33.9 0.0 collective-permute-done.8.refs_3_
  33.9 11.0 %row_pass.1 = (f32[16,32,128]{2,1,0:T(8,128)S(1)}, bf16[16,80,256]{2,1,0:T(8,128)(2,1)S(1)}, bf16[16,80,256]{2,1,0:T(8,128)(2,1)S(1)}) custom-call(bf16[4,80,256]{2,1,0:T(8,128)(2,1)S(1)} %pad_maximum_fusion.refs_0_, bf16[4,80,256]{2,1,0:T(8,128)(2,1)S(1)} %collective-permute-done.6.refs_1_, bf16[4,80,256]{2,1,0:T(8,128)(2,1)S(1)} %collective-permute-done.7.refs_2_, ...), custom_call_target="tpu_custom_call" | custom-call | tf_op jit(solution)/shard_map/row_pass/pallas_call | solution.py:207
  45.0 10.9 %all_to_all.10.lse_ref = f32[16,32,128]{2,1,0:T(8,128)S(1)} all-to-all(f32[16,32,128]{2,1,0:T(8,128)S(1)} %get-tuple-element.29), channel_id=1, replica_groups=mesh['y'=4,'zh'=4,'zl'=2,'x'=4,'c'=2] {'zl','x','c'}, dimensions={0} | all-to-all | bytes 524288 | tf_op jit(solution)/shard_map/all_to_all | solution.py:261
  55.8 12.1 %col_pass.1 = (f32[16,128]{1,0:T(8,128)}, f32[16,32,128]{2,1,0:T(8,128)S(1)}) custom-call(bf16[16,80,256]{2,1,0:T(8,128)(2,1)S(1)} %get-tuple-element.27.x_ref, bf16[16,80,256]{2,1,0:T(8,128)(2,1)S(1)} %get-tuple-element.28.y_ref, f32[16,32,128]{2,1,0:T(8,128)S(1)} %all_to_all.10.lse_ref), custom_call_target="tpu_custom_call" | custom-call | tf_op jit(solution)/shard_map/col_pass/pallas_call | solution.py:207
  68.0 19.9 %all_to_all.11.u_ref = f32[16,32,128]{2,1,0:T(8,128)S(1)} all-to-all(f32[16,32,128]{2,1,0:T(8,128)S(1)} %get-tuple-element.31), channel_id=1, replica_groups=mesh['y'=4,'zh'=4,'zl'=2,'x'=4,'c'=2] {'y','zh'}, dimensions={0} | all-to-all | bytes 524288 | tf_op jit(solution)/shard_map/all_to_all | solution.py:269
  87.9 0.1 merge.1.mine_ref
  88.0 0.4 collective-permute-start.12
  88.4 3.4 %collective-permute-done.12.other_ref = f32[32,128]{1,0:T(8,128)S(1)} collective-permute-done((f32[32,128]{1,0:T(8,128)S(1)}, f32[32,128]{1,0:T(8,128)S(1)}, u32[]{:S(2)}, u32[]{:S(2)}) %collective-permute-start.12) | collective-permute-done | bytes 16416 | tf_op jit(solution)/shard_map/ppermute | solution.py:271
  91.8 0.6 last.1
  (1 shorter events, 0.0 us)
Async XLA Ops:
  2.1 12.8 %collective-permute-start.2 = (bf16[80,256]{1,0:T(8,128)(2,1)}, bf16[80,256]{1,0:T(8,128)(2,1)S(1)}, u32[]{:S(2)}, u32[]{:S(2)}) collective-permute-start(bf16[80,256]{1,0:T(8,128)(2,1)} %get-tuple-element.23), channel_id=1, source_target_pairs={{0,48},{16,0},{32,16},{48,32},{1,49},{17,1},{33,17},{49,33},{2,50}... | collective-permute-start | bytes 122888 | tf_op jit(solution)/shard_map/ppermute | solution.py:219
  7.5 8.3 %collective-permute-start.1 = (bf16[80,256]{1,0:T(8,128)(2,1)}, bf16[80,256]{1,0:T(8,128)(2,1)S(1)}, u32[]{:S(2)}, u32[]{:S(2)}) collective-permute-start(bf16[80,256]{1,0:T(8,128)(2,1)} %get-tuple-element.23), channel_id=1, source_target_pairs={{0,32},{16,48},{32,0},{48,16},{1,33},{17,49},{33,1},{49,17},{2,34}... | collective-permute-start | bytes 122888 | tf_op jit(solution)/shard_map/ppermute | solution.py:219
  9.0 6.8 %collective-permute-start = (bf16[80,256]{1,0:T(8,128)(2,1)}, bf16[80,256]{1,0:T(8,128)(2,1)S(1)}, u32[]{:S(2)}, u32[]{:S(2)}) collective-permute-start(bf16[80,256]{1,0:T(8,128)(2,1)} %get-tuple-element.23), channel_id=1, source_target_pairs={{0,16},{16,32},{32,48},{48,0},{1,17},{17,33},{33,49},{49,1},{2,18}... | collective-permute-start | bytes 122888 | tf_op jit(solution)/shard_map/ppermute | solution.py:219
  11.3 4.7 %collective-permute-start.5 = (bf16[80,256]{1,0:T(8,128)(2,1)}, bf16[80,256]{1,0:T(8,128)(2,1)S(1)}, u32[]{:S(2)}, u32[]{:S(2)}) collective-permute-start(bf16[80,256]{1,0:T(8,128)(2,1)} %get-tuple-element.19), channel_id=1, source_target_pairs={{0,6},{2,0},{4,2},{6,4},{1,7},{3,1},{5,3},{7,5},{8,14},{10,8},{12,... | collective-permute-start | bytes 122888 | tf_op jit(solution)/shard_map/ppermute | solution.py:219
  14.1 5.7 %collective-permute-start.4 = (bf16[80,256]{1,0:T(8,128)(2,1)}, bf16[80,256]{1,0:T(8,128)(2,1)S(1)}, u32[]{:S(2)}, u32[]{:S(2)}) collective-permute-start(bf16[80,256]{1,0:T(8,128)(2,1)} %get-tuple-element.19), channel_id=1, source_target_pairs={{0,4},{2,6},{4,0},{6,2},{1,5},{3,7},{5,1},{7,3},{8,12},{10,14},{12... | collective-permute-start | bytes 122888 | tf_op jit(solution)/shard_map/ppermute | solution.py:219
  14.9 5.4 %collective-permute-start.3 = (bf16[80,256]{1,0:T(8,128)(2,1)}, bf16[80,256]{1,0:T(8,128)(2,1)S(1)}, u32[]{:S(2)}, u32[]{:S(2)}) collective-permute-start(bf16[80,256]{1,0:T(8,128)(2,1)} %get-tuple-element.19), channel_id=1, source_target_pairs={{0,2},{2,4},{4,6},{6,0},{1,3},{3,5},{5,7},{7,1},{8,10},{10,12},{12... | collective-permute-start | bytes 122888 | tf_op jit(solution)/shard_map/ppermute | solution.py:219
  20.3 1.9 %copy-start = (bf16[80,256]{1,0:T(8,128)(2,1)S(1)}, bf16[80,256]{1,0:T(8,128)(2,1)}, u32[]{:S(2)}) copy-start(bf16[80,256]{1,0:T(8,128)(2,1)} %get-tuple-element.23) | copy-start | bytes 122884
  21.1 5.8 %collective-permute-start.7 = (bf16[4,80,256]{2,1,0:T(8,128)(2,1)S(1)}, bf16[4,80,256]{2,1,0:T(8,128)(2,1)S(1)}, u32[]{:S(2)}, u32[]{:S(2)}) collective-permute-start(bf16[4,80,256]{2,1,0:T(8,128)(2,1)S(1)} %pad_maximum_fusion.refs_0_), channel_id=1, source_target_pairs={{0,8},{8,0},{1,9},{9,1},{2,10},{10,2},{3,11},{11,3},{4,12},{12,4},... | collective-permute-start | bytes 491528 | tf_op jit(solution)/shard_map/ppermute | solution.py:248
  22.3 7.7 %collective-permute-start.11 = (bf16[4,80,256]{2,1,0:T(8,128)(2,1)S(1)}, bf16[4,80,256]{2,1,0:T(8,128)(2,1)S(1)}, u32[]{:S(2)}, u32[]{:S(2)}) collective-permute-start(bf16[4,80,256]{2,1,0:T(8,128)(2,1)S(1)} %pad_maximum_fusion.1.refs_4_), channel_id=1, source_target_pairs={{0,192},{64,0},{128,64},{192,128},{1,193},{65,1},{129,65},{193,129... | collective-permute-start | bytes 491528 | tf_op jit(solution)/shard_map/ppermute | solution.py:219
  25.3 6.9 %collective-permute-start.10 = (bf16[4,80,256]{2,1,0:T(8,128)(2,1)S(1)}, bf16[4,80,256]{2,1,0:T(8,128)(2,1)S(1)}, u32[]{:S(2)}, u32[]{:S(2)}) collective-permute-start(bf16[4,80,256]{2,1,0:T(8,128)(2,1)S(1)} %pad_maximum_fusion.1.refs_4_), channel_id=1, source_target_pairs={{0,128},{64,192},{128,0},{192,64},{1,129},{65,193},{129,1},{193,65... | collective-permute-start | bytes 491528 | tf_op jit(solution)/shard_map/ppermute | solution.py:219
  26.0 7.9 %collective-permute-start.9 = (bf16[4,80,256]{2,1,0:T(8,128)(2,1)S(1)}, bf16[4,80,256]{2,1,0:T(8,128)(2,1)S(1)}, u32[]{:S(2)}, u32[]{:S(2)}) collective-permute-start(bf16[4,80,256]{2,1,0:T(8,128)(2,1)S(1)} %pad_maximum_fusion.1.refs_4_), channel_id=1, source_target_pairs={{0,64},{64,128},{128,192},{192,0},{1,65},{65,129},{129,193},{193,1... | collective-permute-start | bytes 491528 | tf_op jit(solution)/shard_map/ppermute | solution.py:219
  26.9 7.0 %collective-permute-start.6 = (bf16[4,80,256]{2,1,0:T(8,128)(2,1)S(1)}, bf16[4,80,256]{2,1,0:T(8,128)(2,1)S(1)}, u32[]{:S(2)}, u32[]{:S(2)}) collective-permute-start(bf16[4,80,256]{2,1,0:T(8,128)(2,1)S(1)} %pad_maximum_fusion.refs_0_), channel_id=1, source_target_pairs={{0,1},{1,0},{2,3},{3,2},{4,5},{5,4},{6,7},{7,6},{8,9},{9,8},{10,11... | collective-permute-start | bytes 491528 | tf_op jit(solution)/shard_map/ppermute | solution.py:247
  27.0 7.0 %collective-permute-start.8 = (bf16[4,80,256]{2,1,0:T(8,128)(2,1)S(1)}, bf16[4,80,256]{2,1,0:T(8,128)(2,1)S(1)}, u32[]{:S(2)}, u32[]{:S(2)}) collective-permute-start(bf16[4,80,256]{2,1,0:T(8,128)(2,1)S(1)} %collective-permute-done.7.refs_2_), channel_id=1, source_target_pairs={{0,1},{1,0},{2,3},{3,2},{4,5},{5,4},{6,7},{7,6},{8,9},{9,8},{10,11... | collective-permute-start | bytes 491528 | tf_op jit(solution)/shard_map/ppermute | solution.py:249
  88.0 3.8 %collective-permute-start.12 = (f32[32,128]{1,0:T(8,128)S(1)}, f32[32,128]{1,0:T(8,128)S(1)}, u32[]{:S(2)}, u32[]{:S(2)}) collective-permute-start(f32[32,128]{1,0:T(8,128)S(1)} %merge.1.mine_ref), channel_id=1, source_target_pairs={{0,8},{8,0},{1,9},{9,1},{2,10},{10,2},{3,11},{11,3},{4,12},{12,4},... | collective-permute-start | bytes 49160 | tf_op jit(solution)/shard_map/ppermute | solution.py:271

commit v6 on v5

--- a/solution.py
+++ b/solution.py
@@ -96,11 +96,12 @@
 
 CHUNK = 1024
 SAMPLE = 64
-LIFT = 60.0
-ROOM = 100.0
-
-
-def sweep(a_ref, r_ref, top_ref, peak_ref, acc_ref):
+STEP = 4
+LIFT = 80.0
+ROOM = 110.0
+
+
+def sweep(fill, a_ref, r_ref, top_ref, peak_ref, acc_ref):
     n, tiles = a_ref.shape[0], r_ref.shape[0]
 
     def dot(first, count, right):
@@ -108,27 +109,45 @@
 
     def sample(t):
         return jnp.max(dot(0, SAMPLE, right_side(r_ref, t)), axis=0, keepdims=True) + LIFT
+
+    def chunk(c, right, top, acc, peak):
+        s = dot(c * CHUNK, CHUNK, right)
+        if peak is not None:
+            peak = jnp.maximum(peak, fold(s, jnp.max))
+        return acc + fold(jnp.exp2(s - top), jnp.sum), peak
+
+    def keep(t, top, acc, peak):
+        top_ref[t] = jnp.broadcast_to(top, (8, PIECE))
+        acc_ref[t] = acc
+        if peak is not None:
+            peak_ref[t] = peak
 
     def total(t, top, peak):
         right = right_side(r_ref, t)
         acc = jnp.zeros((8, PIECE), F32)
-        for first in range(0, n, CHUNK):
-            s = dot(first, CHUNK, right)
-            if peak is not None:
-                peak = jnp.maximum(peak, fold(s, jnp.max))
-            acc = acc + fold(jnp.exp2(s - top), jnp.sum)
-        top_ref[t] = jnp.broadcast_to(top, (8, PIECE))
-        acc_ref[t] = acc
-        return peak
+        for c in range(n // CHUNK):
+            acc, peak = chunk(c, right, top, acc, peak)
+        keep(t, top, acc, peak)
+
+    low = jnp.full((8, PIECE), LOW, F32)
+    fill(0)
+    tops = [sample(t) for t in range(STEP)]
+    state = [(jnp.zeros((8, PIECE), F32), low)] * STEP
+    for c in range(n // CHUNK):
+        if (c + 1) * CHUNK < n:
+            fill(c + 1)
+        state = [chunk(c, right_side(r_ref, t), tops[t], *state[t]) for t in range(STEP)]
+    for t in range(STEP):
+        keep(t, tops[t], *state[t])
 
     def body(u, top):
-        for t in (4 * u, 4 * u + 1, 4 * u + 2, 4 * u + 3):
-            later = sample(jnp.minimum(t + 1, tiles - 1))
-            peak_ref[t] = total(t, top, jnp.full((8, PIECE), LOW, F32))
+        for t in range(STEP):
+            later = sample(jnp.minimum(STEP * u + t + 1, tiles - 1))
+            total(STEP * u + t, top, low)
             top = later
         return top
 
-    lax.fori_loop(0, tiles // 4, body, sample(0))
+    lax.fori_loop(1, tiles // STEP, body, sample(STEP))
 
     over = jnp.max(jnp.max(peak_ref[...] - top_ref[...], axis=1), axis=1, keepdims=True) > ROOM
     bits = jnp.exp2(lax.broadcasted_iota(jnp.int32, (tiles, 1), 0).astype(F32))
@@ -159,32 +178,41 @@
         for j in range(4):
             x_ref[((zl + k // 2) % 2 * 4 + (xi + 4 - j) % 4) * 2 + (core + k % 2) % 2] = xs[k][j]
             y_ref[(yi + 4 - k) % 4 * 4 + (zh + 4 - j) % 4] = ys[k][j]
-            p = 4 * k + j
-            left = left_side(ys[k].at[j], scale, own_term(ys[k].at[j]))
-            a_ref[p * PIECE : (p + 1) * PIECE, :] = left
-    sweep(a_ref, x_ref, top_ref, peak_ref, acc_ref)
+
+    def fill(c):
+        for j in range(CHUNK // PIECE):
+            left = left_side(ys[c].at[j], scale, own_term(ys[c].at[j]))
+            a_ref[(4 * c + j) * PIECE : (4 * c + j + 1) * PIECE, :] = left
+
+    sweep(fill, a_ref, x_ref, top_ref, peak_ref, acc_ref)
     for p in range(GROUP):
-        lse = lse_of(top_ref, acc_ref, p)
-        for d in range(out_ref.shape[0]):
-            put_wide(out_ref.at[d], 2 * p, lse)
-
-
-def col_kernel(x_ref, y_ref, lse_ref, f_ref, out_ref, a_ref, top_ref, peak_ref, acc_ref, fs_ref, *, scale):
+        put_wide(out_ref.at[0], 2 * p, lse_of(top_ref, acc_ref, p))
+    lse = out_ref[0]
+    for d in range(1, out_ref.shape[0]):
+        out_ref[d] = lse
+
+
+def col_kernel(x_ref, y_ref, lse_ref, f_ref, out_ref, a_ref, top_ref, peak_ref, acc_ref, fs_ref, ny_ref, *, scale):
     feat = x_ref.shape[1] - EXTRA
     part = lse_ref[...]
     top = jnp.max(part, axis=0)
     whole = top + jnp.log2(jnp.sum(jnp.exp2(part - top[None]), axis=0))
+
+    def fill(c):
+        for p in range(c * CHUNK // PIECE, (c + 1) * CHUNK // PIECE):
+            lse = jnp.concatenate([whole[2 * p : 2 * p + 1], whole[2 * p + 1 : 2 * p + 2]], axis=1)
+            put_wide(fs_ref, 2 * p, norm(x_ref.at[p]) / feat - (EPS * LN2) * lse)
+            put_wide(ny_ref, 2 * p, norm(y_ref.at[p]) * (LOG2E / (feat * EPS)))
+            left = left_side(x_ref.at[p], scale, own_term(x_ref.at[p]) - lse)
+            a_ref[p * PIECE : (p + 1) * PIECE, :] = left
+
+    sweep(fill, a_ref, y_ref, top_ref, peak_ref, acc_ref)
+    f_ref[...] = fs_ref[pl.ds(pl.multiple_of(lax.axis_index("zl") * GROUP, GROUP), GROUP), :]
     for p in range(GROUP):
-        lse = jnp.concatenate([whole[2 * p : 2 * p + 1], whole[2 * p + 1 : 2 * p + 2]], axis=1)
-        put_wide(fs_ref, 2 * p, norm(x_ref.at[p]) / feat - (EPS * LN2) * lse)
-        left = left_side(x_ref.at[p], scale, own_term(x_ref.at[p]) - lse)
-        a_ref[p * PIECE : (p + 1) * PIECE, :] = left
-    f_ref[...] = fs_ref[pl.ds(pl.multiple_of(lax.axis_index("zl") * GROUP, GROUP), GROUP), :]
-    sweep(a_ref, y_ref, top_ref, peak_ref, acc_ref)
-    for p in range(GROUP):
-        u = lse_of(top_ref, acc_ref, p) - norm(y_ref.at[p]) * (LOG2E / (feat * EPS))
-        for d in range(out_ref.shape[0]):
-            put_wide(out_ref.at[d], 2 * p, u)
+        put_wide(out_ref.at[0], 2 * p, lse_of(top_ref, acc_ref, p))
+    u = out_ref[0] - ny_ref[...]
+    for d in range(out_ref.shape[0]):
+        out_ref[d] = u
 
 
 def merge_kernel(u_ref, out_ref):
@@ -263,7 +291,7 @@
         functools.partial(col_kernel, scale=scale),
         [shape((n // 256, 128), F32), spread],
         (xs, ys, parts),
-        [left] + stats + [pltpu.VMEM((n // 128, 128), F32)],
+        [left] + stats + [pltpu.VMEM((n // 128, 128), F32)] * 2,
         name="col_pass",
     )
     u = lax.all_to_all(u, ("y", "zh"), 0, 0)

time: 92.3 us -> 91 us (0.986)
  blocking collectives: 30.8 us -> 29.2 us
    all_to_all x1, blocking collectives: 19.9 us -> 17.9 us  [local(): u = lax.all_to_all(u, ('y', 'zh'), 0, 0)]
where the time goes in v6:
time: 91 us; the launch traced here: 90.5 us
  blocking collectives  29.2 us (32%)
  Pallas kernels  25 us (27%)
  starting transfers between devices  20 us (22%)
  waiting for transfers between devices  14.7 us (16%)
    pallas_call x5, Pallas kernels, call(): pl.pallas_call(kernel, out_shape=outs, in_specs=[vmem] * len(args), out_s...  25 us
    ppermute x9, starting transfers between devices, ring(): lax.ppermute(v, axis, [(i, (i + k) % 4) for i in range(4)])  18.4 us
    all_to_all x1, blocking collectives, local(): u = lax.all_to_all(u, ('y', 'zh'), 0, 0)  17.9 us
    all_to_all x1, blocking collectives, local(): parts = lax.all_to_all(lse, ('zl', 'x', 'c'), 0, 0)  11.3 us
    ppermute x9, waiting for transfers between devices, ring(): lax.ppermute(v, axis, [(i, (i + k) % 4) for i in range(4)])  11 us
    ppermute x1, waiting for transfers between devices, local(): other = lax.ppermute(mine, 'zl', [(0, 1), (1, 0)])  3.73 us
  transfers between devices with their start and end apart: 13, of which 7 were waited for; matrix products, arithmetic and copies ran while one was open for 0% of the time, Pallas kernels for 0%

profile of v6, /device:TPU:32, one launch (start us, length us, event | category | flops | bytes accessed | tf_op | source)
XLA Modules:
  0.0 90.5 jit_solution(15433913717299021224)
XLA Ops:
  0.6 1.5 %pack.1 = (bf16[80,256]{1,0:T(8,128)(2,1)}, bf16[80,256]{1,0:T(8,128)(2,1)}) custom-call(bf16[64,256]{1,0:T(8,128)(2,1)} %x_ref.1, bf16[64,256]{1,0:T(8,128)(2,1)} %y_ref.1, f32[2,128]{1,0:T(2,128)} %bitcast.23, f32[2,128]{1,0:T(2,128)} %bitcast.24, f32[64,128]{1,0:T(8,128)} %bitcast.21), custom_call_target="tpu_custom_call" | custom-call | tf_op jit(solution)/shard_map/pack/pallas_call | solution.py:235
  2.1 5.4 %collective-permute-start.2 = (bf16[80,256]{1,0:T(8,128)(2,1)}, bf16[80,256]{1,0:T(8,128)(2,1)S(1)}, u32[]{:S(2)}, u32[]{:S(2)}) collective-permute-start(bf16[80,256]{1,0:T(8,128)(2,1)} %get-tuple-element.23), channel_id=1, source_target_pairs={{0,48},{16,0},{32,16},{48,32},{1,49},{17,1},{33,17},{49,33},{2,50}... | collective-permute-start | bytes 122888 | tf_op jit(solution)/shard_map/ppermute | solution.py:247
  7.5 1.4 %collective-permute-start.1 = (bf16[80,256]{1,0:T(8,128)(2,1)}, bf16[80,256]{1,0:T(8,128)(2,1)S(1)}, u32[]{:S(2)}, u32[]{:S(2)}) collective-permute-start(bf16[80,256]{1,0:T(8,128)(2,1)} %get-tuple-element.23), channel_id=1, source_target_pairs={{0,32},{16,48},{32,0},{48,16},{1,33},{17,49},{33,1},{49,17},{2,34}... | collective-permute-start | bytes 122888 | tf_op jit(solution)/shard_map/ppermute | solution.py:247
  9.0 2.4 %collective-permute-start = (bf16[80,256]{1,0:T(8,128)(2,1)}, bf16[80,256]{1,0:T(8,128)(2,1)S(1)}, u32[]{:S(2)}, u32[]{:S(2)}) collective-permute-start(bf16[80,256]{1,0:T(8,128)(2,1)} %get-tuple-element.23), channel_id=1, source_target_pairs={{0,16},{16,32},{32,48},{48,0},{1,17},{17,33},{33,49},{49,1},{2,18}... | collective-permute-start | bytes 122888 | tf_op jit(solution)/shard_map/ppermute | solution.py:247
  11.3 2.8 %collective-permute-start.5 = (bf16[80,256]{1,0:T(8,128)(2,1)}, bf16[80,256]{1,0:T(8,128)(2,1)S(1)}, u32[]{:S(2)}, u32[]{:S(2)}) collective-permute-start(bf16[80,256]{1,0:T(8,128)(2,1)} %get-tuple-element.19), channel_id=1, source_target_pairs={{0,6},{2,0},{4,2},{6,4},{1,7},{3,1},{5,3},{7,5},{8,14},{10,8},{12,... | collective-permute-start | bytes 122888 | tf_op jit(solution)/shard_map/ppermute | solution.py:247
  14.1 0.8 collective-permute-start.4
  14.9 0.0 collective-permute-done.2
  14.9 0.9 collective-permute-start.3
  15.8 0.0 collective-permute-done.1
  15.8 0.0 collective-permute-done
  15.8 0.3 collective-permute-done.5
  16.1 3.7 %collective-permute-done.4 = bf16[80,256]{1,0:T(8,128)(2,1)S(1)} collective-permute-done((bf16[80,256]{1,0:T(8,128)(2,1)}, bf16[80,256]{1,0:T(8,128)(2,1)S(1)}, u32[]{:S(2)}, u32[]{:S(2)}) %collective-permute-start.4) | collective-permute-done | bytes 40992 | tf_op jit(solution)/shard_map/ppermute | solution.py:247
  19.8 0.5 collective-permute-done.3
  20.3 0.0 copy-start
  20.3 0.8 pad_maximum_fusion.refs_0_
  21.1 1.1 %collective-permute-start.7 = (bf16[4,80,256]{2,1,0:T(8,128)(2,1)S(1)}, bf16[4,80,256]{2,1,0:T(8,128)(2,1)S(1)}, u32[]{:S(2)}, u32[]{:S(2)}) collective-permute-start(bf16[4,80,256]{2,1,0:T(8,128)(2,1)S(1)} %pad_maximum_fusion.refs_0_), channel_id=1, source_target_pairs={{0,8},{8,0},{1,9},{9,1},{2,10},{10,2},{3,11},{11,3},{4,12},{12,4},... | collective-permute-start | bytes 491528 | tf_op jit(solution)/shard_map/ppermute | solution.py:276
  22.2 0.0 copy-done
  22.3 3.1 %collective-permute-start.11 = (bf16[4,80,256]{2,1,0:T(8,128)(2,1)S(1)}, bf16[4,80,256]{2,1,0:T(8,128)(2,1)S(1)}, u32[]{:S(2)}, u32[]{:S(2)}) collective-permute-start(bf16[4,80,256]{2,1,0:T(8,128)(2,1)S(1)} %pad_maximum_fusion.1.refs_4_), channel_id=1, source_target_pairs={{0,192},{64,0},{128,64},{192,128},{1,193},{65,1},{129,65},{193,129... | collective-permute-start | bytes 491528 | tf_op jit(solution)/shard_map/ppermute | solution.py:247
  25.3 0.6 collective-permute-start.10
  26.0 1.0 %collective-permute-start.9 = (bf16[4,80,256]{2,1,0:T(8,128)(2,1)S(1)}, bf16[4,80,256]{2,1,0:T(8,128)(2,1)S(1)}, u32[]{:S(2)}, u32[]{:S(2)}) collective-permute-start(bf16[4,80,256]{2,1,0:T(8,128)(2,1)S(1)} %pad_maximum_fusion.1.refs_4_), channel_id=1, source_target_pairs={{0,64},{64,128},{128,192},{192,0},{1,65},{65,129},{129,193},{193,1... | collective-permute-start | bytes 491528 | tf_op jit(solution)/shard_map/ppermute | solution.py:247
  26.9 0.0 collective-permute-start.6
  26.9 0.0 collective-permute-done.7.refs_2_
  27.0 0.5 collective-permute-start.8
  27.5 2.5 %collective-permute-done.11.refs_7_ = bf16[4,80,256]{2,1,0:T(8,128)(2,1)S(1)} collective-permute-done((bf16[4,80,256]{2,1,0:T(8,128)(2,1)S(1)}, bf16[4,80,256]{2,1,0:T(8,128)(2,1)S(1)}, u32[]{:S(2)}, u32[]{:S(2)}) %collective-permute-start.11) | collective-permute-done | bytes 163872 | tf_op jit(solution)/shard_map/ppermute | solution.py:247
  30.0 2.3 %collective-permute-done.10.refs_6_ = bf16[4,80,256]{2,1,0:T(8,128)(2,1)S(1)} collective-permute-done((bf16[4,80,256]{2,1,0:T(8,128)(2,1)S(1)}, bf16[4,80,256]{2,1,0:T(8,128)(2,1)S(1)}, u32[]{:S(2)}, u32[]{:S(2)}) %collective-permute-start.10) | collective-permute-done | bytes 163872 | tf_op jit(solution)/shard_map/ppermute | solution.py:247
  32.3 1.7 %collective-permute-done.9.refs_5_ = bf16[4,80,256]{2,1,0:T(8,128)(2,1)S(1)} collective-permute-done((bf16[4,80,256]{2,1,0:T(8,128)(2,1)S(1)}, bf16[4,80,256]{2,1,0:T(8,128)(2,1)S(1)}, u32[]{:S(2)}, u32[]{:S(2)}) %collective-permute-start.9) | collective-permute-done | bytes 163872 | tf_op jit(solution)/shard_map/ppermute | solution.py:247
  33.9 0.0 collective-permute-done.6.refs_1_
  33.9 0.0 collective-permute-done.8.refs_3_
  33.9 10.6 %row_pass.1 = (f32[16,32,128]{2,1,0:T(8,128)S(1)}, bf16[16,80,256]{2,1,0:T(8,128)(2,1)S(1)}, bf16[16,80,256]{2,1,0:T(8,128)(2,1)S(1)}) custom-call(bf16[4,80,256]{2,1,0:T(8,128)(2,1)S(1)} %pad_maximum_fusion.refs_0_, bf16[4,80,256]{2,1,0:T(8,128)(2,1)S(1)} %collective-permute-done.6.refs_1_, bf16[4,80,256]{2,1,0:T(8,128)(2,1)S(1)} %collective-permute-done.7.refs_2_, ...), custom_call_target="tpu_custom_call" | custom-call | tf_op jit(solution)/shard_map/row_pass/pallas_call | solution.py:235
  44.6 11.3 %all_to_all.10.lse_ref = f32[16,32,128]{2,1,0:T(8,128)S(1)} all-to-all(f32[16,32,128]{2,1,0:T(8,128)S(1)} %get-tuple-element.29), channel_id=1, replica_groups=mesh['y'=4,'zh'=4,'zl'=2,'x'=4,'c'=2] {'zl','x','c'}, dimensions={0} | all-to-all | bytes 524288 | tf_op jit(solution)/shard_map/all_to_all | solution.py:289
  55.9 12.2 %col_pass.1 = (f32[16,128]{1,0:T(8,128)}, f32[16,32,128]{2,1,0:T(8,128)S(1)}) custom-call(bf16[16,80,256]{2,1,0:T(8,128)(2,1)S(1)} %get-tuple-element.27.x_ref, bf16[16,80,256]{2,1,0:T(8,128)(2,1)S(1)} %get-tuple-element.28.y_ref, f32[16,32,128]{2,1,0:T(8,128)S(1)} %all_to_all.10.lse_ref), custom_call_target="tpu_custom_call" | custom-call | tf_op jit(solution)/shard_map/col_pass/pallas_call | solution.py:235
  68.1 17.9 %all_to_all.11.u_ref = f32[16,32,128]{2,1,0:T(8,128)S(1)} all-to-all(f32[16,32,128]{2,1,0:T(8,128)S(1)} %get-tuple-element.31), channel_id=1, replica_groups=mesh['y'=4,'zh'=4,'zl'=2,'x'=4,'c'=2] {'y','zh'}, dimensions={0} | all-to-all | bytes 524288 | tf_op jit(solution)/shard_map/all_to_all | solution.py:297
  86.0 0.1 merge.1.mine_ref
  86.0 0.1 collective-permute-start.12
  86.1 3.7 %collective-permute-done.12.other_ref = f32[32,128]{1,0:T(8,128)S(1)} collective-permute-done((f32[32,128]{1,0:T(8,128)S(1)}, f32[32,128]{1,0:T(8,128)S(1)}, u32[]{:S(2)}, u32[]{:S(2)}) %collective-permute-start.12) | collective-permute-done | bytes 16416 | tf_op jit(solution)/shard_map/ppermute | solution.py:299
  89.8 0.6 last.1
  (1 shorter events, 0.0 us)
Async XLA Ops:
  2.1 12.8 %collective-permute-start.2 = (bf16[80,256]{1,0:T(8,128)(2,1)}, bf16[80,256]{1,0:T(8,128)(2,1)S(1)}, u32[]{:S(2)}, u32[]{:S(2)}) collective-permute-start(bf16[80,256]{1,0:T(8,128)(2,1)} %get-tuple-element.23), channel_id=1, source_target_pairs={{0,48},{16,0},{32,16},{48,32},{1,49},{17,1},{33,17},{49,33},{2,50}... | collective-permute-start | bytes 122888 | tf_op jit(solution)/shard_map/ppermute | solution.py:247
  7.5 8.3 %collective-permute-start.1 = (bf16[80,256]{1,0:T(8,128)(2,1)}, bf16[80,256]{1,0:T(8,128)(2,1)S(1)}, u32[]{:S(2)}, u32[]{:S(2)}) collective-permute-start(bf16[80,256]{1,0:T(8,128)(2,1)} %get-tuple-element.23), channel_id=1, source_target_pairs={{0,32},{16,48},{32,0},{48,16},{1,33},{17,49},{33,1},{49,17},{2,34}... | collective-permute-start | bytes 122888 | tf_op jit(solution)/shard_map/ppermute | solution.py:247
  9.0 6.8 %collective-permute-start = (bf16[80,256]{1,0:T(8,128)(2,1)}, bf16[80,256]{1,0:T(8,128)(2,1)S(1)}, u32[]{:S(2)}, u32[]{:S(2)}) collective-permute-start(bf16[80,256]{1,0:T(8,128)(2,1)} %get-tuple-element.23), channel_id=1, source_target_pairs={{0,16},{16,32},{32,48},{48,0},{1,17},{17,33},{33,49},{49,1},{2,18}... | collective-permute-start | bytes 122888 | tf_op jit(solution)/shard_map/ppermute | solution.py:247
  11.3 4.7 %collective-permute-start.5 = (bf16[80,256]{1,0:T(8,128)(2,1)}, bf16[80,256]{1,0:T(8,128)(2,1)S(1)}, u32[]{:S(2)}, u32[]{:S(2)}) collective-permute-start(bf16[80,256]{1,0:T(8,128)(2,1)} %get-tuple-element.19), channel_id=1, source_target_pairs={{0,6},{2,0},{4,2},{6,4},{1,7},{3,1},{5,3},{7,5},{8,14},{10,8},{12,... | collective-permute-start | bytes 122888 | tf_op jit(solution)/shard_map/ppermute | solution.py:247
  14.1 5.7 %collective-permute-start.4 = (bf16[80,256]{1,0:T(8,128)(2,1)}, bf16[80,256]{1,0:T(8,128)(2,1)S(1)}, u32[]{:S(2)}, u32[]{:S(2)}) collective-permute-start(bf16[80,256]{1,0:T(8,128)(2,1)} %get-tuple-element.19), channel_id=1, source_target_pairs={{0,4},{2,6},{4,0},{6,2},{1,5},{3,7},{5,1},{7,3},{8,12},{10,14},{12... | collective-permute-start | bytes 122888 | tf_op jit(solution)/shard_map/ppermute | solution.py:247
  14.9 5.4 %collective-permute-start.3 = (bf16[80,256]{1,0:T(8,128)(2,1)}, bf16[80,256]{1,0:T(8,128)(2,1)S(1)}, u32[]{:S(2)}, u32[]{:S(2)}) collective-permute-start(bf16[80,256]{1,0:T(8,128)(2,1)} %get-tuple-element.19), channel_id=1, source_target_pairs={{0,2},{2,4},{4,6},{6,0},{1,3},{3,5},{5,7},{7,1},{8,10},{10,12},{12... | collective-permute-start | bytes 122888 | tf_op jit(solution)/shard_map/ppermute | solution.py:247
  20.3 1.9 %copy-start = (bf16[80,256]{1,0:T(8,128)(2,1)S(1)}, bf16[80,256]{1,0:T(8,128)(2,1)}, u32[]{:S(2)}) copy-start(bf16[80,256]{1,0:T(8,128)(2,1)} %get-tuple-element.23) | copy-start | bytes 122884
  21.1 5.8 %collective-permute-start.7 = (bf16[4,80,256]{2,1,0:T(8,128)(2,1)S(1)}, bf16[4,80,256]{2,1,0:T(8,128)(2,1)S(1)}, u32[]{:S(2)}, u32[]{:S(2)}) collective-permute-start(bf16[4,80,256]{2,1,0:T(8,128)(2,1)S(1)} %pad_maximum_fusion.refs_0_), channel_id=1, source_target_pairs={{0,8},{8,0},{1,9},{9,1},{2,10},{10,2},{3,11},{11,3},{4,12},{12,4},... | collective-permute-start | bytes 491528 | tf_op jit(solution)/shard_map/ppermute | solution.py:276
  22.3 7.7 %collective-permute-start.11 = (bf16[4,80,256]{2,1,0:T(8,128)(2,1)S(1)}, bf16[4,80,256]{2,1,0:T(8,128)(2,1)S(1)}, u32[]{:S(2)}, u32[]{:S(2)}) collective-permute-start(bf16[4,80,256]{2,1,0:T(8,128)(2,1)S(1)} %pad_maximum_fusion.1.refs_4_), channel_id=1, source_target_pairs={{0,192},{64,0},{128,64},{192,128},{1,193},{65,1},{129,65},{193,129... | collective-permute-start | bytes 491528 | tf_op jit(solution)/shard_map/ppermute | solution.py:247
  25.3 6.9 %collective-permute-start.10 = (bf16[4,80,256]{2,1,0:T(8,128)(2,1)S(1)}, bf16[4,80,256]{2,1,0:T(8,128)(2,1)S(1)}, u32[]{:S(2)}, u32[]{:S(2)}) collective-permute-start(bf16[4,80,256]{2,1,0:T(8,128)(2,1)S(1)} %pad_maximum_fusion.1.refs_4_), channel_id=1, source_target_pairs={{0,128},{64,192},{128,0},{192,64},{1,129},{65,193},{129,1},{193,65... | collective-permute-start | bytes 491528 | tf_op jit(solution)/shard_map/ppermute | solution.py:247
  26.0 7.9 %collective-permute-start.9 = (bf16[4,80,256]{2,1,0:T(8,128)(2,1)S(1)}, bf16[4,80,256]{2,1,0:T(8,128)(2,1)S(1)}, u32[]{:S(2)}, u32[]{:S(2)}) collective-permute-start(bf16[4,80,256]{2,1,0:T(8,128)(2,1)S(1)} %pad_maximum_fusion.1.refs_4_), channel_id=1, source_target_pairs={{0,64},{64,128},{128,192},{192,0},{1,65},{65,129},{129,193},{193,1... | collective-permute-start | bytes 491528 | tf_op jit(solution)/shard_map/ppermute | solution.py:247
  26.9 7.0 %collective-permute-start.6 = (bf16[4,80,256]{2,1,0:T(8,128)(2,1)S(1)}, bf16[4,80,256]{2,1,0:T(8,128)(2,1)S(1)}, u32[]{:S(2)}, u32[]{:S(2)}) collective-permute-start(bf16[4,80,256]{2,1,0:T(8,128)(2,1)S(1)} %pad_maximum_fusion.refs_0_), channel_id=1, source_target_pairs={{0,1},{1,0},{2,3},{3,2},{4,5},{5,4},{6,7},{7,6},{8,9},{9,8},{10,11... | collective-permute-start | bytes 491528 | tf_op jit(solution)/shard_map/ppermute | solution.py:275
  27.0 7.0 %collective-permute-start.8 = (bf16[4,80,256]{2,1,0:T(8,128)(2,1)S(1)}, bf16[4,80,256]{2,1,0:T(8,128)(2,1)S(1)}, u32[]{:S(2)}, u32[]{:S(2)}) collective-permute-start(bf16[4,80,256]{2,1,0:T(8,128)(2,1)S(1)} %collective-permute-done.7.refs_2_), channel_id=1, source_target_pairs={{0,1},{1,0},{2,3},{3,2},{4,5},{5,4},{6,7},{7,6},{8,9},{9,8},{10,11... | collective-permute-start | bytes 491528 | tf_op jit(solution)/shard_map/ppermute | solution.py:277
  86.0 3.8 %collective-permute-start.12 = (f32[32,128]{1,0:T(8,128)S(1)}, f32[32,128]{1,0:T(8,128)S(1)}, u32[]{:S(2)}, u32[]{:S(2)}) collective-permute-start(f32[32,128]{1,0:T(8,128)S(1)} %merge.1.mine_ref), channel_id=1, source_target_pairs={{0,8},{8,0},{1,9},{9,1},{2,10},{10,2},{3,11},{11,3},{4,12},{12,4},... | collective-permute-start | bytes 49160 | tf_op jit(solution)/shard_map/ppermute | solution.py:299

commit v7 on v6

--- a/solution.py
+++ b/solution.py
@@ -96,7 +96,7 @@
 
 CHUNK = 1024
 SAMPLE = 64
-STEP = 4
+STEP = 8
 LIFT = 80.0
 ROOM = 110.0
 

time: 91 us -> 89.8 us (0.987); the launches traced: 90.5 us -> 90.3 us
  no operation moved by 1% of the time
where the time goes in v7:
time: 89.8 us; the launch traced here: 90.3 us
  blocking collectives  29.9 us (33%)
  Pallas kernels  24.1 us (27%)
  starting transfers between devices  20.9 us (23%)
  waiting for transfers between devices  13.8 us (15%)
    pallas_call x5, Pallas kernels, call(): pl.pallas_call(kernel, out_shape=outs, in_specs=[vmem] * len(args), out_s...  24.1 us
    all_to_all x1, blocking collectives, local(): u = lax.all_to_all(u, ('y', 'zh'), 0, 0)  18.8 us
    ppermute x9, starting transfers between devices, ring(): lax.ppermute(v, axis, [(i, (i + k) % 4) for i in range(4)])  18.4 us
    all_to_all x1, blocking collectives, local(): parts = lax.all_to_all(lse, ('zl', 'x', 'c'), 0, 0)  11.1 us
    ppermute x9, waiting for transfers between devices, ring(): lax.ppermute(v, axis, [(i, (i + k) % 4) for i in range(4)])  11 us
    ppermute x1, waiting for transfers between devices, local(): other = lax.ppermute(mine, 'zl', [(0, 1), (1, 0)])  2.84 us
  transfers between devices with their start and end apart: 13, of which 7 were waited for; matrix products, arithmetic and copies ran while one was open for 0% of the time, Pallas kernels for 0%

profile of v7, /device:TPU:32, one launch (start us, length us, event | category | flops | bytes accessed | tf_op | source)
XLA Modules:
  0.0 90.3 jit_solution(10289810638525215990)
XLA Ops:
  0.6 1.5 %pack.1 = (bf16[80,256]{1,0:T(8,128)(2,1)}, bf16[80,256]{1,0:T(8,128)(2,1)}) custom-call(bf16[64,256]{1,0:T(8,128)(2,1)} %x_ref.1, bf16[64,256]{1,0:T(8,128)(2,1)} %y_ref.1, f32[2,128]{1,0:T(2,128)} %bitcast.23, f32[2,128]{1,0:T(2,128)} %bitcast.24, f32[64,128]{1,0:T(8,128)} %bitcast.21), custom_call_target="tpu_custom_call" | custom-call | tf_op jit(solution)/shard_map/pack/pallas_call | solution.py:235
  2.1 5.4 %collective-permute-start.2 = (bf16[80,256]{1,0:T(8,128)(2,1)}, bf16[80,256]{1,0:T(8,128)(2,1)S(1)}, u32[]{:S(2)}, u32[]{:S(2)}) collective-permute-start(bf16[80,256]{1,0:T(8,128)(2,1)} %get-tuple-element.23), channel_id=1, source_target_pairs={{0,48},{16,0},{32,16},{48,32},{1,49},{17,1},{33,17},{49,33},{2,50}... | collective-permute-start | bytes 122888 | tf_op jit(solution)/shard_map/ppermute | solution.py:247
  7.5 1.4 %collective-permute-start.1 = (bf16[80,256]{1,0:T(8,128)(2,1)}, bf16[80,256]{1,0:T(8,128)(2,1)S(1)}, u32[]{:S(2)}, u32[]{:S(2)}) collective-permute-start(bf16[80,256]{1,0:T(8,128)(2,1)} %get-tuple-element.23), channel_id=1, source_target_pairs={{0,32},{16,48},{32,0},{48,16},{1,33},{17,49},{33,1},{49,17},{2,34}... | collective-permute-start | bytes 122888 | tf_op jit(solution)/shard_map/ppermute | solution.py:247
  9.0 2.4 %collective-permute-start = (bf16[80,256]{1,0:T(8,128)(2,1)}, bf16[80,256]{1,0:T(8,128)(2,1)S(1)}, u32[]{:S(2)}, u32[]{:S(2)}) collective-permute-start(bf16[80,256]{1,0:T(8,128)(2,1)} %get-tuple-element.23), channel_id=1, source_target_pairs={{0,16},{16,32},{32,48},{48,0},{1,17},{17,33},{33,49},{49,1},{2,18}... | collective-permute-start | bytes 122888 | tf_op jit(solution)/shard_map/ppermute | solution.py:247
  11.3 2.8 %collective-permute-start.5 = (bf16[80,256]{1,0:T(8,128)(2,1)}, bf16[80,256]{1,0:T(8,128)(2,1)S(1)}, u32[]{:S(2)}, u32[]{:S(2)}) collective-permute-start(bf16[80,256]{1,0:T(8,128)(2,1)} %get-tuple-element.19), channel_id=1, source_target_pairs={{0,6},{2,0},{4,2},{6,4},{1,7},{3,1},{5,3},{7,5},{8,14},{10,8},{12,... | collective-permute-start | bytes 122888 | tf_op jit(solution)/shard_map/ppermute | solution.py:247
  14.1 0.8 collective-permute-start.4
  14.9 0.0 collective-permute-done.2
  14.9 0.9 collective-permute-start.3
  15.8 0.0 collective-permute-done.1
  15.8 0.0 collective-permute-done
  15.8 0.3 collective-permute-done.5
  16.1 3.7 %collective-permute-done.4 = bf16[80,256]{1,0:T(8,128)(2,1)S(1)} collective-permute-done((bf16[80,256]{1,0:T(8,128)(2,1)}, bf16[80,256]{1,0:T(8,128)(2,1)S(1)}, u32[]{:S(2)}, u32[]{:S(2)}) %collective-permute-start.4) | collective-permute-done | bytes 40992 | tf_op jit(solution)/shard_map/ppermute | solution.py:247
  19.8 0.5 collective-permute-done.3
  20.3 0.0 copy-start
  20.3 0.8 pad_maximum_fusion.refs_0_
  21.1 1.1 %collective-permute-start.7 = (bf16[4,80,256]{2,1,0:T(8,128)(2,1)S(1)}, bf16[4,80,256]{2,1,0:T(8,128)(2,1)S(1)}, u32[]{:S(2)}, u32[]{:S(2)}) collective-permute-start(bf16[4,80,256]{2,1,0:T(8,128)(2,1)S(1)} %pad_maximum_fusion.refs_0_), channel_id=1, source_target_pairs={{0,8},{8,0},{1,9},{9,1},{2,10},{10,2},{3,11},{11,3},{4,12},{12,4},... | collective-permute-start | bytes 491528 | tf_op jit(solution)/shard_map/ppermute | solution.py:276
  22.2 0.0 copy-done
  22.3 3.1 %collective-permute-start.11 = (bf16[4,80,256]{2,1,0:T(8,128)(2,1)S(1)}, bf16[4,80,256]{2,1,0:T(8,128)(2,1)S(1)}, u32[]{:S(2)}, u32[]{:S(2)}) collective-permute-start(bf16[4,80,256]{2,1,0:T(8,128)(2,1)S(1)} %pad_maximum_fusion.1.refs_4_), channel_id=1, source_target_pairs={{0,192},{64,0},{128,64},{192,128},{1,193},{65,1},{129,65},{193,129... | collective-permute-start | bytes 491528 | tf_op jit(solution)/shard_map/ppermute | solution.py:247
  25.3 0.6 collective-permute-start.10
  26.0 1.0 %collective-permute-start.9 = (bf16[4,80,256]{2,1,0:T(8,128)(2,1)S(1)}, bf16[4,80,256]{2,1,0:T(8,128)(2,1)S(1)}, u32[]{:S(2)}, u32[]{:S(2)}) collective-permute-start(bf16[4,80,256]{2,1,0:T(8,128)(2,1)S(1)} %pad_maximum_fusion.1.refs_4_), channel_id=1, source_target_pairs={{0,64},{64,128},{128,192},{192,0},{1,65},{65,129},{129,193},{193,1... | collective-permute-start | bytes 491528 | tf_op jit(solution)/shard_map/ppermute | solution.py:247
  26.9 0.0 collective-permute-start.6
  26.9 0.0 collective-permute-done.7.refs_2_
  27.0 0.5 collective-permute-start.8
  27.5 2.5 %collective-permute-done.11.refs_7_ = bf16[4,80,256]{2,1,0:T(8,128)(2,1)S(1)} collective-permute-done((bf16[4,80,256]{2,1,0:T(8,128)(2,1)S(1)}, bf16[4,80,256]{2,1,0:T(8,128)(2,1)S(1)}, u32[]{:S(2)}, u32[]{:S(2)}) %collective-permute-start.11) | collective-permute-done | bytes 163872 | tf_op jit(solution)/shard_map/ppermute | solution.py:247
  30.0 2.3 %collective-permute-done.10.refs_6_ = bf16[4,80,256]{2,1,0:T(8,128)(2,1)S(1)} collective-permute-done((bf16[4,80,256]{2,1,0:T(8,128)(2,1)S(1)}, bf16[4,80,256]{2,1,0:T(8,128)(2,1)S(1)}, u32[]{:S(2)}, u32[]{:S(2)}) %collective-permute-start.10) | collective-permute-done | bytes 163872 | tf_op jit(solution)/shard_map/ppermute | solution.py:247
  32.3 1.7 %collective-permute-done.9.refs_5_ = bf16[4,80,256]{2,1,0:T(8,128)(2,1)S(1)} collective-permute-done((bf16[4,80,256]{2,1,0:T(8,128)(2,1)S(1)}, bf16[4,80,256]{2,1,0:T(8,128)(2,1)S(1)}, u32[]{:S(2)}, u32[]{:S(2)}) %collective-permute-start.9) | collective-permute-done | bytes 163872 | tf_op jit(solution)/shard_map/ppermute | solution.py:247
  33.9 0.0 collective-permute-done.6.refs_1_
  33.9 0.0 collective-permute-done.8.refs_3_
  33.9 10.2 %row_pass.1 = (f32[16,32,128]{2,1,0:T(8,128)S(1)}, bf16[16,80,256]{2,1,0:T(8,128)(2,1)S(1)}, bf16[16,80,256]{2,1,0:T(8,128)(2,1)S(1)}) custom-call(bf16[4,80,256]{2,1,0:T(8,128)(2,1)S(1)} %pad_maximum_fusion.refs_0_, bf16[4,80,256]{2,1,0:T(8,128)(2,1)S(1)} %collective-permute-done.6.refs_1_, bf16[4,80,256]{2,1,0:T(8,128)(2,1)S(1)} %collective-permute-done.7.refs_2_, ...), custom_call_target="tpu_custom_call" | custom-call | tf_op jit(solution)/shard_map/row_pass/pallas_call | solution.py:235
  44.2 11.1 %all_to_all.10.lse_ref = f32[16,32,128]{2,1,0:T(8,128)S(1)} all-to-all(f32[16,32,128]{2,1,0:T(8,128)S(1)} %get-tuple-element.29), channel_id=1, replica_groups=mesh['y'=4,'zh'=4,'zl'=2,'x'=4,'c'=2] {'zl','x','c'}, dimensions={0} | all-to-all | bytes 524288 | tf_op jit(solution)/shard_map/all_to_all | solution.py:289
  55.3 11.7 %col_pass.1 = (f32[16,128]{1,0:T(8,128)}, f32[16,32,128]{2,1,0:T(8,128)S(1)}) custom-call(bf16[16,80,256]{2,1,0:T(8,128)(2,1)S(1)} %get-tuple-element.27.x_ref, bf16[16,80,256]{2,1,0:T(8,128)(2,1)S(1)} %get-tuple-element.28.y_ref, f32[16,32,128]{2,1,0:T(8,128)S(1)} %all_to_all.10.lse_ref), custom_call_target="tpu_custom_call" | custom-call | tf_op jit(solution)/shard_map/col_pass/pallas_call | solution.py:235
  67.0 18.8 %all_to_all.11.u_ref = f32[16,32,128]{2,1,0:T(8,128)S(1)} all-to-all(f32[16,32,128]{2,1,0:T(8,128)S(1)} %get-tuple-element.31), channel_id=1, replica_groups=mesh['y'=4,'zh'=4,'zl'=2,'x'=4,'c'=2] {'y','zh'}, dimensions={0} | all-to-all | bytes 524288 | tf_op jit(solution)/shard_map/all_to_all | solution.py:297
  85.7 0.1 merge.1.mine_ref
  85.8 1.0 %collective-permute-start.12 = (f32[32,128]{1,0:T(8,128)S(1)}, f32[32,128]{1,0:T(8,128)S(1)}, u32[]{:S(2)}, u32[]{:S(2)}) collective-permute-start(f32[32,128]{1,0:T(8,128)S(1)} %merge.1.mine_ref), channel_id=1, source_target_pairs={{0,8},{8,0},{1,9},{9,1},{2,10},{10,2},{3,11},{11,3},{4,12},{12,4},... | collective-permute-start | bytes 49160 | tf_op jit(solution)/shard_map/ppermute | solution.py:299
  86.8 2.8 %collective-permute-done.12.other_ref = f32[32,128]{1,0:T(8,128)S(1)} collective-permute-done((f32[32,128]{1,0:T(8,128)S(1)}, f32[32,128]{1,0:T(8,128)S(1)}, u32[]{:S(2)}, u32[]{:S(2)}) %collective-permute-start.12) | collective-permute-done | bytes 16416 | tf_op jit(solution)/shard_map/ppermute | solution.py:299
  89.6 0.6 last.1
  (1 shorter events, 0.0 us)
Async XLA Ops:
  2.1 12.8 %collective-permute-start.2 = (bf16[80,256]{1,0:T(8,128)(2,1)}, bf16[80,256]{1,0:T(8,128)(2,1)S(1)}, u32[]{:S(2)}, u32[]{:S(2)}) collective-permute-start(bf16[80,256]{1,0:T(8,128)(2,1)} %get-tuple-element.23), channel_id=1, source_target_pairs={{0,48},{16,0},{32,16},{48,32},{1,49},{17,1},{33,17},{49,33},{2,50}... | collective-permute-start | bytes 122888 | tf_op jit(solution)/shard_map/ppermute | solution.py:247
  7.5 8.3 %collective-permute-start.1 = (bf16[80,256]{1,0:T(8,128)(2,1)}, bf16[80,256]{1,0:T(8,128)(2,1)S(1)}, u32[]{:S(2)}, u32[]{:S(2)}) collective-permute-start(bf16[80,256]{1,0:T(8,128)(2,1)} %get-tuple-element.23), channel_id=1, source_target_pairs={{0,32},{16,48},{32,0},{48,16},{1,33},{17,49},{33,1},{49,17},{2,34}... | collective-permute-start | bytes 122888 | tf_op jit(solution)/shard_map/ppermute | solution.py:247
  9.0 6.8 %collective-permute-start = (bf16[80,256]{1,0:T(8,128)(2,1)}, bf16[80,256]{1,0:T(8,128)(2,1)S(1)}, u32[]{:S(2)}, u32[]{:S(2)}) collective-permute-start(bf16[80,256]{1,0:T(8,128)(2,1)} %get-tuple-element.23), channel_id=1, source_target_pairs={{0,16},{16,32},{32,48},{48,0},{1,17},{17,33},{33,49},{49,1},{2,18}... | collective-permute-start | bytes 122888 | tf_op jit(solution)/shard_map/ppermute | solution.py:247
  11.3 4.7 %collective-permute-start.5 = (bf16[80,256]{1,0:T(8,128)(2,1)}, bf16[80,256]{1,0:T(8,128)(2,1)S(1)}, u32[]{:S(2)}, u32[]{:S(2)}) collective-permute-start(bf16[80,256]{1,0:T(8,128)(2,1)} %get-tuple-element.19), channel_id=1, source_target_pairs={{0,6},{2,0},{4,2},{6,4},{1,7},{3,1},{5,3},{7,5},{8,14},{10,8},{12,... | collective-permute-start | bytes 122888 | tf_op jit(solution)/shard_map/ppermute | solution.py:247
  14.1 5.7 %collective-permute-start.4 = (bf16[80,256]{1,0:T(8,128)(2,1)}, bf16[80,256]{1,0:T(8,128)(2,1)S(1)}, u32[]{:S(2)}, u32[]{:S(2)}) collective-permute-start(bf16[80,256]{1,0:T(8,128)(2,1)} %get-tuple-element.19), channel_id=1, source_target_pairs={{0,4},{2,6},{4,0},{6,2},{1,5},{3,7},{5,1},{7,3},{8,12},{10,14},{12... | collective-permute-start | bytes 122888 | tf_op jit(solution)/shard_map/ppermute | solution.py:247
  14.9 5.4 %collective-permute-start.3 = (bf16[80,256]{1,0:T(8,128)(2,1)}, bf16[80,256]{1,0:T(8,128)(2,1)S(1)}, u32[]{:S(2)}, u32[]{:S(2)}) collective-permute-start(bf16[80,256]{1,0:T(8,128)(2,1)} %get-tuple-element.19), channel_id=1, source_target_pairs={{0,2},{2,4},{4,6},{6,0},{1,3},{3,5},{5,7},{7,1},{8,10},{10,12},{12... | collective-permute-start | bytes 122888 | tf_op jit(solution)/shard_map/ppermute | solution.py:247
  20.3 1.9 %copy-start = (bf16[80,256]{1,0:T(8,128)(2,1)S(1)}, bf16[80,256]{1,0:T(8,128)(2,1)}, u32[]{:S(2)}) copy-start(bf16[80,256]{1,0:T(8,128)(2,1)} %get-tuple-element.23) | copy-start | bytes 122884
  21.1 5.8 %collective-permute-start.7 = (bf16[4,80,256]{2,1,0:T(8,128)(2,1)S(1)}, bf16[4,80,256]{2,1,0:T(8,128)(2,1)S(1)}, u32[]{:S(2)}, u32[]{:S(2)}) collective-permute-start(bf16[4,80,256]{2,1,0:T(8,128)(2,1)S(1)} %pad_maximum_fusion.refs_0_), channel_id=1, source_target_pairs={{0,8},{8,0},{1,9},{9,1},{2,10},{10,2},{3,11},{11,3},{4,12},{12,4},... | collective-permute-start | bytes 491528 | tf_op jit(solution)/shard_map/ppermute | solution.py:276
  22.3 7.7 %collective-permute-start.11 = (bf16[4,80,256]{2,1,0:T(8,128)(2,1)S(1)}, bf16[4,80,256]{2,1,0:T(8,128)(2,1)S(1)}, u32[]{:S(2)}, u32[]{:S(2)}) collective-permute-start(bf16[4,80,256]{2,1,0:T(8,128)(2,1)S(1)} %pad_maximum_fusion.1.refs_4_), channel_id=1, source_target_pairs={{0,192},{64,0},{128,64},{192,128},{1,193},{65,1},{129,65},{193,129... | collective-permute-start | bytes 491528 | tf_op jit(solution)/shard_map/ppermute | solution.py:247
  25.3 6.9 %collective-permute-start.10 = (bf16[4,80,256]{2,1,0:T(8,128)(2,1)S(1)}, bf16[4,80,256]{2,1,0:T(8,128)(2,1)S(1)}, u32[]{:S(2)}, u32[]{:S(2)}) collective-permute-start(bf16[4,80,256]{2,1,0:T(8,128)(2,1)S(1)} %pad_maximum_fusion.1.refs_4_), channel_id=1, source_target_pairs={{0,128},{64,192},{128,0},{192,64},{1,129},{65,193},{129,1},{193,65... | collective-permute-start | bytes 491528 | tf_op jit(solution)/shard_map/ppermute | solution.py:247
  26.0 7.9 %collective-permute-start.9 = (bf16[4,80,256]{2,1,0:T(8,128)(2,1)S(1)}, bf16[4,80,256]{2,1,0:T(8,128)(2,1)S(1)}, u32[]{:S(2)}, u32[]{:S(2)}) collective-permute-start(bf16[4,80,256]{2,1,0:T(8,128)(2,1)S(1)} %pad_maximum_fusion.1.refs_4_), channel_id=1, source_target_pairs={{0,64},{64,128},{128,192},{192,0},{1,65},{65,129},{129,193},{193,1... | collective-permute-start | bytes 491528 | tf_op jit(solution)/shard_map/ppermute | solution.py:247
  26.9 7.0 %collective-permute-start.6 = (bf16[4,80,256]{2,1,0:T(8,128)(2,1)S(1)}, bf16[4,80,256]{2,1,0:T(8,128)(2,1)S(1)}, u32[]{:S(2)}, u32[]{:S(2)}) collective-permute-start(bf16[4,80,256]{2,1,0:T(8,128)(2,1)S(1)} %pad_maximum_fusion.refs_0_), channel_id=1, source_target_pairs={{0,1},{1,0},{2,3},{3,2},{4,5},{5,4},{6,7},{7,6},{8,9},{9,8},{10,11... | collective-permute-start | bytes 491528 | tf_op jit(solution)/shard_map/ppermute | solution.py:275
  27.0 7.0 %collective-permute-start.8 = (bf16[4,80,256]{2,1,0:T(8,128)(2,1)S(1)}, bf16[4,80,256]{2,1,0:T(8,128)(2,1)S(1)}, u32[]{:S(2)}, u32[]{:S(2)}) collective-permute-start(bf16[4,80,256]{2,1,0:T(8,128)(2,1)S(1)} %collective-permute-done.7.refs_2_), channel_id=1, source_target_pairs={{0,1},{1,0},{2,3},{3,2},{4,5},{5,4},{6,7},{7,6},{8,9},{9,8},{10,11... | collective-permute-start | bytes 491528 | tf_op jit(solution)/shard_map/ppermute | solution.py:277
  85.8 3.8 %collective-permute-start.12 = (f32[32,128]{1,0:T(8,128)S(1)}, f32[32,128]{1,0:T(8,128)S(1)}, u32[]{:S(2)}, u32[]{:S(2)}) collective-permute-start(f32[32,128]{1,0:T(8,128)S(1)} %merge.1.mine_ref), channel_id=1, source_target_pairs={{0,8},{8,0},{1,9},{9,1},{2,10},{10,2},{3,11},{11,3},{4,12},{12,4},... | collective-permute-start | bytes 49160 | tf_op jit(solution)/shard_map/ppermute | solution.py:299

commit v8 on v7

--- a/solution.py
+++ b/solution.py
@@ -14,7 +14,7 @@
 BF16 = jnp.bfloat16
 F32 = jnp.float32
 PIECE = 256
-EXTRA = 16
+EXTRA = 8
 DEPTH = 256
 GROUP = 16
 LOW = -1e30
@@ -55,10 +55,10 @@
     g = wide(g_ref, 2 * mine)
     own = (wide(lb_ref, 0) + (g - ny / feat) / EPS) * LOG2E
     one = jnp.ones((1, PIECE), F32)
-    xo_ref[0:feat, :] = x_ref[...]
-    xo_ref[feat : feat + EXTRA, :] = rows_of(split3(la) + (one, one, one), EXTRA, PIECE).astype(BF16)
-    yo_ref[0:feat, :] = y_ref[...]
-    yo_ref[feat : feat + EXTRA, :] = rows_of(split3(own) + (one, one, one), EXTRA, PIECE).astype(BF16)
+    x_extra = rows_of(split3(la) + (one, one, one), EXTRA, PIECE)
+    y_extra = rows_of(split3(own) + (one, one, one), EXTRA, PIECE)
+    xo_ref[...] = jnp.concatenate([x_ref[...].astype(F32), x_extra], axis=0).astype(BF16)
+    yo_ref[...] = jnp.concatenate([y, y_extra], axis=0).astype(BF16)
 
 
 def left_side(ref, scale, term):
@@ -72,16 +72,18 @@
 def right_side(ref, p):
     feat = ref.shape[1] - EXTRA
     v = ref[p, 0:feat, :]
-    extra = ref[p, feat : feat + EXTRA, :]
-    fill = jnp.zeros((DEPTH - 3 * feat - EXTRA, PIECE), BF16)
-    return jnp.concatenate([v, v, v, extra, fill], axis=0)
+    extra = extra_rows(ref.at[p])
+    fill = jnp.zeros((DEPTH - 3 * feat - EXTRA, PIECE), F32)
+    return jnp.concatenate([v, v, v, jnp.concatenate([extra, fill], axis=0).astype(BF16)], axis=0)
+
+
+def extra_rows(ref):
+    return ref[...].astype(F32)[ref.shape[0] - EXTRA :, :]
 
 
 def own_term(ref):
-    feat = ref.shape[0] - EXTRA
     row = lax.broadcasted_iota(jnp.int32, (EXTRA, PIECE), 0)
-    extra = ref[feat : feat + EXTRA, :].astype(F32)
-    return jnp.sum(jnp.where(row < 3, extra, 0.0), axis=0, keepdims=True)
+    return jnp.sum(jnp.where(row < 3, extra_rows(ref), 0.0), axis=0, keepdims=True)
 
 
 def norm(ref):

time: 89.8 us -> 89.8 us (level)
  blocking collectives: 29.9 us -> 28.1 us
  Pallas kernels: 24.1 us -> 25.7 us
    pallas_call x5, Pallas kernels: 24.1 us -> 25.7 us  [call(): pl.pallas_call(kernel, out_shape=outs, in_specs=[vmem] * len(args), out_s...]
    all_to_all x1, blocking collectives: 11.1 us -> 9.98 us  [local(): parts = lax.all_to_all(lse, ('zl', 'x', 'c'), 0, 0)]
where the time goes in v8:
time: 89.8 us; the launch traced here: 89.7 us
  blocking collectives  28.1 us (31%)
  Pallas kernels  25.7 us (29%)
  starting transfers between devices  21 us (23%)
  waiting for transfers between devices  13.4 us (15%)
    pallas_call x5, Pallas kernels, call(): pl.pallas_call(kernel, out_shape=outs, in_specs=[vmem] * len(args), out_s...  25.7 us
    ppermute x9, starting transfers between devices, ring(): lax.ppermute(v, axis, [(i, (i + k) % 4) for i in range(4)])  18.4 us
    all_to_all x1, blocking collectives, local(): u = lax.all_to_all(u, ('y', 'zh'), 0, 0)  18.1 us
    ppermute x9, waiting for transfers between devices, ring(): lax.ppermute(v, axis, [(i, (i + k) % 4) for i in range(4)])  10.6 us
    all_to_all x1, blocking collectives, local(): parts = lax.all_to_all(lse, ('zl', 'x', 'c'), 0, 0)  9.98 us
    ppermute x1, waiting for transfers between devices, local(): other = lax.ppermute(mine, 'zl', [(0, 1), (1, 0)])  2.74 us
  transfers between devices with their start and end apart: 13, of which 7 were waited for; matrix products, arithmetic and copies ran while one was open for 0% of the time, Pallas kernels for 0%

profile of v8, /device:TPU:32, one launch (start us, length us, event | category | flops | bytes accessed | tf_op | source)
XLA Modules:
  0.0 89.7 jit_solution(2293381568947685907)
XLA Ops:
  0.6 1.5 %pack.1 = (bf16[72,256]{1,0:T(8,128)(2,1)}, bf16[72,256]{1,0:T(8,128)(2,1)}) custom-call(bf16[64,256]{1,0:T(8,128)(2,1)} %x_ref.1, bf16[64,256]{1,0:T(8,128)(2,1)} %y_ref.1, f32[2,128]{1,0:T(2,128)} %bitcast.23, f32[2,128]{1,0:T(2,128)} %bitcast.24, f32[64,128]{1,0:T(8,128)} %bitcast.21), custom_call_target="tpu_custom_call" | custom-call | tf_op jit(solution)/shard_map/pack/pallas_call | solution.py:237
  2.1 5.4 %collective-permute-start.2 = (bf16[72,256]{1,0:T(8,128)(2,1)}, bf16[72,256]{1,0:T(8,128)(2,1)S(1)}, u32[]{:S(2)}, u32[]{:S(2)}) collective-permute-start(bf16[72,256]{1,0:T(8,128)(2,1)} %get-tuple-element.23), channel_id=1, source_target_pairs={{0,48},{16,0},{32,16},{48,32},{1,49},{17,1},{33,17},{49,33},{2,50}... | collective-permute-start | bytes 110600 | tf_op jit(solution)/shard_map/ppermute | solution.py:249
  7.5 1.4 %collective-permute-start.1 = (bf16[72,256]{1,0:T(8,128)(2,1)}, bf16[72,256]{1,0:T(8,128)(2,1)S(1)}, u32[]{:S(2)}, u32[]{:S(2)}) collective-permute-start(bf16[72,256]{1,0:T(8,128)(2,1)} %get-tuple-element.23), channel_id=1, source_target_pairs={{0,32},{16,48},{32,0},{48,16},{1,33},{17,49},{33,1},{49,17},{2,34}... | collective-permute-start | bytes 110600 | tf_op jit(solution)/shard_map/ppermute | solution.py:249
  9.0 2.4 %collective-permute-start = (bf16[72,256]{1,0:T(8,128)(2,1)}, bf16[72,256]{1,0:T(8,128)(2,1)S(1)}, u32[]{:S(2)}, u32[]{:S(2)}) collective-permute-start(bf16[72,256]{1,0:T(8,128)(2,1)} %get-tuple-element.23), channel_id=1, source_target_pairs={{0,16},{16,32},{32,48},{48,0},{1,17},{17,33},{33,49},{49,1},{2,18}... | collective-permute-start | bytes 110600 | tf_op jit(solution)/shard_map/ppermute | solution.py:249
  11.3 2.8 %collective-permute-start.5 = (bf16[72,256]{1,0:T(8,128)(2,1)}, bf16[72,256]{1,0:T(8,128)(2,1)S(1)}, u32[]{:S(2)}, u32[]{:S(2)}) collective-permute-start(bf16[72,256]{1,0:T(8,128)(2,1)} %get-tuple-element.19), channel_id=1, source_target_pairs={{0,6},{2,0},{4,2},{6,4},{1,7},{3,1},{5,3},{7,5},{8,14},{10,8},{12,... | collective-permute-start | bytes 110600 | tf_op jit(solution)/shard_map/ppermute | solution.py:249
  14.1 0.8 collective-permute-start.4
  14.9 0.0 collective-permute-done.2
  14.9 0.9 collective-permute-start.3
  15.8 0.0 collective-permute-done.1
  15.8 0.0 collective-permute-done
  15.8 0.3 collective-permute-done.5
  16.0 3.7 %collective-permute-done.4 = bf16[72,256]{1,0:T(8,128)(2,1)S(1)} collective-permute-done((bf16[72,256]{1,0:T(8,128)(2,1)}, bf16[72,256]{1,0:T(8,128)(2,1)S(1)}, u32[]{:S(2)}, u32[]{:S(2)}) %collective-permute-start.4) | collective-permute-done | bytes 36896 | tf_op jit(solution)/shard_map/ppermute | solution.py:249
  19.8 0.5 collective-permute-done.3
  20.3 0.0 copy-start
  20.3 0.8 pad_maximum_fusion.refs_0_
  21.1 1.1 %collective-permute-start.7 = (bf16[4,72,256]{2,1,0:T(8,128)(2,1)S(1)}, bf16[4,72,256]{2,1,0:T(8,128)(2,1)S(1)}, u32[]{:S(2)}, u32[]{:S(2)}) collective-permute-start(bf16[4,72,256]{2,1,0:T(8,128)(2,1)S(1)} %pad_maximum_fusion.refs_0_), channel_id=1, source_target_pairs={{0,8},{8,0},{1,9},{9,1},{2,10},{10,2},{3,11},{11,3},{4,12},{12,4},... | collective-permute-start | bytes 442376 | tf_op jit(solution)/shard_map/ppermute | solution.py:278
  22.2 0.0 copy-done
  22.2 3.1 %collective-permute-start.11 = (bf16[4,72,256]{2,1,0:T(8,128)(2,1)S(1)}, bf16[4,72,256]{2,1,0:T(8,128)(2,1)S(1)}, u32[]{:S(2)}, u32[]{:S(2)}) collective-permute-start(bf16[4,72,256]{2,1,0:T(8,128)(2,1)S(1)} %pad_maximum_fusion.1.refs_4_), channel_id=1, source_target_pairs={{0,192},{64,0},{128,64},{192,128},{1,193},{65,1},{129,65},{193,129... | collective-permute-start | bytes 442376 | tf_op jit(solution)/shard_map/ppermute | solution.py:249
  25.3 0.6 collective-permute-start.10
  25.9 1.0 %collective-permute-start.9 = (bf16[4,72,256]{2,1,0:T(8,128)(2,1)S(1)}, bf16[4,72,256]{2,1,0:T(8,128)(2,1)S(1)}, u32[]{:S(2)}, u32[]{:S(2)}) collective-permute-start(bf16[4,72,256]{2,1,0:T(8,128)(2,1)S(1)} %pad_maximum_fusion.1.refs_4_), channel_id=1, source_target_pairs={{0,64},{64,128},{128,192},{192,0},{1,65},{65,129},{129,193},{193,1... | collective-permute-start | bytes 442376 | tf_op jit(solution)/shard_map/ppermute | solution.py:249
  26.9 0.0 collective-permute-start.6
  26.9 0.0 collective-permute-done.7.refs_2_
  26.9 0.5 collective-permute-start.8
  27.4 2.2 %collective-permute-done.11.refs_7_ = bf16[4,72,256]{2,1,0:T(8,128)(2,1)S(1)} collective-permute-done((bf16[4,72,256]{2,1,0:T(8,128)(2,1)S(1)}, bf16[4,72,256]{2,1,0:T(8,128)(2,1)S(1)}, u32[]{:S(2)}, u32[]{:S(2)}) %collective-permute-start.11) | collective-permute-done | bytes 147488 | tf_op jit(solution)/shard_map/ppermute | solution.py:249
  29.6 2.5 %collective-permute-done.10.refs_6_ = bf16[4,72,256]{2,1,0:T(8,128)(2,1)S(1)} collective-permute-done((bf16[4,72,256]{2,1,0:T(8,128)(2,1)S(1)}, bf16[4,72,256]{2,1,0:T(8,128)(2,1)S(1)}, u32[]{:S(2)}, u32[]{:S(2)}) %collective-permute-start.10) | collective-permute-done | bytes 147488 | tf_op jit(solution)/shard_map/ppermute | solution.py:249
  32.0 1.5 %collective-permute-done.9.refs_5_ = bf16[4,72,256]{2,1,0:T(8,128)(2,1)S(1)} collective-permute-done((bf16[4,72,256]{2,1,0:T(8,128)(2,1)S(1)}, bf16[4,72,256]{2,1,0:T(8,128)(2,1)S(1)}, u32[]{:S(2)}, u32[]{:S(2)}) %collective-permute-start.9) | collective-permute-done | bytes 147488 | tf_op jit(solution)/shard_map/ppermute | solution.py:249
  33.5 0.0 collective-permute-done.6.refs_1_
  33.5 0.0 collective-permute-done.8.refs_3_
  33.5 11.2 %row_pass.1 = (f32[16,32,128]{2,1,0:T(8,128)S(1)}, bf16[16,72,256]{2,1,0:T(8,128)(2,1)S(1)}, bf16[16,72,256]{2,1,0:T(8,128)(2,1)S(1)}) custom-call(bf16[4,72,256]{2,1,0:T(8,128)(2,1)S(1)} %pad_maximum_fusion.refs_0_, bf16[4,72,256]{2,1,0:T(8,128)(2,1)S(1)} %collective-permute-done.6.refs_1_, bf16[4,72,256]{2,1,0:T(8,128)(2,1)S(1)} %collective-permute-done.7.refs_2_, ...), custom_call_target="tpu_custom_call" | custom-call | tf_op jit(solution)/shard_map/row_pass/pallas_call | solution.py:237
  44.7 10.0 %all_to_all.10.lse_ref = f32[16,32,128]{2,1,0:T(8,128)S(1)} all-to-all(f32[16,32,128]{2,1,0:T(8,128)S(1)} %get-tuple-element.29), channel_id=1, replica_groups=mesh['y'=4,'zh'=4,'zl'=2,'x'=4,'c'=2] {'zl','x','c'}, dimensions={0} | all-to-all | bytes 524288 | tf_op jit(solution)/shard_map/all_to_all | solution.py:291
  54.7 12.4 %col_pass.1 = (f32[16,128]{1,0:T(8,128)}, f32[16,32,128]{2,1,0:T(8,128)S(1)}) custom-call(bf16[16,72,256]{2,1,0:T(8,128)(2,1)S(1)} %get-tuple-element.27.x_ref, bf16[16,72,256]{2,1,0:T(8,128)(2,1)S(1)} %get-tuple-element.28.y_ref, f32[16,32,128]{2,1,0:T(8,128)S(1)} %all_to_all.10.lse_ref), custom_call_target="tpu_custom_call" | custom-call | tf_op jit(solution)/shard_map/col_pass/pallas_call | solution.py:237
  67.1 18.1 %all_to_all.11.u_ref = f32[16,32,128]{2,1,0:T(8,128)S(1)} all-to-all(f32[16,32,128]{2,1,0:T(8,128)S(1)} %get-tuple-element.31), channel_id=1, replica_groups=mesh['y'=4,'zh'=4,'zl'=2,'x'=4,'c'=2] {'y','zh'}, dimensions={0} | all-to-all | bytes 524288 | tf_op jit(solution)/shard_map/all_to_all | solution.py:299
  85.2 0.1 merge.1.mine_ref
  85.3 1.1 %collective-permute-start.12 = (f32[32,128]{1,0:T(8,128)S(1)}, f32[32,128]{1,0:T(8,128)S(1)}, u32[]{:S(2)}, u32[]{:S(2)}) collective-permute-start(f32[32,128]{1,0:T(8,128)S(1)} %merge.1.mine_ref), channel_id=1, source_target_pairs={{0,8},{8,0},{1,9},{9,1},{2,10},{10,2},{3,11},{11,3},{4,12},{12,4},... | collective-permute-start | bytes 49160 | tf_op jit(solution)/shard_map/ppermute | solution.py:301
  86.4 2.7 %collective-permute-done.12.other_ref = f32[32,128]{1,0:T(8,128)S(1)} collective-permute-done((f32[32,128]{1,0:T(8,128)S(1)}, f32[32,128]{1,0:T(8,128)S(1)}, u32[]{:S(2)}, u32[]{:S(2)}) %collective-permute-start.12) | collective-permute-done | bytes 16416 | tf_op jit(solution)/shard_map/ppermute | solution.py:301
  89.1 0.6 last.1
  (1 shorter events, 0.0 us)
Async XLA Ops:
  2.1 12.8 %collective-permute-start.2 = (bf16[72,256]{1,0:T(8,128)(2,1)}, bf16[72,256]{1,0:T(8,128)(2,1)S(1)}, u32[]{:S(2)}, u32[]{:S(2)}) collective-permute-start(bf16[72,256]{1,0:T(8,128)(2,1)} %get-tuple-element.23), channel_id=1, source_target_pairs={{0,48},{16,0},{32,16},{48,32},{1,49},{17,1},{33,17},{49,33},{2,50}... | collective-permute-start | bytes 110600 | tf_op jit(solution)/shard_map/ppermute | solution.py:249
  7.5 8.3 %collective-permute-start.1 = (bf16[72,256]{1,0:T(8,128)(2,1)}, bf16[72,256]{1,0:T(8,128)(2,1)S(1)}, u32[]{:S(2)}, u32[]{:S(2)}) collective-permute-start(bf16[72,256]{1,0:T(8,128)(2,1)} %get-tuple-element.23), channel_id=1, source_target_pairs={{0,32},{16,48},{32,0},{48,16},{1,33},{17,49},{33,1},{49,17},{2,34}... | collective-permute-start | bytes 110600 | tf_op jit(solution)/shard_map/ppermute | solution.py:249
  9.0 6.8 %collective-permute-start = (bf16[72,256]{1,0:T(8,128)(2,1)}, bf16[72,256]{1,0:T(8,128)(2,1)S(1)}, u32[]{:S(2)}, u32[]{:S(2)}) collective-permute-start(bf16[72,256]{1,0:T(8,128)(2,1)} %get-tuple-element.23), channel_id=1, source_target_pairs={{0,16},{16,32},{32,48},{48,0},{1,17},{17,33},{33,49},{49,1},{2,18}... | collective-permute-start | bytes 110600 | tf_op jit(solution)/shard_map/ppermute | solution.py:249
  11.3 4.7 %collective-permute-start.5 = (bf16[72,256]{1,0:T(8,128)(2,1)}, bf16[72,256]{1,0:T(8,128)(2,1)S(1)}, u32[]{:S(2)}, u32[]{:S(2)}) collective-permute-start(bf16[72,256]{1,0:T(8,128)(2,1)} %get-tuple-element.19), channel_id=1, source_target_pairs={{0,6},{2,0},{4,2},{6,4},{1,7},{3,1},{5,3},{7,5},{8,14},{10,8},{12,... | collective-permute-start | bytes 110600 | tf_op jit(solution)/shard_map/ppermute | solution.py:249
  14.1 5.7 %collective-permute-start.4 = (bf16[72,256]{1,0:T(8,128)(2,1)}, bf16[72,256]{1,0:T(8,128)(2,1)S(1)}, u32[]{:S(2)}, u32[]{:S(2)}) collective-permute-start(bf16[72,256]{1,0:T(8,128)(2,1)} %get-tuple-element.19), channel_id=1, source_target_pairs={{0,4},{2,6},{4,0},{6,2},{1,5},{3,7},{5,1},{7,3},{8,12},{10,14},{12... | collective-permute-start | bytes 110600 | tf_op jit(solution)/shard_map/ppermute | solution.py:249
  14.9 5.4 %collective-permute-start.3 = (bf16[72,256]{1,0:T(8,128)(2,1)}, bf16[72,256]{1,0:T(8,128)(2,1)S(1)}, u32[]{:S(2)}, u32[]{:S(2)}) collective-permute-start(bf16[72,256]{1,0:T(8,128)(2,1)} %get-tuple-element.19), channel_id=1, source_target_pairs={{0,2},{2,4},{4,6},{6,0},{1,3},{3,5},{5,7},{7,1},{8,10},{10,12},{12... | collective-permute-start | bytes 110600 | tf_op jit(solution)/shard_map/ppermute | solution.py:249
  20.3 1.9 %copy-start = (bf16[72,256]{1,0:T(8,128)(2,1)S(1)}, bf16[72,256]{1,0:T(8,128)(2,1)}, u32[]{:S(2)}) copy-start(bf16[72,256]{1,0:T(8,128)(2,1)} %get-tuple-element.23) | copy-start | bytes 110596
  21.1 5.8 %collective-permute-start.7 = (bf16[4,72,256]{2,1,0:T(8,128)(2,1)S(1)}, bf16[4,72,256]{2,1,0:T(8,128)(2,1)S(1)}, u32[]{:S(2)}, u32[]{:S(2)}) collective-permute-start(bf16[4,72,256]{2,1,0:T(8,128)(2,1)S(1)} %pad_maximum_fusion.refs_0_), channel_id=1, source_target_pairs={{0,8},{8,0},{1,9},{9,1},{2,10},{10,2},{3,11},{11,3},{4,12},{12,4},... | collective-permute-start | bytes 442376 | tf_op jit(solution)/shard_map/ppermute | solution.py:278
  22.2 7.4 %collective-permute-start.11 = (bf16[4,72,256]{2,1,0:T(8,128)(2,1)S(1)}, bf16[4,72,256]{2,1,0:T(8,128)(2,1)S(1)}, u32[]{:S(2)}, u32[]{:S(2)}) collective-permute-start(bf16[4,72,256]{2,1,0:T(8,128)(2,1)S(1)} %pad_maximum_fusion.1.refs_4_), channel_id=1, source_target_pairs={{0,192},{64,0},{128,64},{192,128},{1,193},{65,1},{129,65},{193,129... | collective-permute-start | bytes 442376 | tf_op jit(solution)/shard_map/ppermute | solution.py:249
  25.3 6.8 %collective-permute-start.10 = (bf16[4,72,256]{2,1,0:T(8,128)(2,1)S(1)}, bf16[4,72,256]{2,1,0:T(8,128)(2,1)S(1)}, u32[]{:S(2)}, u32[]{:S(2)}) collective-permute-start(bf16[4,72,256]{2,1,0:T(8,128)(2,1)S(1)} %pad_maximum_fusion.1.refs_4_), channel_id=1, source_target_pairs={{0,128},{64,192},{128,0},{192,64},{1,129},{65,193},{129,1},{193,65... | collective-permute-start | bytes 442376 | tf_op jit(solution)/shard_map/ppermute | solution.py:249
  25.9 7.6 %collective-permute-start.9 = (bf16[4,72,256]{2,1,0:T(8,128)(2,1)S(1)}, bf16[4,72,256]{2,1,0:T(8,128)(2,1)S(1)}, u32[]{:S(2)}, u32[]{:S(2)}) collective-permute-start(bf16[4,72,256]{2,1,0:T(8,128)(2,1)S(1)} %pad_maximum_fusion.1.refs_4_), channel_id=1, source_target_pairs={{0,64},{64,128},{128,192},{192,0},{1,65},{65,129},{129,193},{193,1... | collective-permute-start | bytes 442376 | tf_op jit(solution)/shard_map/ppermute | solution.py:249
  26.9 6.6 %collective-permute-start.6 = (bf16[4,72,256]{2,1,0:T(8,128)(2,1)S(1)}, bf16[4,72,256]{2,1,0:T(8,128)(2,1)S(1)}, u32[]{:S(2)}, u32[]{:S(2)}) collective-permute-start(bf16[4,72,256]{2,1,0:T(8,128)(2,1)S(1)} %pad_maximum_fusion.refs_0_), channel_id=1, source_target_pairs={{0,1},{1,0},{2,3},{3,2},{4,5},{5,4},{6,7},{7,6},{8,9},{9,8},{10,11... | collective-permute-start | bytes 442376 | tf_op jit(solution)/shard_map/ppermute | solution.py:277
  26.9 6.6 %collective-permute-start.8 = (bf16[4,72,256]{2,1,0:T(8,128)(2,1)S(1)}, bf16[4,72,256]{2,1,0:T(8,128)(2,1)S(1)}, u32[]{:S(2)}, u32[]{:S(2)}) collective-permute-start(bf16[4,72,256]{2,1,0:T(8,128)(2,1)S(1)} %collective-permute-done.7.refs_2_), channel_id=1, source_target_pairs={{0,1},{1,0},{2,3},{3,2},{4,5},{5,4},{6,7},{7,6},{8,9},{9,8},{10,11... | collective-permute-start | bytes 442376 | tf_op jit(solution)/shard_map/ppermute | solution.py:279
  85.3 3.8 %collective-permute-start.12 = (f32[32,128]{1,0:T(8,128)S(1)}, f32[32,128]{1,0:T(8,128)S(1)}, u32[]{:S(2)}, u32[]{:S(2)}) collective-permute-start(f32[32,128]{1,0:T(8,128)S(1)} %merge.1.mine_ref), channel_id=1, source_target_pairs={{0,8},{8,0},{1,9},{9,1},{2,10},{10,2},{3,11},{11,3},{4,12},{12,4},... | collective-permute-start | bytes 49160 | tf_op jit(solution)/shard_map/ppermute | solution.py:301
